TPU v7x, 128 devices: a whole 4x4x4 slice. The times are simulated.
128 devices in a mesh: replica: 64 (over z, y, x), shard: 2 (over core).
Axes of the slice: x: 4, y: 4, z: 4, core: 2. Of those that a mesh axis runs over, the one named last changes fastest.
Arguments:
- hidden_rows: bfloat16 [32768, 6144], P(('replica', 'shard')), may hold values from -6 to 6
- row_counts: int32 [128], P(('replica', 'shard')), may hold values from 1 to 256, 16384 in all
- target_rows: bfloat16 [32768, 2048], P(('replica', 'shard')), may hold values from -6 to 6
- joined_weight: bfloat16 [6144, 2048], P(('replica', 'shard')), may hold values from -0.078125 to 0.078125
- norm_gain: float32 [2048], replicated, may hold values from 0.1 to 1.9
Outputs:
- weight_step: bfloat16 [6144, 2048], P(('replica', 'shard'))
Inputs may be any that keep to these rules, and one draw needn't show every extreme that they name: Device p's live rows are its first row_counts[p] slots; the counts sum to 16384, and some device has all 256 slots live.
All inputs are finite; a program needn't handle non-finite values.
Results may differ from a plain program's by a relative error of at most 0.009.
Values may be sent and summed in bfloat16 or wider, within the bound.
No kernel may reach another device: no remote copies, remote signals or barrier semaphores. Data moves between devices by JAX's collectives and lax.ppermute only.
A program may use at most 128 MiB of HBM per device.

v0:
```python
import jax
import jax.numpy as jnp
from jax import lax
from jax.sharding import PartitionSpec as P

epsilon = 1e-06


def normalize_rows(values):
    return -values * lax.rsqrt(jnp.mean(values * values, axis=-1, keepdims=True) + epsilon)


def local(hidden_rows, row_counts, target_rows, joined_weight, norm_gain):
    slot_count = hidden_rows.shape[0]
    block_rows = joined_weight.shape[0]
    replicas = lax.axis_size("replica")
    shards = lax.axis_size("shard")
    live = (lax.broadcasted_iota(jnp.int32, (slot_count, 1), 0) < row_counts[0]).astype(jnp.float32)
    row_total = hidden_rows.shape[0]
    set_weight = lax.all_gather(joined_weight, "replica", axis=0, tiled=True)
    split_rows = hidden_rows.reshape(row_total, replicas, shards, block_rows)
    pieces = lax.all_to_all(split_rows, "shard", split_axis=2, concat_axis=0, tiled=True).reshape(
        shards * row_total, replicas * block_rows
    )
    block = pieces
    joined = lax.psum_scatter(
        jnp.dot(block, set_weight, preferred_element_type=jnp.float32).astype(jnp.bfloat16),
        "shard",
        scatter_dimension=0,
        tiled=True,
    ).astype(jnp.float32)
    inverse = lax.rsqrt(jnp.mean(joined * joined, axis=1, keepdims=True) + epsilon)
    normed = joined * inverse
    error = live * (normed * norm_gain - target_rows.astype(jnp.float32))
    scaled = error * norm_gain
    joined_grad = (
        inverse * (scaled - normed * jnp.mean(scaled * normed, axis=1, keepdims=True))
    ).astype(jnp.bfloat16)
    block = pieces
    weight_grad = lax.dot_general(
        block,
        lax.all_gather(joined_grad, "shard", axis=0, tiled=True),
        (((0,), (0,)), ((), ())),
        preferred_element_type=jnp.float32,
    )
    owned_grad = lax.psum_scatter(weight_grad, "replica", scatter_dimension=0, tiled=True)
    weight_step = normalize_rows(owned_grad).astype(jnp.bfloat16)
    return weight_step


def solution(mesh):
    return jax.shard_map(
        local,
        mesh=mesh,
        in_specs=(
            P(("replica", "shard"), None),
            P(("replica", "shard")),
            P(("replica", "shard"), None),
            P(("replica", "shard"), None),
            P(),
        ),
        out_specs=P(("replica", "shard"), None),
        check_vma=False,
    )
```

profile of v0, /device:TPU:0, one launch (start us, length us, event | category | flops | bytes accessed | tf_op | source)
XLA Modules:
  0.0 445.4 jit_solution(6674516404343295079)
XLA Ops:
  6.5 0.0 all-gather.3.cloned.1.call-start
  6.5 0.7 all-gather.3.cloned.1.call-update
  7.3 0.0 reduce-scatter.5.cloned.1.call-start
  7.3 3.2 copy.14
  10.5 0.2 copy.15
  10.7 6.3 %all_to_all.15 = bf16[256,64,2,48]{0,3,1,2:T(8,128)(2,1)S(1)} all-to-all(bf16[256,64,2,48]{0,3,1,2:T(8,128)(2,1)S(1)} %copy.15), channel_id=1, replica_groups=mesh['replica'=64,'shard'=2] {'shard'}, dimensions={2} | all-to-all | bytes 6291456 | tf_op jit(solution)/shard_map/all_to_all | solution.py:22
  17.0 3.2 copy.16
  20.2 0.7 copy.20
  20.9 0.0 copy-start.2
  20.9 82.8 %all-gather.3.cloned.1.call-done = bf16[3072,2048]{1,0:T(8,128)(2,1)} async-done(((bf16[48,2048]{1,0:T(8,128)(2,1)}), bf16[3072,2048]{1,0:T(8,128)(2,1)}) %all-gather.3.cloned.1.call-update) | async-done | bytes 12582928 | tf_op jit(solution)/shard_map/all_gather | solution.py:20
  103.7 0.0 copy-done.2
  103.7 10.7 %convolution_convert_fusion = bf16[512,2048]{1,0:T(8,128)(2,1)} fusion(bf16[512,3072]{0,1:T(8,128)(2,1)S(1)} %bitcast.21, bf16[3072,2048]{1,0:T(8,128)(2,1)} %all-gather.3.cloned.1.call-done), kind=kOutput, calls=%fused_computation.1 | convolution fusion | flops 6443499520 | bytes 17825792 | tf_op jit(solution)/shard_map/dot_general | solution.py:27
  114.4 0.0 reduce-scatter.5.cloned.1.call-update
  114.4 0.0 all-gather.5.cloned.1.call-start
  115.2 11.1 %reduce-scatter.5.cloned.1.call-done = bf16[256,2048]{1,0:T(8,128)(2,1)} async-done(((bf16[512,2048]{1,0:T(8,128)(2,1)}), bf16[256,2048]{1,0:T(8,128)(2,1)}) %reduce-scatter.5.cloned.1.call-update) | async-done | bytes 1048592 | tf_op jit(solution)/shard_map/reduce_scatter | solution.py:26
  126.4 1.6 fusion.10
  128.0 0.0 copy-done.1
  128.0 0.0 copy-done.4
  128.0 2.0 fusion.6
  130.0 0.0 copy-done
  130.0 1.8 fusion.9
  131.8 0.0 all-gather.5.cloned.1.call-update
  131.8 0.2 reduce-scatter.7.cloned.1.call-start
  132.0 14.6 %all-gather.5.cloned.1.call-done = bf16[512,2048]{1,0:T(8,128)(2,1)} async-done(((bf16[256,2048]{1,0:T(8,128)(2,1)}), bf16[512,2048]{1,0:T(8,128)(2,1)}) %all-gather.5.cloned.1.call-update) | async-done | bytes 2097168 | tf_op jit(solution)/shard_map/all_gather | solution.py:42
  146.6 13.9 %convolution_bitcast_fusion = f32[3072,2048]{0,1:T(8,128)} fusion(bf16[512,2048]{1,0:T(8,128)(2,1)} %all-gather.5.cloned.1.call-done, bf16[512,3072]{0,1:T(8,128)(2,1)} %bitcast.22), kind=kOutput, calls=%fused_computation | convolution fusion | flops 6442450944 | bytes 30408704 | tf_op jit(solution)/shard_map/dot_general | solution.py:40
  160.6 24.8 %copy.18 = f32[3072,2048]{1,0:T(8,128)} copy(f32[3072,2048]{0,1:T(8,128)} %convolution_bitcast_fusion) | data formatting | bytes 50331648
  185.3 0.0 reduce-scatter.7.cloned.1.call-update
  185.4 251.1 %reduce-scatter.7.cloned.1.call-done = f32[48,2048]{1,0:T(8,128)} async-done(((f32[3072,2048]{1,0:T(8,128)}), f32[48,2048]{1,0:T(8,128)}) %reduce-scatter.7.cloned.1.call-update) | async-done | bytes 393232 | tf_op jit(solution)/shard_map/reduce_scatter | solution.py:46
  436.4 1.4 copy.19
  437.8 0.3 multiply_reduce_fusion
  438.1 0.0 copy-done.3
  438.1 0.8 multiply_convert_fusion
  (8 shorter events, 0.0 us)
Async XLA Ops:
  6.5 97.1 %all-gather.3.cloned.1.call-start = ((), (), s32[]{:S(2)}) async-start(), calls=%async_computation.3 | async-start | bytes 12779520 | tf_op jit(solution)/shard_map/all_gather | solution.py:20
  7.3 119.1 %reduce-scatter.5.cloned.1.call-start = ((), (), s32[]{:S(2)}) async-start(), calls=%async_computation.4 | async-start | bytes 3145728 | tf_op jit(solution)/shard_map/reduce_scatter | solution.py:26
  20.9 82.8 %copy-start.2 = (bf16[384,8,2,256]{3,1,2,0:T(8,128)(2,1)}, bf16[384,8,2,256]{3,1,2,0:T(8,128)(2,1)S(1)}, u32[]{:S(2)}) copy-start(bf16[384,8,2,256]{3,1,2,0:T(8,128)(2,1)S(1)} %copy.20) | copy-start | bytes 9437188
  114.4 13.6 %copy-start.1 = (bf16[256,2048]{1,0:T(8,128)(2,1)S(1)}, bf16[256,2048]{1,0:T(8,128)(2,1)}, u32[]{:S(2)}) copy-start(bf16[256,2048]{1,0:T(8,128)(2,1)} %param.7) | copy-start | bytes 3145732
  114.4 13.6 %copy-start.4 = (f32[2048]{0:T(1024)S(1)}, f32[2048]{0:T(1024)}, u32[]{:S(2)}) copy-start(f32[2048]{0:T(1024)} %param.9) | copy-start | bytes 24580
  114.4 32.2 %all-gather.5.cloned.1.call-start = ((), (), s32[]{:S(2)}) async-start(), calls=%async_computation.5 | async-start | bytes 3145728 | tf_op jit(solution)/shard_map/all_gather | solution.py:42
  126.4 3.6 copy-start
  131.8 304.6 %reduce-scatter.7.cloned.1.call-start = ((), (), s32[]{:S(2)}) async-start(), calls=%async_computation.6 | async-start | bytes 25559040 | tf_op jit(solution)/shard_map/reduce_scatter | solution.py:46
  436.4 1.7 copy-start.3
Sparse Core Ops, SparseCore 0:
  10.1 93.5 all-gather.2
  114.5 11.7 reduce-scatter.4
  131.9 14.6 all-gather.4
  185.5 250.8 reduce-scatter.6
where the time goes:
time: 446 us; the launch traced here: 445 us
  waiting for transfers between devices  360 us (81%)
  local copies, waits for them, and re-layouts  33.5 us (8%)
  matrix products  24.7 us (6%)
  between operations  13.9 us (3%)
  other arithmetic  6.45 us (1%)
  blocking collectives  6.26 us (1%)
    reduce_scatter x1, waiting for transfers between devices, local(): lax.psum_scatter(weight_grad, 'replica', scatter_dimension=0, tiled=True)  251 us
    all_gather x1, waiting for transfers between devices, local(): set_weight = lax.all_gather(joined_weight, 'replica', axis=0, tiled=True)  82.8 us
    unnamed x14, local copies, waits for them, and re-layouts  30 us
    all_gather x1, waiting for transfers between devices, local(): lax.all_gather(joined_grad, 'shard', axis=0, tiled=True)  14.6 us
    dot_general x1, matrix products, local(): lax.dot_general(block, lax.all_gather(joined_grad, 'shard', axis=0, tiled...  13.9 us
    reduce_scatter x1, waiting for transfers between devices, local(): lax.psum_scatter(jnp.dot(block, set_weight, preferred_element_type=jnp.fl...  11.1 us
    dot_general x1, matrix products, local(): jnp.dot(block, set_weight, preferred_element_type=jnp.float32)  10.7 us
  transfers between devices with their start and end apart: 4, of which 4 were waited for; matrix products, arithmetic and copies ran while one was open for 2% of the time, Pallas kernels for 0%

commit v1 on v0

v1 whole, which is shorter than its diff:
```python
import jax
import jax.numpy as jnp
from jax import lax
from jax.experimental import pallas as pl
from jax.experimental.pallas import tpu as pltpu
from jax.sharding import PartitionSpec as P

epsilon = 1e-06
AXES = ("replica", "shard")
STRIDE = {"z": 16, "y": 4, "x": 1}
ROUNDS = (("z", "y", "x"), ("x", "z", "y"), ("y", "x", "z"))
F32, BF16 = jnp.float32, jnp.bfloat16


def half_place(a, core):
    if core == 0:
        return a // 2, a % 2
    return (a + 1) // 2 % 2, a // 2


def chips():
    return [(z, y, x) for z in range(4) for y in range(4) for x in range(4)]


def device(z, y, x, core):
    return (z * 16 + y * 4 + x) * 2 + core


def cubes():
    groups = {}
    for z, y, x in chips():
        for core in range(2):
            halves, places = zip(*(half_place(a, core) for a in (z, y, x)))
            groups.setdefault((core, halves), {})[places] = device(z, y, x, core)
    return [[members[k] for k in sorted(members)] for members in groups.values()]


def swap_pairs(axis):
    pairs = []
    for r in range(64):
        for core in range(2):
            a = r // STRIDE[axis] % 4
            other = r + ((a ^ (3 if core == 0 else 1)) - a) * STRIDE[axis]
            pairs.append((r * 2 + core, other * 2 + core))
    return pairs


def swap(value, axis):
    return lax.ppermute(value, AXES, swap_pairs(axis))


def swap_core(value):
    return lax.ppermute(value, "shard", [(0, 1), (1, 0)])


def cube_exchange(value):
    return lax.all_to_all(value, AXES, 0, 0, axis_index_groups=cubes(), tiled=True)


def arrange_kernel(rows_ref, out_ref):
    step = pl.program_id(0)
    z, y = step // 4, step % 4
    replica, core = lax.axis_index("replica"), lax.axis_index("shard")
    mine = {"z": replica // 16, "y": replica // 4 % 4, "x": replica % 4}
    turned = rows_ref[...].T
    for x in range(4):
        for owner in range(2):
            at = {"z": z, "y": y, "x": x}
            flip, place = {}, {}
            for axis in "zyx":
                half, place[axis] = half_place(at[axis], owner)
                own_half, _ = half_place(mine[axis], owner)
                flip[axis] = lax.rem(half + own_half, 2)
            slot = place["z"] * 4 + place["y"] * 2 + place["x"]
            away = lax.rem(core + owner, 2)
            for s, order in enumerate(ROUNDS):
                chunk = flip[order[0]] + 2 * flip[order[1]] + 4 * flip[order[2]]
                first = ((x * 2 + owner) * 3 + s) * 16
                out_ref[away, s, chunk, slot] = turned[first : first + 16]


def arrange(hidden_rows):
    rows = hidden_rows.shape[0]
    return pl.pallas_call(
        arrange_kernel,
        grid=(16,),
        in_specs=[pl.BlockSpec((rows, 384), lambda i: (0, i))],
        out_specs=pl.BlockSpec((2, 3, 8, 8, 16, rows), lambda i: (0,) * 6),
        out_shape=jax.ShapeDtypeStruct((2, 3, 8, 8, 16, rows), BF16),
        compiler_params=pltpu.CompilerParams(vmem_limit_bytes=32 << 20),
        cost_estimate=pl.CostEstimate(flops=0, bytes_accessed=4 * rows * 6144, transcendentals=0),
    )(hidden_rows)


def forward_kernel(n, started, finished, *refs):
    rows_ref, pieces = refs[0], refs[1 : n + 1]
    out_ref = refs[-1]
    total = refs[n + 1][...] if started is not None else None
    for i, piece in enumerate(pieces):
        q, s = finished[i]
        part = jnp.dot(rows_ref[s, :, q * 256 : (q + 1) * 256], piece[...], preferred_element_type=F32)
        total = part if total is None else total + part
    out_ref[...] = total.astype(out_ref.dtype)


def forward(rows, pieces, places, total, dtype):
    m, width, cols = rows.shape[1], pieces[0].shape[1], 512
    n = len(pieces)

    def kernel(*refs):
        forward_kernel(n, total, places, *refs)

    operands = [rows, *pieces] + ([total] if total is not None else [])
    return pl.pallas_call(
        kernel,
        grid=(width // cols,),
        in_specs=[pl.BlockSpec(rows.shape, lambda j: (0, 0, 0))]
        + [pl.BlockSpec((256, cols), lambda j: (0, j))] * n
        + [pl.BlockSpec((m, cols), lambda j: (0, j))] * (total is not None),
        out_specs=pl.BlockSpec((m, cols), lambda j: (0, j)),
        out_shape=jax.ShapeDtypeStruct((m, width), dtype),
        compiler_params=pltpu.CompilerParams(vmem_limit_bytes=40 << 20),
        cost_estimate=pl.CostEstimate(flops=2 * m * 256 * n * width, bytes_accessed=n * 512 * width + 6 * m * width, transcendentals=0),
    )(*operands)


def grad_kernel(count_ref, own_ref, other_ref, target_ref, gain_ref, out_ref):
    tile = out_ref.shape[0]
    row = lax.broadcasted_iota(jnp.int32, (tile, 1), 0) + pl.program_id(0) * tile
    live = (row < count_ref[0]).astype(F32)
    joined = own_ref[...].astype(F32) + other_ref[...].astype(F32)
    gain = gain_ref[...]
    inverse = lax.rsqrt(jnp.mean(joined * joined, axis=1, keepdims=True) + epsilon)
    normed = joined * inverse
    error = live * (normed * gain - target_ref[...].astype(F32))
    scaled = error * gain
    mean = jnp.mean(scaled * normed, axis=1, keepdims=True)
    out_ref[...] = (inverse * (scaled - normed * mean)).astype(BF16)


def joined_grad_of(row_counts, own, other, target_rows, norm_gain):
    rows, width = target_rows.shape
    tile = 64
    block = pl.BlockSpec((tile, width), lambda i: (i, 0))
    return pl.pallas_call(
        grad_kernel,
        grid=(rows // tile,),
        in_specs=[pl.BlockSpec(memory_space=pltpu.SMEM), block, block, block, pl.BlockSpec((1, width), lambda i: (0, 0))],
        out_specs=block,
        out_shape=jax.ShapeDtypeStruct((rows, width), BF16),
        compiler_params=pltpu.CompilerParams(vmem_limit_bytes=32 << 20),
        cost_estimate=pl.CostEstimate(flops=12 * rows * width, bytes_accessed=8 * rows * width, transcendentals=rows),
    )(row_counts, own, other, target_rows, norm_gain.reshape(1, width))


def normalize_rows(values):
    return -values * lax.rsqrt(jnp.mean(values * values, axis=-1, keepdims=True) + epsilon)


def local(hidden_rows, row_counts, target_rows, joined_weight, norm_gain):
    row_total, width = target_rows.shape
    streams = range(3)

    near = cube_exchange(jnp.tile(joined_weight, (8, 1))).reshape(8, 3, 16, width)
    first = [near[:, s].reshape(128, width) for s in streams]
    second = [swap(first[s], ROUNDS[s][0]) for s in streams]
    quarter = [[jnp.concatenate([first[s], second[s]], 0) for s in streams]]
    quarter.append([swap(quarter[0][s], ROUNDS[s][1]) for s in streams])
    quarter.append([swap(quarter[0][s], ROUNDS[s][2]) for s in streams])
    quarter.append([swap(quarter[1][s], ROUNDS[s][2]) for s in streams])

    both = arrange(hidden_rows).reshape(2, 3, 1024, row_total)
    features = jnp.concatenate([both[0], swap_core(both[1])], axis=-1)
    rows = jnp.swapaxes(features, 1, 2)

    places = [(q, s) for q in range(3) for s in streams]
    total = forward(rows, [quarter[q][s] for q, s in places], places, None, F32)
    places = [(3, s) for s in streams]
    joined = forward(rows, quarter[3], places, total, BF16)
    grad = joined_grad_of(row_counts, joined[:row_total], swap_core(joined[row_total:]), target_rows, norm_gain)
    grads = jnp.concatenate([grad, swap_core(grad)], 0)

    def product(s, q):
        return jnp.dot(features[s, q * 256 : (q + 1) * 256], grads, preferred_element_type=F32)

    sent = [product(s, 3).astype(BF16) for s in streams]
    got3 = [swap(sent[s], ROUNDS[s][2]) for s in streams]
    sent = [product(s, 2).astype(BF16) for s in streams]
    got2 = [swap(sent[s], ROUNDS[s][2]) for s in streams]
    sent = [(product(s, 1) + got3[s].astype(F32)).astype(BF16) for s in streams]
    got1 = [swap(sent[s], ROUNDS[s][1]) for s in streams]
    kept = [product(s, 0) + got2[s].astype(F32) + got1[s].astype(F32) for s in streams]
    got0 = [swap(kept[s][128:].astype(BF16), ROUNDS[s][0]) for s in streams]
    kept = [(kept[s][:128] + got0[s].astype(F32)).astype(BF16).reshape(8, 1, 16, width) for s in streams]
    near = jnp.concatenate(kept, 1).reshape(8 * 48, width)
    owned_grad = jnp.sum(cube_exchange(near).reshape(8, 48, width).astype(F32), axis=0)
    return normalize_rows(owned_grad).astype(BF16)


def solution(mesh):
    return jax.shard_map(
        local,
        mesh=mesh,
        in_specs=(
            P(("replica", "shard"), None),
            P(("replica", "shard")),
            P(("replica", "shard"), None),
            P(("replica", "shard"), None),
            P(),
        ),
        out_specs=P(("replica", "shard"), None),
        check_vma=False,
    )
```

time: 446 us -> 182 us (0.41)
  waiting for transfers between devices: 360 us -> 68.6 us
  starting transfers between devices: 0.31 us -> 44.2 us
  local copies, waits for them, and re-layouts: 33.5 us -> 16.7 us
  matrix products: 24.7 us -> 8.87 us
  Pallas kernels: 0 us -> 15.8 us
  between operations: 13.9 us -> 0.99 us
  blocking collectives: 6.26 us -> 16.4 us
    reduce_scatter x2 -> x0, waiting for transfers between devices: 262 us -> none  [the longest x1 251 us: local(): lax.psum_scatter(weight_grad, 'replica', scatter_dimension=0, tiled=True)]
    all_gather x2 -> x0, waiting for transfers between devices: 97.4 us -> none  [the longest x1 82.8 us: local(): set_weight = lax.all_gather(joined_weight, 'replica', axis=0, tiled=True)]
    ppermute x0 -> x27, waiting for transfers between devices: none -> 59 us  [the longest x24 54.5 us: swap(): return lax.ppermute(value, AXES, swap_pairs(axis))]
    ppermute x0 -> x27, starting transfers between devices: none -> 39 us  [the longest x24 36.3 us: swap(): return lax.ppermute(value, AXES, swap_pairs(axis))]
    unnamed x14 -> x24, local copies, waits for them, and re-layouts: 30 us -> 5.21 us
    pallas_call x0 -> x4, Pallas kernels: none -> 15.8 us  [the longest x2 11.6 us: forward(): pl.pallas_call(kernel, grid=(width // cols,), in_specs=[pl.BlockSpec(rows...]
    dot_general x2 -> x12, matrix products: 24.7 us -> 8.87 us  [product(): jnp.dot(features[s, q * 256:(q + 1) * 256], grads, preferred_element_type...]
    all_to_all x1, blocking collectives: 6.26 us -> 16.4 us  [cube_exchange(): lax.all_to_all(value, AXES, 0, 0, axis_index_groups=cubes(), tiled=True)]
  transfers between devices with their start and end apart: 4 -> 28, of which waited for: 4 -> 17; matrix products, arithmetic and copies ran while one was open for 2% -> 12% of each run, Pallas kernels for 0% -> 6%
where the time goes in v1:
time: 182 us; the launch traced here: 180 us
  waiting for transfers between devices  68.6 us (38%)
  starting transfers between devices  44.2 us (24%)
  local copies, waits for them, and re-layouts  16.7 us (9%)
  blocking collectives  16.4 us (9%)
  Pallas kernels  15.8 us (9%)
  matrix products  8.87 us (5%)
  other arithmetic  8.68 us (5%)
    ppermute x24, waiting for transfers between devices, swap(): return lax.ppermute(value, AXES, swap_pairs(axis))  54.5 us
    ppermute x24, starting transfers between devices, swap(): return lax.ppermute(value, AXES, swap_pairs(axis))  36.3 us
    all_to_all x1, blocking collectives, cube_exchange(): lax.all_to_all(value, AXES, 0, 0, axis_index_groups=cubes(), tiled=True)  16.4 us
    pallas_call x2, Pallas kernels, forward(): pl.pallas_call(kernel, grid=(width // cols,), in_specs=[pl.BlockSpec(rows...  11.6 us
    all_to_all x1, waiting for transfers between devices, cube_exchange(): lax.all_to_all(value, AXES, 0, 0, axis_index_groups=cubes(), tiled=True)  9.56 us
    dot_general x12, matrix products, product(): jnp.dot(features[s, q * 256:(q + 1) * 256], grads, preferred_element_type...  8.87 us
    all_to_all x1, starting transfers between devices, cube_exchange(): lax.all_to_all(value, AXES, 0, 0, axis_index_groups=cubes(), tiled=True)  5.22 us
    unnamed x24, local copies, waits for them, and re-layouts  5.21 us
  transfers between devices with their start and end apart: 28, of which 17 were waited for; matrix products, arithmetic and copies ran while one was open for 12% of the time, Pallas kernels for 6%

profile of v1, /device:TPU:0, one launch (start us, length us, event | category | flops | bytes accessed | tf_op | source)
XLA Modules:
  0.0 180.3 jit_solution(18290682694208957932)
XLA Ops:
  0.0 2.3 %tile.2 = bf16[8,48,2048]{2,1,0:T(8,128)(2,1)} broadcast(bf16[48,2048]{1,0:T(8,128)(2,1)} %param.8), dimensions={1,2} | broadcast | bytes 1769472 | tf_op jit(solution)/shard_map/tile | solution.py:164
  2.3 5.2 %all-to-all-start = ((bf16[8,48,2048]{2,1,0:T(8,128)(2,1)}), bf16[8,48,2048]{2,1,0:T(8,128)(2,1)}, u32[]{:S(2)}, u32[]{:S(2)}) async-start(bf16[8,48,2048]{2,1,0:T(8,128)(2,1)} %tile.2), calls=%async_computation | async-start | bytes 3145728 | tf_op jit(solution)/shard_map/all_to_all | solution.py:57
  9.4 2.8 %shard_map.55 = bf16[2,3,8,8,16,256]{5,4,3,2,1,0:T(8,128)(2,1)S(1)} custom-call(bf16[256,6144]{1,0:T(8,128)(2,1)S(1)} %copy-done.1), custom_call_target="tpu_custom_call" | custom-call | bytes 6291456 | tf_op jit(solution)/shard_map/pallas_call | solution.py:84
  12.1 9.6 %all-to-all-done = bf16[8,48,2048]{2,1,0:T(8,128)(2,1)} async-done(((bf16[8,48,2048]{2,1,0:T(8,128)(2,1)}), bf16[8,48,2048]{2,1,0:T(8,128)(2,1)}, u32[]{:S(2)}, u32[]{:S(2)}) %all-to-all-start) | async-done | bytes 1572896 | tf_op jit(solution)/shard_map/all_to_all | solution.py:57
  21.7 2.6 %fusion.60 = (bf16[8,1,16,2048]{3,2,1,0:T(8,128)(2,1)}, bf16[8,1,16,2048]{3,2,1,0:T(8,128)(2,1)}, bf16[8,1,16,2048]{3,2,1,0:T(8,128)(2,1)}) fusion(bf16[8,3,16,2048]{3,2,1,0:T(8,128)(2,1)} %bitcast.4), kind=kLoop, calls=%fused_computation.100 | loop fusion | bytes 3145728 | tf_op jit(solution)/shard_map/slice | solution.py:165
  24.3 2.7 %collective-permute-start.1 = (bf16[128,2048]{1,0:T(8,128)(2,1)}, bf16[128,2048]{1,0:T(8,128)(2,1)}, u32[]{:S(2)}, u32[]{:S(2)}) collective-permute-start(bf16[128,2048]{1,0:T(8,128)(2,1)} %bitcast.5), channel_id=1, source_target_pairs={{0,96},{1,33},{2,98},{3,35},{4,100},{5,37},{6,102},{7,39},{8,104},... | collective-permute-start | bytes 1572872 | tf_op jit(solution)/shard_map/ppermute | solution.py:49
  32.5 2.3 %collective-permute-start = (bf16[3,1024,256]{1,2,0:T(8,128)(2,1)S(1)}, bf16[3,1024,256]{1,2,0:T(8,128)(2,1)S(1)}, u32[]{:S(2)}, u32[]{:S(2)}) collective-permute-start(bf16[3,1024,256]{1,2,0:T(8,128)(2,1)S(1)} %copy.8), channel_id=1, source_target_pairs={{0,1},{1,0},{2,3},{3,2},{4,5},{5,4},{6,7},{7,6},{8,9},{9,8},{10,11... | collective-permute-start | bytes 4718600 | tf_op jit(solution)/shard_map/ppermute | solution.py:53
  37.0 2.5 %collective-permute-start.2 = (bf16[256,2048]{1,0:T(8,128)(2,1)S(1)}, bf16[256,2048]{1,0:T(8,128)(2,1)}, u32[]{:S(2)}, u32[]{:S(2)}) collective-permute-start(bf16[256,2048]{1,0:T(8,128)(2,1)S(1)} %pad_maximum_fusion.3.refs_1_), channel_id=1, source_target_pairs={{0,24},{1,9},{2,26},{3,11},{4,28},{5,13},{6,30},{7,15},{8,16},{9,1... | collective-permute-start | bytes 3145736 | tf_op jit(solution)/shard_map/ppermute | solution.py:49
  39.5 2.3 %pad_maximum_fusion.4.refs_2_ = bf16[256,2048]{1,0:T(8,128)(2,1)} fusion(bf16[128,2048]{1,0:T(8,128)(2,1)} %collective-permute-done.4, bf16[128,2048]{1,0:T(8,128)(2,1)} %bitcast.6), kind=kLoop, calls=%fused_computation.57 | loop fusion | flops 2097152 | bytes 2097152 | tf_op jit(solution)/shard_map/concatenate | solution.py:167
  41.8 2.7 %collective-permute-start.5 = (bf16[256,2048]{1,0:T(8,128)(2,1)}, bf16[256,2048]{1,0:T(8,128)(2,1)}, u32[]{:S(2)}, u32[]{:S(2)}) collective-permute-start(bf16[256,2048]{1,0:T(8,128)(2,1)} %pad_maximum_fusion.4.refs_2_), channel_id=1, source_target_pairs={{0,96},{1,33},{2,98},{3,35},{4,100},{5,37},{6,102},{7,39},{8,104},... | collective-permute-start | bytes 3145736 | tf_op jit(solution)/shard_map/ppermute | solution.py:49
  47.3 2.2 %collective-permute-start.10 = (bf16[256,2048]{1,0:T(8,128)(2,1)S(1)}, bf16[256,2048]{1,0:T(8,128)(2,1)S(1)}, u32[]{:S(2)}, u32[]{:S(2)}) collective-permute-start(bf16[256,2048]{1,0:T(8,128)(2,1)S(1)} %pad_maximum_fusion.3.refs_1_), channel_id=1, source_target_pairs={{0,6},{1,3},{2,4},{3,1},{4,2},{5,7},{6,0},{7,5},{8,14},{9,11},{10,... | collective-permute-start | bytes 3145736 | tf_op jit(solution)/shard_map/ppermute | solution.py:49
  50.4 6.1 %collective-permute-done.2.refs_4_ = bf16[256,2048]{1,0:T(8,128)(2,1)} collective-permute-done((bf16[256,2048]{1,0:T(8,128)(2,1)S(1)}, bf16[256,2048]{1,0:T(8,128)(2,1)}, u32[]{:S(2)}, u32[]{:S(2)}) %collective-permute-start.2) | collective-permute-done | bytes 1048608 | tf_op jit(solution)/shard_map/ppermute | solution.py:49
  59.3 3.4 %collective-permute-done.8.refs_6_ = bf16[256,2048]{1,0:T(8,128)(2,1)} collective-permute-done((bf16[256,2048]{1,0:T(8,128)(2,1)}, bf16[256,2048]{1,0:T(8,128)(2,1)}, u32[]{:S(2)}, u32[]{:S(2)}) %collective-permute-start.8) | collective-permute-done | bytes 1048608 | tf_op jit(solution)/shard_map/ppermute | solution.py:49
  63.5 10.3 %collective-permute-done.10.refs_7_ = bf16[256,2048]{1,0:T(8,128)(2,1)S(1)} collective-permute-done((bf16[256,2048]{1,0:T(8,128)(2,1)S(1)}, bf16[256,2048]{1,0:T(8,128)(2,1)S(1)}, u32[]{:S(2)}, u32[]{:S(2)}) %collective-permute-start.10) | collective-permute-done | bytes 1048608 | tf_op jit(solution)/shard_map/ppermute | solution.py:49
  75.3 2.6 %copy.9 = bf16[3,1024,256]{1,2,0:T(8,128)(2,1)} copy(bf16[3,1024,256]{2,1,0:T(8,128)(2,1)} %bitcast.57) | data formatting | bytes 3145728 | tf_op jit(solution)/shard_map/squeeze | solution.py:173
  78.0 2.3 %fusion.refs_0_ = bf16[3,512,1024]{2,1,0:T(8,128)(2,1)S(1)} fusion(bf16[3,1024,256]{1,2,0:T(8,128)(2,1)} %copy-done.9, bf16[3,1024,256]{1,2,0:T(8,128)(2,1)} %copy.9), kind=kLoop, calls=%fused_computation.25 | loop fusion | flops 6291456 | bytes 6291456 | tf_op jit(solution)/shard_map/transpose | solution.py:174
  80.5 8.6 %shard_map.56.refs_4_ = f32[512,2048]{1,0:T(8,128)} custom-call(bf16[3,512,1024]{2,1,0:T(8,128)(2,1)S(1)} %fusion.refs_0_, bf16[256,2048]{1,0:T(8,128)(2,1)S(1)} %copy-done.4, bf16[256,2048]{1,0:T(8,128)(2,1)} %pad_maximum_fusion.4.refs_2_, bf16[256,2048]{1,0:T(8,128)(2,1)} %pad_maximum_fusion.5.refs_3_, bf16[256,2048]{1,0:T(8,128)(2,1)} %collective-permute-done.2.refs_4_, ...), custom_call_target="tpu_custom_call" | custom-call | flops 4831838208 | bytes 15728640 | tf_op jit(solution)/shard_map/pallas_call | solution.py:114
  91.0 2.2 %copy-done = f32[512,2048]{1,0:T(8,128)S(1)} copy-done((f32[512,2048]{1,0:T(8,128)S(1)}, f32[512,2048]{1,0:T(8,128)}, u32[]{:S(2)}) %copy-start) | copy-done | bytes 4194328
  93.2 3.0 %shard_map.57 = bf16[512,2048]{1,0:T(8,128)(2,1)S(1)} custom-call(bf16[3,512,1024]{2,1,0:T(8,128)(2,1)S(1)} %fusion.refs_0_, bf16[256,2048]{1,0:T(8,128)(2,1)S(1)} %collective-permute-done.3.refs_1_, bf16[256,2048]{1,0:T(8,128)(2,1)S(1)} %collective-permute-done.6.refs_2_, bf16[256,2048]{1,0:T(8,128)(2,1)S(1)} %collective-permute-done.9.refs_3_, ...), custom_call_target="tpu_custom_call" | custom-call | flops 1610612736 | bytes 9437184 | tf_op jit(solution)/shard_map/pallas_call | solution.py:114
  97.2 2.0 %collective-permute-done.13.other_ref = bf16[256,2048]{1,0:T(8,128)(2,1)S(1)} collective-permute-done((bf16[256,2048]{1,0:T(8,128)(2,1)S(1)}, bf16[256,2048]{1,0:T(8,128)(2,1)S(1)}, u32[]{:S(2)}, u32[]{:S(2)}) %collective-permute-start.13) | collective-permute-done | bytes 1048608 | tf_op jit(solution)/shard_map/ppermute | solution.py:53
  100.9 2.5 %collective-permute-done.14 = bf16[256,2048]{1,0:T(8,128)(2,1)S(1)} collective-permute-done((bf16[256,2048]{1,0:T(8,128)(2,1)S(1)}, bf16[256,2048]{1,0:T(8,128)(2,1)S(1)}, u32[]{:S(2)}, u32[]{:S(2)}) %collective-permute-start.14) | collective-permute-done | bytes 1048608 | tf_op jit(solution)/shard_map/ppermute | solution.py:53
  109.6 2.1 %collective-permute-start.15 = (bf16[256,2048]{1,0:T(8,128)(2,1)S(1)}, bf16[256,2048]{1,0:T(8,128)(2,1)S(1)}, u32[]{:S(2)}, u32[]{:S(2)}) collective-permute-start(bf16[256,2048]{1,0:T(8,128)(2,1)S(1)} %convolution_convert_fusion.5), channel_id=1, source_target_pairs={{0,6},{1,3},{2,4},{3,1},{4,2},{5,7},{6,0},{7,5},{8,14},{9,11},{10,... | collective-permute-start | bytes 3145736 | tf_op jit(solution)/shard_map/ppermute | solution.py:49
  112.4 2.5 %collective-permute-start.19 = (bf16[256,2048]{1,0:T(8,128)(2,1)S(1)}, bf16[256,2048]{1,0:T(8,128)(2,1)S(1)}, u32[]{:S(2)}, u32[]{:S(2)}) collective-permute-start(bf16[256,2048]{1,0:T(8,128)(2,1)S(1)} %convolution_convert_fusion.3), channel_id=1, source_target_pairs={{0,24},{1,9},{2,26},{3,11},{4,28},{5,13},{6,30},{7,15},{8,16},{9,1... | collective-permute-start | bytes 3145736 | tf_op jit(solution)/shard_map/ppermute | solution.py:49
  114.9 5.3 %collective-permute-done.16 = bf16[256,2048]{1,0:T(8,128)(2,1)S(1)} collective-permute-done((bf16[256,2048]{1,0:T(8,128)(2,1)S(1)}, bf16[256,2048]{1,0:T(8,128)(2,1)S(1)}, u32[]{:S(2)}, u32[]{:S(2)}) %collective-permute-start.16) | collective-permute-done | bytes 1048608 | tf_op jit(solution)/shard_map/ppermute | solution.py:49
  124.3 2.6 %collective-permute-start.23 = (bf16[256,2048]{1,0:T(8,128)(2,1)S(1)}, bf16[256,2048]{1,0:T(8,128)(2,1)S(1)}, u32[]{:S(2)}, u32[]{:S(2)}) collective-permute-start(bf16[256,2048]{1,0:T(8,128)(2,1)S(1)} %convolution_convert_fusion.1), channel_id=1, source_target_pairs={{0,96},{1,33},{2,98},{3,35},{4,100},{5,37},{6,102},{7,39},{8,104},... | collective-permute-start | bytes 3145736 | tf_op jit(solution)/shard_map/ppermute | solution.py:49
  127.6 3.8 %collective-permute-done.15 = bf16[256,2048]{1,0:T(8,128)(2,1)S(1)} collective-permute-done((bf16[256,2048]{1,0:T(8,128)(2,1)S(1)}, bf16[256,2048]{1,0:T(8,128)(2,1)S(1)}, u32[]{:S(2)}, u32[]{:S(2)}) %collective-permute-start.15) | collective-permute-done | bytes 1048608 | tf_op jit(solution)/shard_map/ppermute | solution.py:49
  132.4 12.1 %collective-permute-done.17 = bf16[256,2048]{1,0:T(8,128)(2,1)S(1)} collective-permute-done((bf16[256,2048]{1,0:T(8,128)(2,1)S(1)}, bf16[256,2048]{1,0:T(8,128)(2,1)S(1)}, u32[]{:S(2)}, u32[]{:S(2)}) %collective-permute-start.17) | collective-permute-done | bytes 1048608 | tf_op jit(solution)/shard_map/ppermute | solution.py:49
  147.0 2.3 %collective-permute-start.22 = (bf16[128,2048]{1,0:T(8,128)(2,1)S(1)}, bf16[128,2048]{1,0:T(8,128)(2,1)S(1)}, u32[]{:S(2)}, u32[]{:S(2)}) collective-permute-start(bf16[128,2048]{1,0:T(8,128)(2,1)S(1)} %slice.299), channel_id=1, source_target_pairs={{0,6},{1,3},{2,4},{3,1},{4,2},{5,7},{6,0},{7,5},{8,14},{9,11},{10,... | collective-permute-start | bytes 1572872 | tf_op jit(solution)/shard_map/ppermute | solution.py:49
  150.9 2.3 %collective-permute-start.26 = (bf16[128,2048]{1,0:T(8,128)(2,1)S(1)}, bf16[128,2048]{1,0:T(8,128)(2,1)S(1)}, u32[]{:S(2)}, u32[]{:S(2)}) collective-permute-start(bf16[128,2048]{1,0:T(8,128)(2,1)S(1)} %slice.298), channel_id=1, source_target_pairs={{0,24},{1,9},{2,26},{3,11},{4,28},{5,13},{6,30},{7,15},{8,16},{9,1... | collective-permute-start | bytes 1572872 | tf_op jit(solution)/shard_map/ppermute | solution.py:49
  153.3 2.5 %collective-permute-done.18 = bf16[128,2048]{1,0:T(8,128)(2,1)S(1)} collective-permute-done((bf16[128,2048]{1,0:T(8,128)(2,1)S(1)}, bf16[128,2048]{1,0:T(8,128)(2,1)S(1)}, u32[]{:S(2)}, u32[]{:S(2)}) %collective-permute-start.18) | collective-permute-done | bytes 524320 | tf_op jit(solution)/shard_map/ppermute | solution.py:49
  157.6 4.9 %collective-permute-done.26 = bf16[128,2048]{1,0:T(8,128)(2,1)S(1)} collective-permute-done((bf16[128,2048]{1,0:T(8,128)(2,1)S(1)}, bf16[128,2048]{1,0:T(8,128)(2,1)S(1)}, u32[]{:S(2)}, u32[]{:S(2)}) %collective-permute-start.26) | collective-permute-done | bytes 524320 | tf_op jit(solution)/shard_map/ppermute | solution.py:49
  162.7 16.4 %all_to_all.15 = bf16[8,48,2048]{2,1,0:T(8,128)(2,1)S(1)} all-to-all(bf16[8,48,2048]{2,1,0:T(8,128)(2,1)S(1)} %bitcast.56), channel_id=1, replica_groups={{0,2,8,10,32,34,40,42},{1,7,25,31,97,103,121,127},{3,5,27,29,99,101,123..., dimensions={0} | all-to-all | bytes 3145728 | tf_op jit(solution)/shard_map/all_to_all | solution.py:57
  (86 shorter events, 42.4 us)
Async XLA Ops:
  2.3 19.4 %all-to-all-start = ((bf16[8,48,2048]{2,1,0:T(8,128)(2,1)}), bf16[8,48,2048]{2,1,0:T(8,128)(2,1)}, u32[]{:S(2)}, u32[]{:S(2)}) async-start(bf16[8,48,2048]{2,1,0:T(8,128)(2,1)} %tile.2), calls=%async_computation | async-start | bytes 3145728 | tf_op jit(solution)/shard_map/all_to_all | solution.py:57
  24.3 11.4 %collective-permute-start.1 = (bf16[128,2048]{1,0:T(8,128)(2,1)}, bf16[128,2048]{1,0:T(8,128)(2,1)}, u32[]{:S(2)}, u32[]{:S(2)}) collective-permute-start(bf16[128,2048]{1,0:T(8,128)(2,1)} %bitcast.5), channel_id=1, source_target_pairs={{0,96},{1,33},{2,98},{3,35},{4,100},{5,37},{6,102},{7,39},{8,104},... | collective-permute-start | bytes 1572872 | tf_op jit(solution)/shard_map/ppermute | solution.py:49
  27.0 12.5 %collective-permute-start.4 = (bf16[128,2048]{1,0:T(8,128)(2,1)}, bf16[128,2048]{1,0:T(8,128)(2,1)}, u32[]{:S(2)}, u32[]{:S(2)}) collective-permute-start(bf16[128,2048]{1,0:T(8,128)(2,1)} %bitcast.6), channel_id=1, source_target_pairs={{0,6},{1,3},{2,4},{3,1},{4,2},{5,7},{6,0},{7,5},{8,14},{9,11},{10,... | collective-permute-start | bytes 1572872 | tf_op jit(solution)/shard_map/ppermute | solution.py:49
  32.5 17.1 %collective-permute-start = (bf16[3,1024,256]{1,2,0:T(8,128)(2,1)S(1)}, bf16[3,1024,256]{1,2,0:T(8,128)(2,1)S(1)}, u32[]{:S(2)}, u32[]{:S(2)}) collective-permute-start(bf16[3,1024,256]{1,2,0:T(8,128)(2,1)S(1)} %copy.8), channel_id=1, source_target_pairs={{0,1},{1,0},{2,3},{3,2},{4,5},{5,4},{6,7},{7,6},{8,9},{9,8},{10,11... | collective-permute-start | bytes 4718600 | tf_op jit(solution)/shard_map/ppermute | solution.py:53
  34.8 10.4 %collective-permute-start.7 = (bf16[128,2048]{1,0:T(8,128)(2,1)S(1)}, bf16[128,2048]{1,0:T(8,128)(2,1)S(1)}, u32[]{:S(2)}, u32[]{:S(2)}) collective-permute-start(bf16[128,2048]{1,0:T(8,128)(2,1)S(1)} %bitcast.59), channel_id=1, source_target_pairs={{0,24},{1,9},{2,26},{3,11},{4,28},{5,13},{6,30},{7,15},{8,16},{9,1... | collective-permute-start | bytes 1572872 | tf_op jit(solution)/shard_map/ppermute | solution.py:49
  37.0 10.3 %copy-start.3 = (bf16[256,2048]{1,0:T(8,128)(2,1)}, bf16[256,2048]{1,0:T(8,128)(2,1)S(1)}, u32[]{:S(2)}) copy-start(bf16[256,2048]{1,0:T(8,128)(2,1)S(1)} %pad_maximum_fusion.3.refs_1_) | copy-start | bytes 3145732
  37.0 19.6 %collective-permute-start.2 = (bf16[256,2048]{1,0:T(8,128)(2,1)S(1)}, bf16[256,2048]{1,0:T(8,128)(2,1)}, u32[]{:S(2)}, u32[]{:S(2)}) collective-permute-start(bf16[256,2048]{1,0:T(8,128)(2,1)S(1)} %pad_maximum_fusion.3.refs_1_), channel_id=1, source_target_pairs={{0,24},{1,9},{2,26},{3,11},{4,28},{5,13},{6,30},{7,15},{8,16},{9,1... | collective-permute-start | bytes 3145736 | tf_op jit(solution)/shard_map/ppermute | solution.py:49
  41.8 16.3 %collective-permute-start.5 = (bf16[256,2048]{1,0:T(8,128)(2,1)}, bf16[256,2048]{1,0:T(8,128)(2,1)}, u32[]{:S(2)}, u32[]{:S(2)}) collective-permute-start(bf16[256,2048]{1,0:T(8,128)(2,1)} %pad_maximum_fusion.4.refs_2_), channel_id=1, source_target_pairs={{0,96},{1,33},{2,98},{3,35},{4,100},{5,37},{6,102},{7,39},{8,104},... | collective-permute-start | bytes 3145736 | tf_op jit(solution)/shard_map/ppermute | solution.py:49
  46.3 16.3 %collective-permute-start.8 = (bf16[256,2048]{1,0:T(8,128)(2,1)}, bf16[256,2048]{1,0:T(8,128)(2,1)}, u32[]{:S(2)}, u32[]{:S(2)}) collective-permute-start(bf16[256,2048]{1,0:T(8,128)(2,1)} %pad_maximum_fusion.5.refs_3_), channel_id=1, source_target_pairs={{0,6},{1,3},{2,4},{3,1},{4,2},{5,7},{6,0},{7,5},{8,14},{9,11},{10,... | collective-permute-start | bytes 3145736 | tf_op jit(solution)/shard_map/ppermute | solution.py:49
  47.3 26.5 %collective-permute-start.10 = (bf16[256,2048]{1,0:T(8,128)(2,1)S(1)}, bf16[256,2048]{1,0:T(8,128)(2,1)S(1)}, u32[]{:S(2)}, u32[]{:S(2)}) collective-permute-start(bf16[256,2048]{1,0:T(8,128)(2,1)S(1)} %pad_maximum_fusion.3.refs_1_), channel_id=1, source_target_pairs={{0,6},{1,3},{2,4},{3,1},{4,2},{5,7},{6,0},{7,5},{8,14},{9,11},{10,... | collective-permute-start | bytes 3145736 | tf_op jit(solution)/shard_map/ppermute | solution.py:49
  49.6 24.2 %copy-start.9 = (bf16[3,1024,256]{1,2,0:T(8,128)(2,1)}, bf16[3,1024,256]{1,2,0:T(8,128)(2,1)S(1)}, u32[]{:S(2)}) copy-start(bf16[3,1024,256]{1,2,0:T(8,128)(2,1)S(1)} %collective-permute-done) | copy-start | bytes 4718596
  49.6 30.7 %collective-permute-start.11 = (bf16[256,2048]{1,0:T(8,128)(2,1)}, bf16[256,2048]{1,0:T(8,128)(2,1)}, u32[]{:S(2)}, u32[]{:S(2)}) collective-permute-start(bf16[256,2048]{1,0:T(8,128)(2,1)} %pad_maximum_fusion.4.refs_2_), channel_id=1, source_target_pairs={{0,24},{1,9},{2,26},{3,11},{4,28},{5,13},{6,30},{7,15},{8,16},{9,1... | collective-permute-start | bytes 3145736 | tf_op jit(solution)/shard_map/ppermute | solution.py:49
  56.6 23.8 %collective-permute-start.12 = (bf16[256,2048]{1,0:T(8,128)(2,1)}, bf16[256,2048]{1,0:T(8,128)(2,1)}, u32[]{:S(2)}, u32[]{:S(2)}) collective-permute-start(bf16[256,2048]{1,0:T(8,128)(2,1)} %pad_maximum_fusion.5.refs_3_), channel_id=1, source_target_pairs={{0,96},{1,33},{2,98},{3,35},{4,100},{5,37},{6,102},{7,39},{8,104},... | collective-permute-start | bytes 3145736 | tf_op jit(solution)/shard_map/ppermute | solution.py:49
  58.1 31.0 %collective-permute-start.3 = (bf16[256,2048]{1,0:T(8,128)(2,1)}, bf16[256,2048]{1,0:T(8,128)(2,1)S(1)}, u32[]{:S(2)}, u32[]{:S(2)}) collective-permute-start(bf16[256,2048]{1,0:T(8,128)(2,1)} %collective-permute-done.2.refs_4_), channel_id=1, source_target_pairs={{0,6},{1,3},{2,4},{3,1},{4,2},{5,7},{6,0},{7,5},{8,14},{9,11},{10,... | collective-permute-start | bytes 3145736 | tf_op jit(solution)/shard_map/ppermute | solution.py:49
  62.7 26.4 %collective-permute-start.6 = (bf16[256,2048]{1,0:T(8,128)(2,1)}, bf16[256,2048]{1,0:T(8,128)(2,1)S(1)}, u32[]{:S(2)}, u32[]{:S(2)}) collective-permute-start(bf16[256,2048]{1,0:T(8,128)(2,1)} %collective-permute-done.5.refs_5_), channel_id=1, source_target_pairs={{0,24},{1,9},{2,26},{3,11},{4,28},{5,13},{6,30},{7,15},{8,16},{9,1... | collective-permute-start | bytes 3145736 | tf_op jit(solution)/shard_map/ppermute | solution.py:49
  74.8 16.2 %collective-permute-start.9 = (bf16[256,2048]{1,0:T(8,128)(2,1)}, bf16[256,2048]{1,0:T(8,128)(2,1)S(1)}, u32[]{:S(2)}, u32[]{:S(2)}) collective-permute-start(bf16[256,2048]{1,0:T(8,128)(2,1)} %collective-permute-done.8.refs_6_), channel_id=1, source_target_pairs={{0,96},{1,33},{2,98},{3,35},{4,100},{5,37},{6,102},{7,39},{8,104},... | collective-permute-start | bytes 3145736 | tf_op jit(solution)/shard_map/ppermute | solution.py:49
  96.4 2.7 %collective-permute-start.13 = (bf16[256,2048]{1,0:T(8,128)(2,1)S(1)}, bf16[256,2048]{1,0:T(8,128)(2,1)S(1)}, u32[]{:S(2)}, u32[]{:S(2)}) collective-permute-start(bf16[256,2048]{1,0:T(8,128)(2,1)S(1)} %get-tuple-element.7), channel_id=1, source_target_pairs={{0,1},{1,0},{2,3},{3,2},{4,5},{5,4},{6,7},{7,6},{8,9},{9,8},{10,11... | collective-permute-start | bytes 3145736 | tf_op jit(solution)/shard_map/ppermute | solution.py:53
  99.2 4.2 %copy-start.8 = (bf16[3,1024,256]{1,2,0:T(8,128)(2,1)S(1)}, bf16[3,1024,256]{1,2,0:T(8,128)(2,1)}, u32[]{:S(2)}) copy-start(bf16[3,1024,256]{1,2,0:T(8,128)(2,1)} %copy.9) | copy-start | bytes 4718596
  99.2 4.2 %copy-start.10 = (bf16[3,1024,256]{1,2,0:T(8,128)(2,1)S(1)}, bf16[3,1024,256]{1,2,0:T(8,128)(2,1)}, u32[]{:S(2)}) copy-start(bf16[3,1024,256]{1,2,0:T(8,128)(2,1)} %copy-done.9) | copy-start | bytes 4718596
  100.6 2.7 %collective-permute-start.14 = (bf16[256,2048]{1,0:T(8,128)(2,1)S(1)}, bf16[256,2048]{1,0:T(8,128)(2,1)S(1)}, u32[]{:S(2)}, u32[]{:S(2)}) collective-permute-start(bf16[256,2048]{1,0:T(8,128)(2,1)S(1)} %shard_map.58), channel_id=1, source_target_pairs={{0,1},{1,0},{2,3},{3,2},{4,5},{5,4},{6,7},{7,6},{8,9},{9,8},{10,11... | collective-permute-start | bytes 3145736 | tf_op jit(solution)/shard_map/ppermute | solution.py:53
  104.1 16.1 %collective-permute-start.16 = (bf16[256,2048]{1,0:T(8,128)(2,1)S(1)}, bf16[256,2048]{1,0:T(8,128)(2,1)S(1)}, u32[]{:S(2)}, u32[]{:S(2)}) collective-permute-start(bf16[256,2048]{1,0:T(8,128)(2,1)S(1)} %convolution_convert_fusion.4), channel_id=1, source_target_pairs={{0,6},{1,3},{2,4},{3,1},{4,2},{5,7},{6,0},{7,5},{8,14},{9,11},{10,... | collective-permute-start | bytes 3145736 | tf_op jit(solution)/shard_map/ppermute | solution.py:49
  105.9 16.1 %collective-permute-start.20 = (bf16[256,2048]{1,0:T(8,128)(2,1)S(1)}, bf16[256,2048]{1,0:T(8,128)(2,1)S(1)}, u32[]{:S(2)}, u32[]{:S(2)}) collective-permute-start(bf16[256,2048]{1,0:T(8,128)(2,1)S(1)} %convolution_convert_fusion.2), channel_id=1, source_target_pairs={{0,24},{1,9},{2,26},{3,11},{4,28},{5,13},{6,30},{7,15},{8,16},{9,1... | collective-permute-start | bytes 3145736 | tf_op jit(solution)/shard_map/ppermute | solution.py:49
  108.0 16.3 %collective-permute-start.24 = (bf16[256,2048]{1,0:T(8,128)(2,1)S(1)}, bf16[256,2048]{1,0:T(8,128)(2,1)S(1)}, u32[]{:S(2)}, u32[]{:S(2)}) collective-permute-start(bf16[256,2048]{1,0:T(8,128)(2,1)S(1)} %convolution_convert_fusion), channel_id=1, source_target_pairs={{0,96},{1,33},{2,98},{3,35},{4,100},{5,37},{6,102},{7,39},{8,104},... | collective-permute-start | bytes 3145736 | tf_op jit(solution)/shard_map/ppermute | solution.py:49
  109.6 21.8 %collective-permute-start.15 = (bf16[256,2048]{1,0:T(8,128)(2,1)S(1)}, bf16[256,2048]{1,0:T(8,128)(2,1)S(1)}, u32[]{:S(2)}, u32[]{:S(2)}) collective-permute-start(bf16[256,2048]{1,0:T(8,128)(2,1)S(1)} %convolution_convert_fusion.5), channel_id=1, source_target_pairs={{0,6},{1,3},{2,4},{3,1},{4,2},{5,7},{6,0},{7,5},{8,14},{9,11},{10,... | collective-permute-start | bytes 3145736 | tf_op jit(solution)/shard_map/ppermute | solution.py:49
  112.4 33.8 %collective-permute-start.19 = (bf16[256,2048]{1,0:T(8,128)(2,1)S(1)}, bf16[256,2048]{1,0:T(8,128)(2,1)S(1)}, u32[]{:S(2)}, u32[]{:S(2)}) collective-permute-start(bf16[256,2048]{1,0:T(8,128)(2,1)S(1)} %convolution_convert_fusion.3), channel_id=1, source_target_pairs={{0,24},{1,9},{2,26},{3,11},{4,28},{5,13},{6,30},{7,15},{8,16},{9,1... | collective-permute-start | bytes 3145736 | tf_op jit(solution)/shard_map/ppermute | solution.py:49
  121.0 23.5 %collective-permute-start.17 = (bf16[256,2048]{1,0:T(8,128)(2,1)S(1)}, bf16[256,2048]{1,0:T(8,128)(2,1)S(1)}, u32[]{:S(2)}, u32[]{:S(2)}) collective-permute-start(bf16[256,2048]{1,0:T(8,128)(2,1)S(1)} %fusion.4), channel_id=1, source_target_pairs={{0,24},{1,9},{2,26},{3,11},{4,28},{5,13},{6,30},{7,15},{8,16},{9,1... | collective-permute-start | bytes 3145736 | tf_op jit(solution)/shard_map/ppermute | solution.py:49
  122.8 23.4 %collective-permute-start.21 = (bf16[256,2048]{1,0:T(8,128)(2,1)S(1)}, bf16[256,2048]{1,0:T(8,128)(2,1)S(1)}, u32[]{:S(2)}, u32[]{:S(2)}) collective-permute-start(bf16[256,2048]{1,0:T(8,128)(2,1)S(1)} %fusion.5), channel_id=1, source_target_pairs={{0,96},{1,33},{2,98},{3,35},{4,100},{5,37},{6,102},{7,39},{8,104},... | collective-permute-start | bytes 3145736 | tf_op jit(solution)/shard_map/ppermute | solution.py:49
  124.3 25.7 %collective-permute-start.23 = (bf16[256,2048]{1,0:T(8,128)(2,1)S(1)}, bf16[256,2048]{1,0:T(8,128)(2,1)S(1)}, u32[]{:S(2)}, u32[]{:S(2)}) collective-permute-start(bf16[256,2048]{1,0:T(8,128)(2,1)S(1)} %convolution_convert_fusion.1), channel_id=1, source_target_pairs={{0,96},{1,33},{2,98},{3,35},{4,100},{5,37},{6,102},{7,39},{8,104},... | collective-permute-start | bytes 3145736 | tf_op jit(solution)/shard_map/ppermute | solution.py:49
  131.4 18.6 %collective-permute-start.25 = (bf16[256,2048]{1,0:T(8,128)(2,1)S(1)}, bf16[256,2048]{1,0:T(8,128)(2,1)S(1)}, u32[]{:S(2)}, u32[]{:S(2)}) collective-permute-start(bf16[256,2048]{1,0:T(8,128)(2,1)S(1)} %fusion.6), channel_id=1, source_target_pairs={{0,6},{1,3},{2,4},{3,1},{4,2},{5,7},{6,0},{7,5},{8,14},{9,11},{10,... | collective-permute-start | bytes 3145736 | tf_op jit(solution)/shard_map/ppermute | solution.py:49
  145.3 10.5 %collective-permute-start.18 = (bf16[128,2048]{1,0:T(8,128)(2,1)S(1)}, bf16[128,2048]{1,0:T(8,128)(2,1)S(1)}, u32[]{:S(2)}, u32[]{:S(2)}) collective-permute-start(bf16[128,2048]{1,0:T(8,128)(2,1)S(1)} %slice.300), channel_id=1, source_target_pairs={{0,96},{1,33},{2,98},{3,35},{4,100},{5,37},{6,102},{7,39},{8,104},... | collective-permute-start | bytes 1572872 | tf_op jit(solution)/shard_map/ppermute | solution.py:49
  147.0 10.5 %collective-permute-start.22 = (bf16[128,2048]{1,0:T(8,128)(2,1)S(1)}, bf16[128,2048]{1,0:T(8,128)(2,1)S(1)}, u32[]{:S(2)}, u32[]{:S(2)}) collective-permute-start(bf16[128,2048]{1,0:T(8,128)(2,1)S(1)} %slice.299), channel_id=1, source_target_pairs={{0,6},{1,3},{2,4},{3,1},{4,2},{5,7},{6,0},{7,5},{8,14},{9,11},{10,... | collective-permute-start | bytes 1572872 | tf_op jit(solution)/shard_map/ppermute | solution.py:49
  150.9 11.5 %collective-permute-start.26 = (bf16[128,2048]{1,0:T(8,128)(2,1)S(1)}, bf16[128,2048]{1,0:T(8,128)(2,1)S(1)}, u32[]{:S(2)}, u32[]{:S(2)}) collective-permute-start(bf16[128,2048]{1,0:T(8,128)(2,1)S(1)} %slice.298), channel_id=1, source_target_pairs={{0,24},{1,9},{2,26},{3,11},{4,28},{5,13},{6,30},{7,15},{8,16},{9,1... | collective-permute-start | bytes 1572872 | tf_op jit(solution)/shard_map/ppermute | solution.py:49
  (8 other events, 19.9 us)

commit v2 on v1

v2 whole, which is shorter than its diff:
```python
import jax
import jax.numpy as jnp
from jax import lax
from jax.experimental import pallas as pl
from jax.experimental.pallas import tpu as pltpu
from jax.sharding import PartitionSpec as P

epsilon = 1e-06
AXES = ("replica", "shard")
STRIDE = {"z": 16, "y": 4, "x": 1}
ROUNDS = (("z", "y", "x"), ("x", "z", "y"), ("y", "x", "z"))
F32, BF16 = jnp.float32, jnp.bfloat16


def half_place(a, core):
    if core == 0:
        return a // 2, a % 2
    return (a + 1) // 2 % 2, a // 2


def chips():
    return [(z, y, x) for z in range(4) for y in range(4) for x in range(4)]


def device(z, y, x, core):
    return (z * 16 + y * 4 + x) * 2 + core


def cubes():
    groups = {}
    for z, y, x in chips():
        for core in range(2):
            halves, places = zip(*(half_place(a, core) for a in (z, y, x)))
            groups.setdefault((core, halves), {})[places] = device(z, y, x, core)
    return [[members[k] for k in sorted(members)] for members in groups.values()]


def swap_pairs(axis):
    pairs = []
    for r in range(64):
        for core in range(2):
            a = r // STRIDE[axis] % 4
            other = r + ((a ^ (3 if core == 0 else 1)) - a) * STRIDE[axis]
            pairs.append((r * 2 + core, other * 2 + core))
    return pairs


def swap(value, axis):
    return lax.ppermute(value, AXES, swap_pairs(axis))


def swap_core(value):
    return lax.ppermute(value, "shard", [(0, 1), (1, 0)])


def cube_exchange(value):
    return lax.all_to_all(value, AXES, 0, 0, axis_index_groups=cubes(), tiled=True)


def arrange_kernel(own_ref, other_ref, out_ref):
    step = pl.program_id(0)
    replica, core = lax.axis_index("replica"), lax.axis_index("shard")
    mine = {"z": replica // 16, "y": replica // 4 % 4, "x": replica % 4}
    m = own_ref.shape[0]
    turned = [own_ref[...].T, other_ref[...].T]
    for x in range(4):
        at = {"z": step // 4, "y": step % 4, "x": x}
        slots, orders = [], []
        for owner in range(2):
            flip, place = {}, {}
            for axis in "zyx":
                half, place[axis] = half_place(at[axis], owner)
                own_half, _ = half_place(mine[axis], owner)
                flip[axis] = lax.rem(half + own_half, 2)
            slots.append(place["z"] * 4 + place["y"] * 2 + place["x"])
            orders.append([flip[order[0]] + 2 * flip[order[1]] + 4 * flip[order[2]] for order in ROUNDS])
        slot = jnp.where(core == 0, *slots)
        chunks = [jnp.where(core == 0, *pair) for pair in zip(*orders)]
        for third in range(3):
            near = slot * 3 + third
            s = near // 8
            chunk = jnp.where(s == 0, chunks[0], jnp.where(s == 1, chunks[1], chunks[2]))
            first = (x * 6 + third) * 16
            for part, value in enumerate(turned):
                tile = jnp.where(core == 0, value[first : first + 16], value[first + 48 : first + 64])
                out_ref[s, chunk, lax.rem(near, 8), :, part * m : (part + 1) * m] = tile


def arrange(own_rows, other_rows):
    m = own_rows.shape[0]
    shape = (3, 8, 8, 16, 2 * m)
    out = pl.pallas_call(
        arrange_kernel,
        grid=(16,),
        in_specs=[pl.BlockSpec((m, 384), lambda i: (0, i))] * 2,
        out_specs=pl.BlockSpec(shape, lambda i: (0,) * 5),
        out_shape=jax.ShapeDtypeStruct(shape, BF16),
        compiler_params=pltpu.CompilerParams(vmem_limit_bytes=32 << 20),
        cost_estimate=pl.CostEstimate(flops=0, bytes_accessed=1024, transcendentals=0),
    )(own_rows, other_rows)
    return out.reshape(3, 1024, 2 * m)


def turn_kernel(in_ref, out_ref):
    out_ref[0] = in_ref[0].T


def turn(features):
    streams, k, m = features.shape
    return pl.pallas_call(
        turn_kernel,
        grid=(streams, 2),
        in_specs=[pl.BlockSpec((1, k // 2, m), lambda i, j: (i, j, 0))],
        out_specs=pl.BlockSpec((1, m, k // 2), lambda i, j: (i, 0, j)),
        out_shape=jax.ShapeDtypeStruct((streams, m, k), BF16),
        compiler_params=pltpu.CompilerParams(vmem_limit_bytes=32 << 20),
        cost_estimate=pl.CostEstimate(flops=0, bytes_accessed=1024, transcendentals=0),
    )(features)


def forward(rows, pieces, places, added, half, dtypes):
    m, width, cols = rows.shape[1] // 2, pieces[0].shape[1], 512
    n, e = len(pieces), len(added)
    halves = (0, 1) if half is None else (half,)

    def kernel(*refs):
        rows_ref, outs = refs[0], refs[1 + n + e :]
        for h, out_ref in enumerate(outs):
            total = None
            for (q, s), piece in zip(places, refs[1 : 1 + n]):
                left = rows_ref[s, h * m : (h + 1) * m, q * 256 : (q + 1) * 256]
                part = jnp.dot(left, piece[...], preferred_element_type=F32)
                total = part if total is None else total + part
            for ref in refs[1 + n + h : 1 + n + e : len(halves)]:
                total = total + ref[...].astype(F32)
            out_ref[...] = total.astype(out_ref.dtype)

    block = pl.BlockSpec((m, cols), lambda j: (0, j))
    return pl.pallas_call(
        kernel,
        grid=(width // cols,),
        in_specs=[pl.BlockSpec((3, m * len(halves), 1024), lambda j: (0, half or 0, 0))]
        + [pl.BlockSpec((256, cols), lambda j: (0, j))] * n
        + [block] * e,
        out_specs=[block] * len(halves),
        out_shape=[jax.ShapeDtypeStruct((m, width), dtype) for dtype in dtypes],
        compiler_params=pltpu.CompilerParams(vmem_limit_bytes=40 << 20),
        cost_estimate=pl.CostEstimate(
            flops=2 * m * len(halves) * 256 * n * width, bytes_accessed=n * 512 * width + 4 * (e + 2) * m * width, transcendentals=0
        ),
    )(rows, *pieces, *added)


def grad_kernel(count_ref, own_ref, other_ref, target_ref, gain_ref, out_ref):
    tile = out_ref.shape[0]
    row = lax.broadcasted_iota(jnp.int32, (tile, 1), 0) + pl.program_id(0) * tile
    live = (row < count_ref[0]).astype(F32)
    joined = own_ref[...].astype(F32) + other_ref[...].astype(F32)
    gain = gain_ref[...]
    inverse = lax.rsqrt(jnp.mean(joined * joined, axis=1, keepdims=True) + epsilon)
    normed = joined * inverse
    error = live * (normed * gain - target_ref[...].astype(F32))
    scaled = error * gain
    mean = jnp.mean(scaled * normed, axis=1, keepdims=True)
    out_ref[...] = (inverse * (scaled - normed * mean)).astype(BF16)


def joined_grad_of(row_counts, own, other, target_rows, norm_gain):
    rows, width = target_rows.shape
    tile = 64
    block = pl.BlockSpec((tile, width), lambda i: (i, 0))
    return pl.pallas_call(
        grad_kernel,
        grid=(rows // tile,),
        in_specs=[pl.BlockSpec(memory_space=pltpu.SMEM), block, block, block, pl.BlockSpec((1, width), lambda i: (0, 0))],
        out_specs=block,
        out_shape=jax.ShapeDtypeStruct((rows, width), BF16),
        compiler_params=pltpu.CompilerParams(vmem_limit_bytes=32 << 20),
        cost_estimate=pl.CostEstimate(flops=12 * rows * width, bytes_accessed=8 * rows * width, transcendentals=rows),
    )(row_counts, own, other, target_rows, norm_gain.reshape(1, width))


def normalize_rows(values):
    return -values * lax.rsqrt(jnp.mean(values * values, axis=-1, keepdims=True) + epsilon)


def local(hidden_rows, row_counts, target_rows, joined_weight, norm_gain):
    row_total, width = target_rows.shape
    streams = range(3)

    with jax.named_scope("cube"):
        away_rows = swap_core(hidden_rows)
        sent, hidden_rows = lax.optimization_barrier((jnp.tile(joined_weight, (8, 1)), hidden_rows))
        near = cube_exchange(sent)
    with jax.named_scope("arrange"):
        features = arrange(hidden_rows, away_rows)
        rows = turn(features)
        near, features, rows = lax.optimization_barrier((near, features, rows))
    first = [near[128 * s : 128 * (s + 1)] for s in streams]
    second, quarter = [None] * 3, [[None] * 3 for _ in range(4)]
    for s in streams:
        with jax.named_scope(f"gather_a{s}"):
            second[s] = swap(first[s], ROUNDS[s][0])
            quarter[0][s] = jnp.concatenate([first[s], second[s]], 0)
    for s in streams:
        with jax.named_scope(f"gather_b{s}"):
            quarter[1][s] = swap(quarter[0][s], ROUNDS[s][1])
    for s in streams:
        with jax.named_scope(f"gather_c{s}"):
            quarter[2][s] = swap(quarter[0][s], ROUNDS[s][2])
        with jax.named_scope(f"gather_d{s}"):
            quarter[3][s] = swap(quarter[1][s], ROUNDS[s][2])

    def step(quarters, added, half, dtypes):
        places = [(q, s) for q in quarters for s in streams]
        return forward(rows, [quarter[q][s] for q, s in places], places, added, half, dtypes)

    with jax.named_scope("forward0"):
        part = step((0, 1), [], None, (F32, F32))
    with jax.named_scope("forward1"):
        own, away = step((2,), part, None, (F32, BF16))
        own_rest = swap_core(away)
    with jax.named_scope("forward2"):
        (away,) = step((3,), [], 1, (BF16,))
        other = swap_core(away)
    with jax.named_scope("forward3"):
        (own,) = step((3,), [own, own_rest], 0, (F32,))
    with jax.named_scope("grad"):
        grad = joined_grad_of(row_counts, own, other, target_rows, norm_gain)
        other_grad = swap_core(grad)
        grads = jnp.concatenate([grad, other_grad], 0)

    def product(s, q):
        return jnp.dot(features[s, q * 256 : (q + 1) * 256], grads, preferred_element_type=F32)

    got, kept = [[None] * 3 for _ in range(4)], []
    for s in streams:
        with jax.named_scope(f"reduce_d{s}"):
            got[3][s] = swap(product(s, 3).astype(BF16), ROUNDS[s][2])
    for s in streams:
        with jax.named_scope(f"reduce_c{s}"):
            got[2][s] = swap(product(s, 2).astype(BF16), ROUNDS[s][2])
    for s in streams:
        with jax.named_scope(f"reduce_b{s}"):
            got[1][s] = swap((product(s, 1) + got[3][s].astype(F32)).astype(BF16), ROUNDS[s][1])
    for s in streams:
        with jax.named_scope(f"reduce_a{s}"):
            part = product(s, 0) + got[2][s].astype(F32) + got[1][s].astype(F32)
            got[0][s] = swap(part[128:].astype(BF16), ROUNDS[s][0])
            kept.append((part[:128] + got[0][s].astype(F32)).astype(BF16))
    near = jnp.concatenate(kept, 0)
    owned_grad = jnp.sum(cube_exchange(near).reshape(8, 48, width).astype(F32), axis=0)
    return normalize_rows(owned_grad).astype(BF16)


def solution(mesh):
    return jax.shard_map(
        local,
        mesh=mesh,
        in_specs=(
            P(("replica", "shard"), None),
            P(("replica", "shard")),
            P(("replica", "shard"), None),
            P(("replica", "shard"), None),
            P(),
        ),
        out_specs=P(("replica", "shard"), None),
        check_vma=False,
    )
```

time: 182 us -> 167 us (0.918)
  waiting for transfers between devices: 68.6 us -> 43.7 us
  starting transfers between devices: 44.2 us -> 64.7 us
  local copies, waits for them, and re-layouts: 16.7 us -> 5.82 us
  Pallas kernels: 15.8 us -> 24.6 us
  other arithmetic: 8.68 us -> 1.96 us
    ppermute x24, starting transfers between devices: 36.3 us -> 58.8 us  [swap(): return lax.ppermute(value, AXES, swap_pairs(axis))]
    ppermute x24, waiting for transfers between devices: 54.5 us -> 40.2 us  [swap(): return lax.ppermute(value, AXES, swap_pairs(axis))]
    pallas_call x3 -> x6, Pallas kernels: 14.4 us -> 23.1 us  [the longest x4 11.9 us: forward(): pl.pallas_call(kernel, grid=(width // cols,), in_specs=[pl.BlockSpec((3,...]
    all_to_all x1, waiting for transfers between devices: 9.56 us -> 1.27 us  [cube_exchange(): lax.all_to_all(value, AXES, 0, 0, axis_index_groups=cubes(), tiled=True)]
    concatenate x4, other arithmetic: 4.86 us -> 0.46 us  [the longest x3 0.3 us: local(): quarter[0][s] = jnp.concatenate([first[s], second[s]], 0)]
    squeeze x2 -> x0, local copies, waits for them, and re-layouts: 4.39 us -> none  [local(): features = jnp.concatenate([both[0], swap_core(both[1])], axis=-1)]
    unnamed x24 -> x10, local copies, waits for them, and re-layouts: 5.21 us -> 1.65 us
    slice x6 -> x4, local copies, waits for them, and re-layouts: 4.88 us -> 1.71 us  [the longest x1 1.52 us: local(): first = [near[128 * s:128 * (s + 1)] for s in streams]]
  transfers between devices with their start and end apart: 28 -> 29, of which waited for: 17 -> 17; matrix products, arithmetic and copies ran while one was open for 12% -> 7% of each run, Pallas kernels for 6% -> 14%
where the time goes in v2:
time: 167 us
  starting transfers between devices  64.7 us (39%)
  waiting for transfers between devices  43.7 us (26%)
  Pallas kernels  24.6 us (15%)
  blocking collectives  16.4 us (10%)
  matrix products  8.66 us (5%)
  local copies, waits for them, and re-layouts  5.82 us (3%)
  other arithmetic  1.96 us (1%)
    ppermute x24, starting transfers between devices, swap(): return lax.ppermute(value, AXES, swap_pairs(axis))  58.8 us
    ppermute x24, waiting for transfers between devices, swap(): return lax.ppermute(value, AXES, swap_pairs(axis))  40.2 us
    all_to_all x1, blocking collectives, cube_exchange(): lax.all_to_all(value, AXES, 0, 0, axis_index_groups=cubes(), tiled=True)  16.4 us
    pallas_call x4, Pallas kernels, forward(): pl.pallas_call(kernel, grid=(width // cols,), in_specs=[pl.BlockSpec((3,...  11.9 us
    pallas_call x1, Pallas kernels, arrange(): pl.pallas_call(arrange_kernel, grid=(16,), in_specs=[pl.BlockSpec((m, 384...  9.84 us
    dot_general x12, matrix products, product(): jnp.dot(features[s, q * 256:(q + 1) * 256], grads, preferred_element_type...  8.66 us
    all_to_all x1, starting transfers between devices, cube_exchange(): lax.all_to_all(value, AXES, 0, 0, axis_index_groups=cubes(), tiled=True)  5.22 us
  transfers between devices with their start and end apart: 29, of which 17 were waited for; matrix products, arithmetic and copies ran while one was open for 7% of the time, Pallas kernels for 14%

profile of v2, /device:TPU:0, one launch (start us, length us, event | category | flops | bytes accessed | tf_op | source)
XLA Modules:
  0.0 167.0 jit_solution(7019422702156044058)
XLA Ops:
  0.0 2.5 %tile.4 = bf16[8,48,2048]{2,1,0:T(8,128)(2,1)} broadcast(bf16[48,2048]{1,0:T(8,128)(2,1)} %param.8), dimensions={1,2} | broadcast | bytes 1769472 | tf_op jit(solution)/shard_map/cube/tile | solution.py:193
  2.5 5.2 %all-to-all-start = ((bf16[8,48,2048]{2,1,0:T(8,128)(2,1)}), bf16[8,48,2048]{2,1,0:T(8,128)(2,1)}, u32[]{:S(2)}, u32[]{:S(2)}) async-start(bf16[8,48,2048]{2,1,0:T(8,128)(2,1)} %tile.4), calls=%async_computation | async-start | bytes 3145728 | tf_op jit(solution)/shard_map/cube/all_to_all | solution.py:57
  7.7 9.8 %arrange.2 = bf16[3,8,8,16,512]{4,3,2,1,0:T(8,128)(2,1)S(1)} custom-call(bf16[256,6144]{1,0:T(8,128)(2,1)S(1)} %copy-done.2, bf16[256,6144]{1,0:T(8,128)(2,1)} %collective-permute-done.other_ref), custom_call_target="tpu_custom_call" | custom-call | bytes 1024 | tf_op jit(solution)/shard_map/arrange/pallas_call | solution.py:92
  23.4 2.3 %collective-permute-start.7 = (bf16[128,2048]{1,0:T(8,128)(2,1)S(1)}, bf16[128,2048]{1,0:T(8,128)(2,1)S(1)}, u32[]{:S(2)}, u32[]{:S(2)}) collective-permute-start(bf16[128,2048]{1,0:T(8,128)(2,1)S(1)} %get-tuple-element.23), channel_id=1, source_target_pairs={{0,24},{1,9},{2,26},{3,11},{4,28},{5,13},{6,30},{7,15},{8,16},{9,1... | collective-permute-start | bytes 1572872 | tf_op jit(solution)/shard_map/gather_a2/ppermute | solution.py:49
  25.7 2.7 %collective-permute-start.4 = (bf16[128,2048]{1,0:T(8,128)(2,1)S(1)}, bf16[128,2048]{1,0:T(8,128)(2,1)S(1)}, u32[]{:S(2)}, u32[]{:S(2)}) collective-permute-start(bf16[128,2048]{1,0:T(8,128)(2,1)S(1)} %get-tuple-element.24), channel_id=1, source_target_pairs={{0,6},{1,3},{2,4},{3,1},{4,2},{5,7},{6,0},{7,5},{8,14},{9,11},{10,... | collective-permute-start | bytes 1572872 | tf_op jit(solution)/shard_map/gather_a1/ppermute | solution.py:49
  28.4 3.6 %collective-permute-start.1 = (bf16[128,2048]{1,0:T(8,128)(2,1)S(1)}, bf16[128,2048]{1,0:T(8,128)(2,1)S(1)}, u32[]{:S(2)}, u32[]{:S(2)}) collective-permute-start(bf16[128,2048]{1,0:T(8,128)(2,1)S(1)} %get-tuple-element.25), channel_id=1, source_target_pairs={{0,96},{1,33},{2,98},{3,35},{4,100},{5,37},{6,102},{7,39},{8,104},... | collective-permute-start | bytes 1572872 | tf_op jit(solution)/shard_map/gather_a0/ppermute | solution.py:49
  34.0 2.1 %collective-permute-start.8 = (bf16[256,2048]{1,0:T(8,128)(2,1)S(1)}, bf16[256,2048]{1,0:T(8,128)(2,1)S(1)}, u32[]{:S(2)}, u32[]{:S(2)}) collective-permute-start(bf16[256,2048]{1,0:T(8,128)(2,1)S(1)} %pad_maximum_fusion.4.refs_3_), channel_id=1, source_target_pairs={{0,6},{1,3},{2,4},{3,1},{4,2},{5,7},{6,0},{7,5},{8,14},{9,11},{10,... | collective-permute-start | bytes 3145736 | tf_op jit(solution)/shard_map/gather_b2/ppermute | solution.py:49
  36.2 3.7 %collective-permute-start.5 = (bf16[256,2048]{1,0:T(8,128)(2,1)S(1)}, bf16[256,2048]{1,0:T(8,128)(2,1)S(1)}, u32[]{:S(2)}, u32[]{:S(2)}) collective-permute-start(bf16[256,2048]{1,0:T(8,128)(2,1)S(1)} %pad_maximum_fusion.3.refs_2_), channel_id=1, source_target_pairs={{0,96},{1,33},{2,98},{3,35},{4,100},{5,37},{6,102},{7,39},{8,104},... | collective-permute-start | bytes 3145736 | tf_op jit(solution)/shard_map/gather_b1/ppermute | solution.py:49
  40.0 3.0 %collective-permute-start.2 = (bf16[256,2048]{1,0:T(8,128)(2,1)S(1)}, bf16[256,2048]{1,0:T(8,128)(2,1)S(1)}, u32[]{:S(2)}, u32[]{:S(2)}) collective-permute-start(bf16[256,2048]{1,0:T(8,128)(2,1)S(1)} %pad_maximum_fusion.2.refs_1_), channel_id=1, source_target_pairs={{0,24},{1,9},{2,26},{3,11},{4,28},{5,13},{6,30},{7,15},{8,16},{9,1... | collective-permute-start | bytes 3145736 | tf_op jit(solution)/shard_map/gather_b0/ppermute | solution.py:49
  43.0 2.8 %collective-permute-start.11 = (bf16[256,2048]{1,0:T(8,128)(2,1)S(1)}, bf16[256,2048]{1,0:T(8,128)(2,1)S(1)}, u32[]{:S(2)}, u32[]{:S(2)}) collective-permute-start(bf16[256,2048]{1,0:T(8,128)(2,1)S(1)} %pad_maximum_fusion.3.refs_2_), channel_id=1, source_target_pairs={{0,24},{1,9},{2,26},{3,11},{4,28},{5,13},{6,30},{7,15},{8,16},{9,1... | collective-permute-start | bytes 3145736 | tf_op jit(solution)/shard_map/gather_c1/ppermute | solution.py:49
  45.8 4.3 %collective-permute-done.8.refs_6_ = bf16[256,2048]{1,0:T(8,128)(2,1)S(1)} collective-permute-done((bf16[256,2048]{1,0:T(8,128)(2,1)S(1)}, bf16[256,2048]{1,0:T(8,128)(2,1)S(1)}, u32[]{:S(2)}, u32[]{:S(2)}) %collective-permute-start.8) | collective-permute-done | bytes 1048608 | tf_op jit(solution)/shard_map/gather_b2/ppermute | solution.py:49
  52.7 3.2 %collective-permute-start.9 = (bf16[256,2048]{1,0:T(8,128)(2,1)S(1)}, bf16[256,2048]{1,0:T(8,128)(2,1)S(1)}, u32[]{:S(2)}, u32[]{:S(2)}) collective-permute-start(bf16[256,2048]{1,0:T(8,128)(2,1)S(1)} %collective-permute-done.8.refs_6_), channel_id=1, source_target_pairs={{0,96},{1,33},{2,98},{3,35},{4,100},{5,37},{6,102},{7,39},{8,104},... | collective-permute-start | bytes 3145736 | tf_op jit(solution)/shard_map/gather_d2/ppermute | solution.py:49
  56.1 2.9 %collective-permute-start.6 = (bf16[256,2048]{1,0:T(8,128)(2,1)S(1)}, bf16[256,2048]{1,0:T(8,128)(2,1)S(1)}, u32[]{:S(2)}, u32[]{:S(2)}) collective-permute-start(bf16[256,2048]{1,0:T(8,128)(2,1)S(1)} %collective-permute-done.5.refs_5_), channel_id=1, source_target_pairs={{0,24},{1,9},{2,26},{3,11},{4,28},{5,13},{6,30},{7,15},{8,16},{9,1... | collective-permute-start | bytes 3145736 | tf_op jit(solution)/shard_map/gather_d1/ppermute | solution.py:49
  59.0 4.9 %collective-permute-done.12.refs_3_ = bf16[256,2048]{1,0:T(8,128)(2,1)S(1)} collective-permute-done((bf16[256,2048]{1,0:T(8,128)(2,1)S(1)}, bf16[256,2048]{1,0:T(8,128)(2,1)S(1)}, u32[]{:S(2)}, u32[]{:S(2)}) %collective-permute-start.12) | collective-permute-done | bytes 1048608 | tf_op jit(solution)/shard_map/gather_c2/ppermute | solution.py:49
  63.9 2.7 %collective-permute-start.3 = (bf16[256,2048]{1,0:T(8,128)(2,1)S(1)}, bf16[256,2048]{1,0:T(8,128)(2,1)S(1)}, u32[]{:S(2)}, u32[]{:S(2)}) collective-permute-start(bf16[256,2048]{1,0:T(8,128)(2,1)S(1)} %collective-permute-done.2.refs_4_), channel_id=1, source_target_pairs={{0,6},{1,3},{2,4},{3,1},{4,2},{5,7},{6,0},{7,5},{8,14},{9,11},{10,... | collective-permute-start | bytes 3145736 | tf_op jit(solution)/shard_map/gather_d0/ppermute | solution.py:49
  66.6 4.7 %forward0.1 = (f32[256,2048]{1,0:T(8,128)S(1)}, f32[256,2048]{1,0:T(8,128)S(1)}) custom-call(bf16[3,512,1024]{2,1,0:T(8,128)(2,1)S(1)} %arrange.3.refs_0_, bf16[256,2048]{1,0:T(8,128)(2,1)S(1)} %pad_maximum_fusion.2.refs_1_, bf16[256,2048]{1,0:T(8,128)(2,1)S(1)} %pad_maximum_fusion.3.refs_2_, bf16[256,2048]{1,0:T(8,128)(2,1)S(1)} %pad_maximum_fusion.4.refs_3_, ...), custom_call_target="tpu_custom_call" | custom-call | flops 3221225472 | bytes 10485760 | tf_op jit(solution)/shard_map/forward0/pallas_call | solution.py:139
  71.3 3.1 %forward1.1 = (f32[256,2048]{1,0:T(8,128)S(1)}, bf16[256,2048]{1,0:T(8,128)(2,1)S(1)}) custom-call(bf16[3,512,1024]{2,1,0:T(8,128)(2,1)S(1)} %arrange.3.refs_0_, bf16[256,2048]{1,0:T(8,128)(2,1)S(1)} %collective-permute-done.10.refs_1_, bf16[256,2048]{1,0:T(8,128)(2,1)S(1)} %collective-permute-done.11.refs_2_, ...), custom_call_target="tpu_custom_call" | custom-call | flops 1610612736 | bytes 11534336 | tf_op jit(solution)/shard_map/forward1/pallas_call | solution.py:139
  75.1 3.4 %collective-permute-done.6.refs_2_ = bf16[256,2048]{1,0:T(8,128)(2,1)S(1)} collective-permute-done((bf16[256,2048]{1,0:T(8,128)(2,1)S(1)}, bf16[256,2048]{1,0:T(8,128)(2,1)S(1)}, u32[]{:S(2)}, u32[]{:S(2)}) %collective-permute-start.6) | collective-permute-done | bytes 1048608 | tf_op jit(solution)/shard_map/gather_d1/ppermute | solution.py:49
  82.6 2.2 %forward3.1.own_ref = f32[256,2048]{1,0:T(8,128)S(1)} custom-call(bf16[3,512,1024]{2,1,0:T(8,128)(2,1)S(1)} %arrange.3.refs_0_, bf16[256,2048]{1,0:T(8,128)(2,1)S(1)} %collective-permute-done.3.refs_1_, bf16[256,2048]{1,0:T(8,128)(2,1)S(1)} %collective-permute-done.6.refs_2_, bf16[256,2048]{1,0:T(8,128)(2,1)S(1)} %collective-permute-done.9.refs_3_, ...), custom_call_target="tpu_custom_call" | custom-call | flops 805306368 | bytes 11534336 | tf_op jit(solution)/shard_map/forward3/pallas_call | solution.py:139
  86.9 2.3 %collective-permute-done.15 = bf16[256,2048]{1,0:T(8,128)(2,1)S(1)} collective-permute-done((bf16[256,2048]{1,0:T(8,128)(2,1)S(1)}, bf16[256,2048]{1,0:T(8,128)(2,1)S(1)}, u32[]{:S(2)}, u32[]{:S(2)}) %collective-permute-start.15) | collective-permute-done | bytes 1048608 | tf_op jit(solution)/shard_map/grad/ppermute | solution.py:53
  89.9 2.8 %collective-permute-start.17 = (bf16[256,2048]{1,0:T(8,128)(2,1)S(1)}, bf16[256,2048]{1,0:T(8,128)(2,1)S(1)}, u32[]{:S(2)}, u32[]{:S(2)}) collective-permute-start(bf16[256,2048]{1,0:T(8,128)(2,1)S(1)} %convolution_convert_fusion.4), channel_id=1, source_target_pairs={{0,6},{1,3},{2,4},{3,1},{4,2},{5,7},{6,0},{7,5},{8,14},{9,11},{10,... | collective-permute-start | bytes 3145736 | tf_op jit(solution)/shard_map/reduce_d0/ppermute | solution.py:49
  94.9 2.8 %collective-permute-start.16 = (bf16[256,2048]{1,0:T(8,128)(2,1)S(1)}, bf16[256,2048]{1,0:T(8,128)(2,1)S(1)}, u32[]{:S(2)}, u32[]{:S(2)}) collective-permute-start(bf16[256,2048]{1,0:T(8,128)(2,1)S(1)} %convolution_convert_fusion.5), channel_id=1, source_target_pairs={{0,6},{1,3},{2,4},{3,1},{4,2},{5,7},{6,0},{7,5},{8,14},{9,11},{10,... | collective-permute-start | bytes 3145736 | tf_op jit(solution)/shard_map/reduce_c0/ppermute | solution.py:49
  98.4 3.5 %collective-permute-start.25 = (bf16[256,2048]{1,0:T(8,128)(2,1)S(1)}, bf16[256,2048]{1,0:T(8,128)(2,1)S(1)}, u32[]{:S(2)}, u32[]{:S(2)}) collective-permute-start(bf16[256,2048]{1,0:T(8,128)(2,1)S(1)} %convolution_convert_fusion), channel_id=1, source_target_pairs={{0,96},{1,33},{2,98},{3,35},{4,100},{5,37},{6,102},{7,39},{8,104},... | collective-permute-start | bytes 3145736 | tf_op jit(solution)/shard_map/reduce_d2/ppermute | solution.py:49
  103.1 2.9 %collective-permute-done.17 = bf16[256,2048]{1,0:T(8,128)(2,1)S(1)} collective-permute-done((bf16[256,2048]{1,0:T(8,128)(2,1)S(1)}, bf16[256,2048]{1,0:T(8,128)(2,1)S(1)}, u32[]{:S(2)}, u32[]{:S(2)}) %collective-permute-start.17) | collective-permute-done | bytes 1048608 | tf_op jit(solution)/shard_map/reduce_d0/ppermute | solution.py:49
  106.7 3.0 %collective-permute-start.18 = (bf16[256,2048]{1,0:T(8,128)(2,1)S(1)}, bf16[256,2048]{1,0:T(8,128)(2,1)S(1)}, u32[]{:S(2)}, u32[]{:S(2)}) collective-permute-start(bf16[256,2048]{1,0:T(8,128)(2,1)S(1)} %fusion.3), channel_id=1, source_target_pairs={{0,24},{1,9},{2,26},{3,11},{4,28},{5,13},{6,30},{7,15},{8,16},{9,1... | collective-permute-start | bytes 3145736 | tf_op jit(solution)/shard_map/reduce_b0/ppermute | solution.py:49
  110.4 3.3 %collective-permute-start.22 = (bf16[256,2048]{1,0:T(8,128)(2,1)S(1)}, bf16[256,2048]{1,0:T(8,128)(2,1)S(1)}, u32[]{:S(2)}, u32[]{:S(2)}) collective-permute-start(bf16[256,2048]{1,0:T(8,128)(2,1)S(1)} %fusion.4), channel_id=1, source_target_pairs={{0,96},{1,33},{2,98},{3,35},{4,100},{5,37},{6,102},{7,39},{8,104},... | collective-permute-start | bytes 3145736 | tf_op jit(solution)/shard_map/reduce_b1/ppermute | solution.py:49
  114.7 3.2 %collective-permute-start.24 = (bf16[256,2048]{1,0:T(8,128)(2,1)S(1)}, bf16[256,2048]{1,0:T(8,128)(2,1)S(1)}, u32[]{:S(2)}, u32[]{:S(2)}) collective-permute-start(bf16[256,2048]{1,0:T(8,128)(2,1)S(1)} %convolution_convert_fusion.1), channel_id=1, source_target_pairs={{0,96},{1,33},{2,98},{3,35},{4,100},{5,37},{6,102},{7,39},{8,104},... | collective-permute-start | bytes 3145736 | tf_op jit(solution)/shard_map/reduce_c2/ppermute | solution.py:49
  119.9 12.0 %collective-permute-done.18 = bf16[256,2048]{1,0:T(8,128)(2,1)S(1)} collective-permute-done((bf16[256,2048]{1,0:T(8,128)(2,1)S(1)}, bf16[256,2048]{1,0:T(8,128)(2,1)S(1)}, u32[]{:S(2)}, u32[]{:S(2)}) %collective-permute-start.18) | collective-permute-done | bytes 1048608 | tf_op jit(solution)/shard_map/reduce_b0/ppermute | solution.py:49
  132.8 3.3 %collective-permute-start.19 = (bf16[128,2048]{1,0:T(8,128)(2,1)S(1)}, bf16[128,2048]{1,0:T(8,128)(2,1)S(1)}, u32[]{:S(2)}, u32[]{:S(2)}) collective-permute-start(bf16[128,2048]{1,0:T(8,128)(2,1)S(1)} %slice.155), channel_id=1, source_target_pairs={{0,96},{1,33},{2,98},{3,35},{4,100},{5,37},{6,102},{7,39},{8,104},... | collective-permute-start | bytes 1572872 | tf_op jit(solution)/shard_map/reduce_a0/ppermute | solution.py:49
  138.6 2.8 %collective-permute-start.27 = (bf16[128,2048]{1,0:T(8,128)(2,1)S(1)}, bf16[128,2048]{1,0:T(8,128)(2,1)S(1)}, u32[]{:S(2)}, u32[]{:S(2)}) collective-permute-start(bf16[128,2048]{1,0:T(8,128)(2,1)S(1)} %slice.153), channel_id=1, source_target_pairs={{0,24},{1,9},{2,26},{3,11},{4,28},{5,13},{6,30},{7,15},{8,16},{9,1... | collective-permute-start | bytes 1572872 | tf_op jit(solution)/shard_map/reduce_a2/ppermute | solution.py:49
  143.5 3.9 %collective-permute-done.23 = bf16[128,2048]{1,0:T(8,128)(2,1)S(1)} collective-permute-done((bf16[128,2048]{1,0:T(8,128)(2,1)S(1)}, bf16[128,2048]{1,0:T(8,128)(2,1)S(1)}, u32[]{:S(2)}, u32[]{:S(2)}) %collective-permute-start.23) | collective-permute-done | bytes 524320 | tf_op jit(solution)/shard_map/reduce_a1/ppermute | solution.py:49
  149.4 16.4 %all_to_all.21 = bf16[8,48,2048]{2,1,0:T(8,128)(2,1)S(1)} all-to-all(bf16[8,48,2048]{2,1,0:T(8,128)(2,1)S(1)} %bitcast.56), channel_id=1, replica_groups={{0,2,8,10,32,34,40,42},{1,7,25,31,97,103,121,127},{3,5,27,29,99,101,123..., dimensions={0} | all-to-all | bytes 3145728 | tf_op jit(solution)/shard_map/all_to_all | solution.py:57
  (72 shorter events, 34.5 us)
Async XLA Ops:
  0.0 7.7 %copy-start.2 = (bf16[256,6144]{1,0:T(8,128)(2,1)S(1)}, bf16[256,6144]{1,0:T(8,128)(2,1)}, u32[]{:S(2)}) copy-start(bf16[256,6144]{1,0:T(8,128)(2,1)} %own_ref) | copy-start | bytes 9437188
  0.0 7.7 %collective-permute-start = (bf16[256,6144]{1,0:T(8,128)(2,1)}, bf16[256,6144]{1,0:T(8,128)(2,1)}, u32[]{:S(2)}, u32[]{:S(2)}) collective-permute-start(bf16[256,6144]{1,0:T(8,128)(2,1)} %own_ref), channel_id=1, source_target_pairs={{0,1},{1,0},{2,3},{3,2},{4,5},{5,4},{6,7},{7,6},{8,9},{9,8},{10,11... | collective-permute-start | bytes 9437192 | tf_op jit(solution)/shard_map/cube/ppermute | solution.py:53
  2.5 19.4 %all-to-all-start = ((bf16[8,48,2048]{2,1,0:T(8,128)(2,1)}), bf16[8,48,2048]{2,1,0:T(8,128)(2,1)}, u32[]{:S(2)}, u32[]{:S(2)}) async-start(bf16[8,48,2048]{2,1,0:T(8,128)(2,1)} %tile.4), calls=%async_computation | async-start | bytes 3145728 | tf_op jit(solution)/shard_map/cube/all_to_all | solution.py:57
  23.4 10.5 %collective-permute-start.7 = (bf16[128,2048]{1,0:T(8,128)(2,1)S(1)}, bf16[128,2048]{1,0:T(8,128)(2,1)S(1)}, u32[]{:S(2)}, u32[]{:S(2)}) collective-permute-start(bf16[128,2048]{1,0:T(8,128)(2,1)S(1)} %get-tuple-element.23), channel_id=1, source_target_pairs={{0,24},{1,9},{2,26},{3,11},{4,28},{5,13},{6,30},{7,15},{8,16},{9,1... | collective-permute-start | bytes 1572872 | tf_op jit(solution)/shard_map/gather_a2/ppermute | solution.py:49
  25.7 10.4 %collective-permute-start.4 = (bf16[128,2048]{1,0:T(8,128)(2,1)S(1)}, bf16[128,2048]{1,0:T(8,128)(2,1)S(1)}, u32[]{:S(2)}, u32[]{:S(2)}) collective-permute-start(bf16[128,2048]{1,0:T(8,128)(2,1)S(1)} %get-tuple-element.24), channel_id=1, source_target_pairs={{0,6},{1,3},{2,4},{3,1},{4,2},{5,7},{6,0},{7,5},{8,14},{9,11},{10,... | collective-permute-start | bytes 1572872 | tf_op jit(solution)/shard_map/gather_a1/ppermute | solution.py:49
  28.4 11.5 %collective-permute-start.1 = (bf16[128,2048]{1,0:T(8,128)(2,1)S(1)}, bf16[128,2048]{1,0:T(8,128)(2,1)S(1)}, u32[]{:S(2)}, u32[]{:S(2)}) collective-permute-start(bf16[128,2048]{1,0:T(8,128)(2,1)S(1)} %get-tuple-element.25), channel_id=1, source_target_pairs={{0,96},{1,33},{2,98},{3,35},{4,100},{5,37},{6,102},{7,39},{8,104},... | collective-permute-start | bytes 1572872 | tf_op jit(solution)/shard_map/gather_a0/ppermute | solution.py:49
  34.0 16.1 %collective-permute-start.8 = (bf16[256,2048]{1,0:T(8,128)(2,1)S(1)}, bf16[256,2048]{1,0:T(8,128)(2,1)S(1)}, u32[]{:S(2)}, u32[]{:S(2)}) collective-permute-start(bf16[256,2048]{1,0:T(8,128)(2,1)S(1)} %pad_maximum_fusion.4.refs_3_), channel_id=1, source_target_pairs={{0,6},{1,3},{2,4},{3,1},{4,2},{5,7},{6,0},{7,5},{8,14},{9,11},{10,... | collective-permute-start | bytes 3145736 | tf_op jit(solution)/shard_map/gather_b2/ppermute | solution.py:49
  36.2 16.4 %collective-permute-start.5 = (bf16[256,2048]{1,0:T(8,128)(2,1)S(1)}, bf16[256,2048]{1,0:T(8,128)(2,1)S(1)}, u32[]{:S(2)}, u32[]{:S(2)}) collective-permute-start(bf16[256,2048]{1,0:T(8,128)(2,1)S(1)} %pad_maximum_fusion.3.refs_2_), channel_id=1, source_target_pairs={{0,96},{1,33},{2,98},{3,35},{4,100},{5,37},{6,102},{7,39},{8,104},... | collective-permute-start | bytes 3145736 | tf_op jit(solution)/shard_map/gather_b1/ppermute | solution.py:49
  40.0 16.1 %collective-permute-start.2 = (bf16[256,2048]{1,0:T(8,128)(2,1)S(1)}, bf16[256,2048]{1,0:T(8,128)(2,1)S(1)}, u32[]{:S(2)}, u32[]{:S(2)}) collective-permute-start(bf16[256,2048]{1,0:T(8,128)(2,1)S(1)} %pad_maximum_fusion.2.refs_1_), channel_id=1, source_target_pairs={{0,24},{1,9},{2,26},{3,11},{4,28},{5,13},{6,30},{7,15},{8,16},{9,1... | collective-permute-start | bytes 3145736 | tf_op jit(solution)/shard_map/gather_b0/ppermute | solution.py:49
  43.0 20.9 %collective-permute-start.12 = (bf16[256,2048]{1,0:T(8,128)(2,1)S(1)}, bf16[256,2048]{1,0:T(8,128)(2,1)S(1)}, u32[]{:S(2)}, u32[]{:S(2)}) collective-permute-start(bf16[256,2048]{1,0:T(8,128)(2,1)S(1)} %pad_maximum_fusion.4.refs_3_), channel_id=1, source_target_pairs={{0,96},{1,33},{2,98},{3,35},{4,100},{5,37},{6,102},{7,39},{8,104},... | collective-permute-start | bytes 3145736 | tf_op jit(solution)/shard_map/gather_c2/ppermute | solution.py:49
  43.0 28.3 %collective-permute-start.11 = (bf16[256,2048]{1,0:T(8,128)(2,1)S(1)}, bf16[256,2048]{1,0:T(8,128)(2,1)S(1)}, u32[]{:S(2)}, u32[]{:S(2)}) collective-permute-start(bf16[256,2048]{1,0:T(8,128)(2,1)S(1)} %pad_maximum_fusion.3.refs_2_), channel_id=1, source_target_pairs={{0,24},{1,9},{2,26},{3,11},{4,28},{5,13},{6,30},{7,15},{8,16},{9,1... | collective-permute-start | bytes 3145736 | tf_op jit(solution)/shard_map/gather_c1/ppermute | solution.py:49
  50.1 21.2 %collective-permute-start.10 = (bf16[256,2048]{1,0:T(8,128)(2,1)S(1)}, bf16[256,2048]{1,0:T(8,128)(2,1)S(1)}, u32[]{:S(2)}, u32[]{:S(2)}) collective-permute-start(bf16[256,2048]{1,0:T(8,128)(2,1)S(1)} %pad_maximum_fusion.2.refs_1_), channel_id=1, source_target_pairs={{0,6},{1,3},{2,4},{3,1},{4,2},{5,7},{6,0},{7,5},{8,14},{9,11},{10,... | collective-permute-start | bytes 3145736 | tf_op jit(solution)/shard_map/gather_c0/ppermute | solution.py:49
  52.7 22.5 %collective-permute-start.9 = (bf16[256,2048]{1,0:T(8,128)(2,1)S(1)}, bf16[256,2048]{1,0:T(8,128)(2,1)S(1)}, u32[]{:S(2)}, u32[]{:S(2)}) collective-permute-start(bf16[256,2048]{1,0:T(8,128)(2,1)S(1)} %collective-permute-done.8.refs_6_), channel_id=1, source_target_pairs={{0,96},{1,33},{2,98},{3,35},{4,100},{5,37},{6,102},{7,39},{8,104},... | collective-permute-start | bytes 3145736 | tf_op jit(solution)/shard_map/gather_d2/ppermute | solution.py:49
  56.1 22.5 %collective-permute-start.6 = (bf16[256,2048]{1,0:T(8,128)(2,1)S(1)}, bf16[256,2048]{1,0:T(8,128)(2,1)S(1)}, u32[]{:S(2)}, u32[]{:S(2)}) collective-permute-start(bf16[256,2048]{1,0:T(8,128)(2,1)S(1)} %collective-permute-done.5.refs_5_), channel_id=1, source_target_pairs={{0,24},{1,9},{2,26},{3,11},{4,28},{5,13},{6,30},{7,15},{8,16},{9,1... | collective-permute-start | bytes 3145736 | tf_op jit(solution)/shard_map/gather_d1/ppermute | solution.py:49
  63.9 16.0 %collective-permute-start.3 = (bf16[256,2048]{1,0:T(8,128)(2,1)S(1)}, bf16[256,2048]{1,0:T(8,128)(2,1)S(1)}, u32[]{:S(2)}, u32[]{:S(2)}) collective-permute-start(bf16[256,2048]{1,0:T(8,128)(2,1)S(1)} %collective-permute-done.2.refs_4_), channel_id=1, source_target_pairs={{0,6},{1,3},{2,4},{3,1},{4,2},{5,7},{6,0},{7,5},{8,14},{9,11},{10,... | collective-permute-start | bytes 3145736 | tf_op jit(solution)/shard_map/gather_d0/ppermute | solution.py:49
  74.4 8.1 %collective-permute-start.13 = (bf16[256,2048]{1,0:T(8,128)(2,1)S(1)}, bf16[256,2048]{1,0:T(8,128)(2,1)S(1)}, u32[]{:S(2)}, u32[]{:S(2)}) collective-permute-start(bf16[256,2048]{1,0:T(8,128)(2,1)S(1)} %get-tuple-element.22), channel_id=1, source_target_pairs={{0,1},{1,0},{2,3},{3,2},{4,5},{5,4},{6,7},{7,6},{8,9},{9,8},{10,11... | collective-permute-start | bytes 3145736 | tf_op jit(solution)/shard_map/forward1/ppermute | solution.py:53
  81.8 3.0 %collective-permute-start.14 = (bf16[256,2048]{1,0:T(8,128)(2,1)S(1)}, bf16[256,2048]{1,0:T(8,128)(2,1)S(1)}, u32[]{:S(2)}, u32[]{:S(2)}) collective-permute-start(bf16[256,2048]{1,0:T(8,128)(2,1)S(1)} %forward2.1), channel_id=1, source_target_pairs={{0,1},{1,0},{2,3},{3,2},{4,5},{5,4},{6,7},{7,6},{8,9},{9,8},{10,11... | collective-permute-start | bytes 3145736 | tf_op jit(solution)/shard_map/forward2/ppermute | solution.py:53
  82.5 2.3 %copy-start.3 = (bf16[256,2048]{1,0:T(8,128)(2,1)S(1)}, bf16[256,2048]{1,0:T(8,128)(2,1)}, u32[]{:S(2)}) copy-start(bf16[256,2048]{1,0:T(8,128)(2,1)} %target_ref.1) | copy-start | bytes 3145732
  84.8 4.3 %copy-start.1 = (bf16[3,8,8,16,512]{4,3,2,1,0:T(8,128)(2,1)S(1)}, bf16[3,8,8,16,512]{4,3,2,1,0:T(8,128)(2,1)}, u32[]{:S(2)}) copy-start(bf16[3,8,8,16,512]{4,3,2,1,0:T(8,128)(2,1)} %copy-done) | copy-start | bytes 9437188
  86.3 2.9 %collective-permute-start.15 = (bf16[256,2048]{1,0:T(8,128)(2,1)S(1)}, bf16[256,2048]{1,0:T(8,128)(2,1)S(1)}, u32[]{:S(2)}, u32[]{:S(2)}) collective-permute-start(bf16[256,2048]{1,0:T(8,128)(2,1)S(1)} %grad.1), channel_id=1, source_target_pairs={{0,1},{1,0},{2,3},{3,2},{4,5},{5,4},{6,7},{7,6},{8,9},{9,8},{10,11... | collective-permute-start | bytes 3145736 | tf_op jit(solution)/shard_map/grad/ppermute | solution.py:53
  89.9 16.1 %collective-permute-start.17 = (bf16[256,2048]{1,0:T(8,128)(2,1)S(1)}, bf16[256,2048]{1,0:T(8,128)(2,1)S(1)}, u32[]{:S(2)}, u32[]{:S(2)}) collective-permute-start(bf16[256,2048]{1,0:T(8,128)(2,1)S(1)} %convolution_convert_fusion.4), channel_id=1, source_target_pairs={{0,6},{1,3},{2,4},{3,1},{4,2},{5,7},{6,0},{7,5},{8,14},{9,11},{10,... | collective-permute-start | bytes 3145736 | tf_op jit(solution)/shard_map/reduce_d0/ppermute | solution.py:49
  93.4 16.3 %collective-permute-start.21 = (bf16[256,2048]{1,0:T(8,128)(2,1)S(1)}, bf16[256,2048]{1,0:T(8,128)(2,1)S(1)}, u32[]{:S(2)}, u32[]{:S(2)}) collective-permute-start(bf16[256,2048]{1,0:T(8,128)(2,1)S(1)} %convolution_convert_fusion.2), channel_id=1, source_target_pairs={{0,24},{1,9},{2,26},{3,11},{4,28},{5,13},{6,30},{7,15},{8,16},{9,1... | collective-permute-start | bytes 3145736 | tf_op jit(solution)/shard_map/reduce_d1/ppermute | solution.py:49
  94.9 23.8 %collective-permute-start.16 = (bf16[256,2048]{1,0:T(8,128)(2,1)S(1)}, bf16[256,2048]{1,0:T(8,128)(2,1)S(1)}, u32[]{:S(2)}, u32[]{:S(2)}) collective-permute-start(bf16[256,2048]{1,0:T(8,128)(2,1)S(1)} %convolution_convert_fusion.5), channel_id=1, source_target_pairs={{0,6},{1,3},{2,4},{3,1},{4,2},{5,7},{6,0},{7,5},{8,14},{9,11},{10,... | collective-permute-start | bytes 3145736 | tf_op jit(solution)/shard_map/reduce_c0/ppermute | solution.py:49
  98.4 16.3 %collective-permute-start.25 = (bf16[256,2048]{1,0:T(8,128)(2,1)S(1)}, bf16[256,2048]{1,0:T(8,128)(2,1)S(1)}, u32[]{:S(2)}, u32[]{:S(2)}) collective-permute-start(bf16[256,2048]{1,0:T(8,128)(2,1)S(1)} %convolution_convert_fusion), channel_id=1, source_target_pairs={{0,96},{1,33},{2,98},{3,35},{4,100},{5,37},{6,102},{7,39},{8,104},... | collective-permute-start | bytes 3145736 | tf_op jit(solution)/shard_map/reduce_d2/ppermute | solution.py:49
  102.6 33.5 %collective-permute-start.20 = (bf16[256,2048]{1,0:T(8,128)(2,1)S(1)}, bf16[256,2048]{1,0:T(8,128)(2,1)S(1)}, u32[]{:S(2)}, u32[]{:S(2)}) collective-permute-start(bf16[256,2048]{1,0:T(8,128)(2,1)S(1)} %convolution_convert_fusion.3), channel_id=1, source_target_pairs={{0,24},{1,9},{2,26},{3,11},{4,28},{5,13},{6,30},{7,15},{8,16},{9,1... | collective-permute-start | bytes 3145736 | tf_op jit(solution)/shard_map/reduce_c1/ppermute | solution.py:49
  106.7 25.3 %collective-permute-start.18 = (bf16[256,2048]{1,0:T(8,128)(2,1)S(1)}, bf16[256,2048]{1,0:T(8,128)(2,1)S(1)}, u32[]{:S(2)}, u32[]{:S(2)}) collective-permute-start(bf16[256,2048]{1,0:T(8,128)(2,1)S(1)} %fusion.3), channel_id=1, source_target_pairs={{0,24},{1,9},{2,26},{3,11},{4,28},{5,13},{6,30},{7,15},{8,16},{9,1... | collective-permute-start | bytes 3145736 | tf_op jit(solution)/shard_map/reduce_b0/ppermute | solution.py:49
  110.4 25.7 %collective-permute-start.22 = (bf16[256,2048]{1,0:T(8,128)(2,1)S(1)}, bf16[256,2048]{1,0:T(8,128)(2,1)S(1)}, u32[]{:S(2)}, u32[]{:S(2)}) collective-permute-start(bf16[256,2048]{1,0:T(8,128)(2,1)S(1)} %fusion.4), channel_id=1, source_target_pairs={{0,96},{1,33},{2,98},{3,35},{4,100},{5,37},{6,102},{7,39},{8,104},... | collective-permute-start | bytes 3145736 | tf_op jit(solution)/shard_map/reduce_b1/ppermute | solution.py:49
  114.7 23.0 %collective-permute-start.24 = (bf16[256,2048]{1,0:T(8,128)(2,1)S(1)}, bf16[256,2048]{1,0:T(8,128)(2,1)S(1)}, u32[]{:S(2)}, u32[]{:S(2)}) collective-permute-start(bf16[256,2048]{1,0:T(8,128)(2,1)S(1)} %convolution_convert_fusion.1), channel_id=1, source_target_pairs={{0,96},{1,33},{2,98},{3,35},{4,100},{5,37},{6,102},{7,39},{8,104},... | collective-permute-start | bytes 3145736 | tf_op jit(solution)/shard_map/reduce_c2/ppermute | solution.py:49
  118.7 19.1 %collective-permute-start.26 = (bf16[256,2048]{1,0:T(8,128)(2,1)S(1)}, bf16[256,2048]{1,0:T(8,128)(2,1)S(1)}, u32[]{:S(2)}, u32[]{:S(2)}) collective-permute-start(bf16[256,2048]{1,0:T(8,128)(2,1)S(1)} %fusion.5), channel_id=1, source_target_pairs={{0,6},{1,3},{2,4},{3,1},{4,2},{5,7},{6,0},{7,5},{8,14},{9,11},{10,... | collective-permute-start | bytes 3145736 | tf_op jit(solution)/shard_map/reduce_b2/ppermute | solution.py:49
  132.8 10.6 %collective-permute-start.19 = (bf16[128,2048]{1,0:T(8,128)(2,1)S(1)}, bf16[128,2048]{1,0:T(8,128)(2,1)S(1)}, u32[]{:S(2)}, u32[]{:S(2)}) collective-permute-start(bf16[128,2048]{1,0:T(8,128)(2,1)S(1)} %slice.155), channel_id=1, source_target_pairs={{0,96},{1,33},{2,98},{3,35},{4,100},{5,37},{6,102},{7,39},{8,104},... | collective-permute-start | bytes 1572872 | tf_op jit(solution)/shard_map/reduce_a0/ppermute | solution.py:49
  136.9 10.5 %collective-permute-start.23 = (bf16[128,2048]{1,0:T(8,128)(2,1)S(1)}, bf16[128,2048]{1,0:T(8,128)(2,1)S(1)}, u32[]{:S(2)}, u32[]{:S(2)}) collective-permute-start(bf16[128,2048]{1,0:T(8,128)(2,1)S(1)} %slice.154), channel_id=1, source_target_pairs={{0,6},{1,3},{2,4},{3,1},{4,2},{5,7},{6,0},{7,5},{8,14},{9,11},{10,... | collective-permute-start | bytes 1572872 | tf_op jit(solution)/shard_map/reduce_a1/ppermute | solution.py:49
  138.6 10.5 %collective-permute-start.27 = (bf16[128,2048]{1,0:T(8,128)(2,1)S(1)}, bf16[128,2048]{1,0:T(8,128)(2,1)S(1)}, u32[]{:S(2)}, u32[]{:S(2)}) collective-permute-start(bf16[128,2048]{1,0:T(8,128)(2,1)S(1)} %slice.153), channel_id=1, source_target_pairs={{0,24},{1,9},{2,26},{3,11},{4,28},{5,13},{6,30},{7,15},{8,16},{9,1... | collective-permute-start | bytes 1572872 | tf_op jit(solution)/shard_map/reduce_a2/ppermute | solution.py:49
  (2 other events, 3.9 us)

commit v3 on v2

--- a/solution.py
+++ b/solution.py
@@ -8,12 +8,13 @@
 epsilon = 1e-06
 AXES = ("replica", "shard")
 STRIDE = {"z": 16, "y": 4, "x": 1}
-ROUNDS = (("z", "y", "x"), ("x", "z", "y"), ("y", "x", "z"))
+ROUNDS = (("y", "z", "x"), ("x", "y", "z"), ("z", "x", "y"))
+LONG = ('zyx', '')
 F32, BF16 = jnp.float32, jnp.bfloat16
 
 
-def half_place(a, core):
-    if core == 0:
+def half_place(a, axis, core):
+    if axis in LONG[core]:
         return a // 2, a % 2
     return (a + 1) // 2 % 2, a // 2
 
@@ -30,7 +31,7 @@
     groups = {}
     for z, y, x in chips():
         for core in range(2):
-            halves, places = zip(*(half_place(a, core) for a in (z, y, x)))
+            halves, places = zip(*(half_place(a, axis, core) for axis, a in zip("zyx", (z, y, x))))
             groups.setdefault((core, halves), {})[places] = device(z, y, x, core)
     return [[members[k] for k in sorted(members)] for members in groups.values()]
 
@@ -40,7 +41,7 @@
     for r in range(64):
         for core in range(2):
             a = r // STRIDE[axis] % 4
-            other = r + ((a ^ (3 if core == 0 else 1)) - a) * STRIDE[axis]
+            other = r + ((a ^ (3 if axis in LONG[core] else 1)) - a) * STRIDE[axis]
             pairs.append((r * 2 + core, other * 2 + core))
     return pairs
 
@@ -58,32 +59,39 @@
 
 
 def arrange_kernel(own_ref, other_ref, out_ref):
-    step = pl.program_id(0)
+    z = pl.program_id(0)
     replica, core = lax.axis_index("replica"), lax.axis_index("shard")
     mine = {"z": replica // 16, "y": replica // 4 % 4, "x": replica % 4}
     m = own_ref.shape[0]
-    turned = [own_ref[...].T, other_ref[...].T]
-    for x in range(4):
-        at = {"z": step // 4, "y": step % 4, "x": x}
-        slots, orders = [], []
-        for owner in range(2):
-            flip, place = {}, {}
-            for axis in "zyx":
-                half, place[axis] = half_place(at[axis], owner)
-                own_half, _ = half_place(mine[axis], owner)
-                flip[axis] = lax.rem(half + own_half, 2)
-            slots.append(place["z"] * 4 + place["y"] * 2 + place["x"])
-            orders.append([flip[order[0]] + 2 * flip[order[1]] + 4 * flip[order[2]] for order in ROUNDS])
-        slot = jnp.where(core == 0, *slots)
-        chunks = [jnp.where(core == 0, *pair) for pair in zip(*orders)]
-        for third in range(3):
-            near = slot * 3 + third
-            s = near // 8
-            chunk = jnp.where(s == 0, chunks[0], jnp.where(s == 1, chunks[1], chunks[2]))
-            first = (x * 6 + third) * 16
-            for part, value in enumerate(turned):
-                tile = jnp.where(core == 0, value[first : first + 16], value[first + 48 : first + 64])
-                out_ref[s, chunk, lax.rem(near, 8), :, part * m : (part + 1) * m] = tile
+    row = lax.broadcasted_iota(jnp.int32, (192, 384), 0)
+    block = (row >= 48).astype(jnp.int32) + (row >= 96).astype(jnp.int32) + (row >= 144).astype(jnp.int32)
+    pick = lax.broadcasted_iota(jnp.int32, (192, 384), 1) == row + 48 * (block + core)
+    pick = pick.astype(F32).astype(BF16)
+    for y in range(4):
+        turned = []
+        for ref in (own_ref, other_ref):
+            value = ref[:, 384 * y : 384 * (y + 1)]
+            turned.append(lax.dot_general(pick, value, (((1,), (1,)), ((), ())), preferred_element_type=F32).astype(BF16))
+        for x in range(4):
+            at = {"z": z, "y": y, "x": x}
+            slots, orders = [], []
+            for owner in range(2):
+                flip, place = {}, {}
+                for axis in "zyx":
+                    half, place[axis] = half_place(at[axis], axis, owner)
+                    own_half, _ = half_place(mine[axis], axis, owner)
+                    flip[axis] = lax.rem(half + own_half, 2)
+                slots.append(place["z"] * 4 + place["y"] * 2 + place["x"])
+                orders.append([flip[order[0]] + 2 * flip[order[1]] + 4 * flip[order[2]] for order in ROUNDS])
+            slot = jnp.where(core == 0, *slots)
+            chunks = [jnp.where(core == 0, *pair) for pair in zip(*orders)]
+            for third in range(3):
+                near = slot * 3 + third
+                s = near // 8
+                chunk = jnp.where(s == 0, chunks[0], jnp.where(s == 1, chunks[1], chunks[2]))
+                first = (x * 3 + third) * 16
+                for part, value in enumerate(turned):
+                    out_ref[s, chunk, lax.rem(near, 8), :, part * m : (part + 1) * m] = value[first : first + 16]
 
 
 def arrange(own_rows, other_rows):
@@ -91,8 +99,8 @@
     shape = (3, 8, 8, 16, 2 * m)
     out = pl.pallas_call(
         arrange_kernel,
-        grid=(16,),
-        in_specs=[pl.BlockSpec((m, 384), lambda i: (0, i))] * 2,
+        grid=(4,),
+        in_specs=[pl.BlockSpec((m, 1536), lambda i: (0, i))] * 2,
         out_specs=pl.BlockSpec(shape, lambda i: (0,) * 5),
         out_shape=jax.ShapeDtypeStruct(shape, BF16),
         compiler_params=pltpu.CompilerParams(vmem_limit_bytes=32 << 20),
@@ -119,7 +127,7 @@
 
 
 def forward(rows, pieces, places, added, half, dtypes):
-    m, width, cols = rows.shape[1] // 2, pieces[0].shape[1], 512
+    m, width, cols = rows.shape[1] // 2, pieces[0].shape[1], 512 if half is None else 1024
     n, e = len(pieces), len(added)
     halves = (0, 1) if half is None else (half,)
 
@@ -152,28 +160,31 @@
 
 
 def grad_kernel(count_ref, own_ref, other_ref, target_ref, gain_ref, out_ref):
-    tile = out_ref.shape[0]
-    row = lax.broadcasted_iota(jnp.int32, (tile, 1), 0) + pl.program_id(0) * tile
-    live = (row < count_ref[0]).astype(F32)
-    joined = own_ref[...].astype(F32) + other_ref[...].astype(F32)
+    rows, width = out_ref.shape
+    tile = 64
     gain = gain_ref[...]
-    inverse = lax.rsqrt(jnp.mean(joined * joined, axis=1, keepdims=True) + epsilon)
-    normed = joined * inverse
-    error = live * (normed * gain - target_ref[...].astype(F32))
-    scaled = error * gain
-    mean = jnp.mean(scaled * normed, axis=1, keepdims=True)
-    out_ref[...] = (inverse * (scaled - normed * mean)).astype(BF16)
+
+    @pl.loop(0, rows // tile)
+    def _(i):
+        at = pl.ds(pl.multiple_of(i * tile, tile), tile)
+        row = lax.broadcasted_iota(jnp.int32, (tile, 1), 0) + i * tile
+        live = (row < count_ref[0]).astype(F32)
+        joined = own_ref[at, :].astype(F32) + other_ref[at, :].astype(F32)
+        inverse = lax.rsqrt(jnp.mean(joined * joined, axis=1, keepdims=True) + epsilon)
+        normed = joined * inverse
+        error = live * (normed * gain - target_ref[at, :].astype(F32))
+        scaled = error * gain
+        mean = jnp.mean(scaled * normed, axis=1, keepdims=True)
+        out_ref[at, :] = (inverse * (scaled - normed * mean)).astype(BF16)
 
 
 def joined_grad_of(row_counts, own, other, target_rows, norm_gain):
     rows, width = target_rows.shape
-    tile = 64
-    block = pl.BlockSpec((tile, width), lambda i: (i, 0))
+    whole = pl.BlockSpec(memory_space=pltpu.VMEM)
     return pl.pallas_call(
         grad_kernel,
-        grid=(rows // tile,),
-        in_specs=[pl.BlockSpec(memory_space=pltpu.SMEM), block, block, block, pl.BlockSpec((1, width), lambda i: (0, 0))],
-        out_specs=block,
+        in_specs=[pl.BlockSpec(memory_space=pltpu.SMEM)] + [whole] * 4,
+        out_specs=whole,
         out_shape=jax.ShapeDtypeStruct((rows, width), BF16),
         compiler_params=pltpu.CompilerParams(vmem_limit_bytes=32 << 20),
         cost_estimate=pl.CostEstimate(flops=12 * rows * width, bytes_accessed=8 * rows * width, transcendentals=rows),

time: 167 us -> 166 us (level)
  waiting for transfers between devices: 43.7 us -> 56.9 us
  starting transfers between devices: 64.7 us -> 56.3 us
  Pallas kernels: 24.6 us -> 18.7 us
    ppermute x24, starting transfers between devices: 58.8 us -> 50.2 us  [swap(): return lax.ppermute(value, AXES, swap_pairs(axis))]
    ppermute x24, waiting for transfers between devices: 40.2 us -> 48.2 us  [swap(): return lax.ppermute(value, AXES, swap_pairs(axis))]
    pallas_call x2, Pallas kernels: 11.3 us -> 6.19 us  [the longest x1 4.8 us: arrange(): pl.pallas_call(arrange_kernel, grid=(4,), in_specs=[pl.BlockSpec((m, 1536...]
    all_to_all x1, waiting for transfers between devices: 1.27 us -> 6.31 us  [cube_exchange(): lax.all_to_all(value, AXES, 0, 0, axis_index_groups=cubes(), tiled=True)]
  transfers between devices with their start and end apart: 29 -> 29, of which waited for: 17 -> 18; matrix products, arithmetic and copies ran while one was open for 7% -> 7% of each run, Pallas kernels for 14% -> 10%
where the time goes in v3:
time: 166 us
  waiting for transfers between devices  56.9 us (34%)
  starting transfers between devices  56.3 us (34%)
  Pallas kernels  18.7 us (11%)
  blocking collectives  16.4 us (10%)
  matrix products  8.67 us (5%)
  local copies, waits for them, and re-layouts  5.82 us (4%)
  other arithmetic  1.96 us (1%)
    ppermute x24, starting transfers between devices, swap(): return lax.ppermute(value, AXES, swap_pairs(axis))  50.2 us
    ppermute x24, waiting for transfers between devices, swap(): return lax.ppermute(value, AXES, swap_pairs(axis))  48.2 us
    all_to_all x1, blocking collectives, cube_exchange(): lax.all_to_all(value, AXES, 0, 0, axis_index_groups=cubes(), tiled=True)  16.4 us
    pallas_call x4, Pallas kernels, forward(): pl.pallas_call(kernel, grid=(width // cols,), in_specs=[pl.BlockSpec((3,...  11.1 us
    dot_general x12, matrix products, product(): jnp.dot(features[s, q * 256:(q + 1) * 256], grads, preferred_element_type...  8.67 us
    all_to_all x1, waiting for transfers between devices, cube_exchange(): lax.all_to_all(value, AXES, 0, 0, axis_index_groups=cubes(), tiled=True)  6.31 us
    all_to_all x1, starting transfers between devices, cube_exchange(): lax.all_to_all(value, AXES, 0, 0, axis_index_groups=cubes(), tiled=True)  5.22 us
    pallas_call x1, Pallas kernels, arrange(): pl.pallas_call(arrange_kernel, grid=(4,), in_specs=[pl.BlockSpec((m, 1536...  4.8 us
  transfers between devices with their start and end apart: 29, of which 18 were waited for; matrix products, arithmetic and copies ran while one was open for 7% of the time, Pallas kernels for 10%

profile of v3, /device:TPU:0, one launch (start us, length us, event | category | flops | bytes accessed | tf_op | source)
XLA Modules:
  0.0 165.8 jit_solution(16438980938746460817)
XLA Ops:
  0.0 2.5 %tile.4 = bf16[8,48,2048]{2,1,0:T(8,128)(2,1)} broadcast(bf16[48,2048]{1,0:T(8,128)(2,1)} %param.8), dimensions={1,2} | broadcast | bytes 1769472 | tf_op jit(solution)/shard_map/cube/tile | solution.py:204
  2.5 5.2 %all-to-all-start = ((bf16[8,48,2048]{2,1,0:T(8,128)(2,1)}), bf16[8,48,2048]{2,1,0:T(8,128)(2,1)}, u32[]{:S(2)}, u32[]{:S(2)}) async-start(bf16[8,48,2048]{2,1,0:T(8,128)(2,1)} %tile.4), calls=%async_computation | async-start | bytes 3145728 | tf_op jit(solution)/shard_map/cube/all_to_all | solution.py:58
  7.7 4.8 %arrange.2 = bf16[3,8,8,16,512]{4,3,2,1,0:T(8,128)(2,1)S(1)} custom-call(bf16[256,6144]{1,0:T(8,128)(2,1)S(1)} %copy-done.2, bf16[256,6144]{1,0:T(8,128)(2,1)} %collective-permute-done.other_ref), custom_call_target="tpu_custom_call" | custom-call | bytes 1024 | tf_op jit(solution)/shard_map/arrange/pallas_call | solution.py:100
  15.6 6.3 %all-to-all-done = bf16[8,48,2048]{2,1,0:T(8,128)(2,1)} async-done(((bf16[8,48,2048]{2,1,0:T(8,128)(2,1)}), bf16[8,48,2048]{2,1,0:T(8,128)(2,1)}, u32[]{:S(2)}, u32[]{:S(2)}) %all-to-all-start) | async-done | bytes 1572896 | tf_op jit(solution)/shard_map/cube/all_to_all | solution.py:58
  23.4 2.8 %collective-permute-start.7 = (bf16[128,2048]{1,0:T(8,128)(2,1)S(1)}, bf16[128,2048]{1,0:T(8,128)(2,1)S(1)}, u32[]{:S(2)}, u32[]{:S(2)}) collective-permute-start(bf16[128,2048]{1,0:T(8,128)(2,1)S(1)} %get-tuple-element.23), channel_id=1, source_target_pairs={{0,96},{1,33},{2,98},{3,35},{4,100},{5,37},{6,102},{7,39},{8,104},... | collective-permute-start | bytes 1572872 | tf_op jit(solution)/shard_map/gather_a2/ppermute | solution.py:50
  28.0 3.0 %collective-permute-start.1 = (bf16[128,2048]{1,0:T(8,128)(2,1)S(1)}, bf16[128,2048]{1,0:T(8,128)(2,1)S(1)}, u32[]{:S(2)}, u32[]{:S(2)}) collective-permute-start(bf16[128,2048]{1,0:T(8,128)(2,1)S(1)} %get-tuple-element.25), channel_id=1, source_target_pairs={{0,24},{1,9},{2,26},{3,11},{4,28},{5,13},{6,30},{7,15},{8,16},{9,1... | collective-permute-start | bytes 1572872 | tf_op jit(solution)/shard_map/gather_a0/ppermute | solution.py:50
  31.0 4.1 %collective-permute-done.7 = bf16[128,2048]{1,0:T(8,128)(2,1)S(1)} collective-permute-done((bf16[128,2048]{1,0:T(8,128)(2,1)S(1)}, bf16[128,2048]{1,0:T(8,128)(2,1)S(1)}, u32[]{:S(2)}, u32[]{:S(2)}) %collective-permute-start.7) | collective-permute-done | bytes 524320 | tf_op jit(solution)/shard_map/gather_a2/ppermute | solution.py:50
  36.7 3.1 %collective-permute-start.5 = (bf16[256,2048]{1,0:T(8,128)(2,1)S(1)}, bf16[256,2048]{1,0:T(8,128)(2,1)S(1)}, u32[]{:S(2)}, u32[]{:S(2)}) collective-permute-start(bf16[256,2048]{1,0:T(8,128)(2,1)S(1)} %pad_maximum_fusion.3.refs_2_), channel_id=1, source_target_pairs={{0,24},{1,9},{2,26},{3,11},{4,28},{5,13},{6,30},{7,15},{8,16},{9,1... | collective-permute-start | bytes 3145736 | tf_op jit(solution)/shard_map/gather_b1/ppermute | solution.py:50
  39.9 2.1 %collective-permute-start.2 = (bf16[256,2048]{1,0:T(8,128)(2,1)S(1)}, bf16[256,2048]{1,0:T(8,128)(2,1)S(1)}, u32[]{:S(2)}, u32[]{:S(2)}) collective-permute-start(bf16[256,2048]{1,0:T(8,128)(2,1)S(1)} %pad_maximum_fusion.2.refs_1_), channel_id=1, source_target_pairs={{0,96},{1,33},{2,98},{3,35},{4,100},{5,37},{6,102},{7,39},{8,104},... | collective-permute-start | bytes 3145736 | tf_op jit(solution)/shard_map/gather_b0/ppermute | solution.py:50
  42.2 2.6 %collective-permute-start.11 = (bf16[256,2048]{1,0:T(8,128)(2,1)S(1)}, bf16[256,2048]{1,0:T(8,128)(2,1)S(1)}, u32[]{:S(2)}, u32[]{:S(2)}) collective-permute-start(bf16[256,2048]{1,0:T(8,128)(2,1)S(1)} %pad_maximum_fusion.3.refs_2_), channel_id=1, source_target_pairs={{0,96},{1,33},{2,98},{3,35},{4,100},{5,37},{6,102},{7,39},{8,104},... | collective-permute-start | bytes 3145736 | tf_op jit(solution)/shard_map/gather_c1/ppermute | solution.py:50
  44.8 6.5 %collective-permute-done.8.refs_6_ = bf16[256,2048]{1,0:T(8,128)(2,1)S(1)} collective-permute-done((bf16[256,2048]{1,0:T(8,128)(2,1)S(1)}, bf16[256,2048]{1,0:T(8,128)(2,1)S(1)}, u32[]{:S(2)}, u32[]{:S(2)}) %collective-permute-start.8) | collective-permute-done | bytes 1048608 | tf_op jit(solution)/shard_map/gather_b2/ppermute | solution.py:50
  52.8 3.0 %collective-permute-start.9 = (bf16[256,2048]{1,0:T(8,128)(2,1)S(1)}, bf16[256,2048]{1,0:T(8,128)(2,1)S(1)}, u32[]{:S(2)}, u32[]{:S(2)}) collective-permute-start(bf16[256,2048]{1,0:T(8,128)(2,1)S(1)} %collective-permute-done.8.refs_6_), channel_id=1, source_target_pairs={{0,24},{1,9},{2,26},{3,11},{4,28},{5,13},{6,30},{7,15},{8,16},{9,1... | collective-permute-start | bytes 3145736 | tf_op jit(solution)/shard_map/gather_d2/ppermute | solution.py:50
  56.0 2.0 %collective-permute-start.6 = (bf16[256,2048]{1,0:T(8,128)(2,1)S(1)}, bf16[256,2048]{1,0:T(8,128)(2,1)S(1)}, u32[]{:S(2)}, u32[]{:S(2)}) collective-permute-start(bf16[256,2048]{1,0:T(8,128)(2,1)S(1)} %collective-permute-done.5.refs_5_), channel_id=1, source_target_pairs={{0,96},{1,33},{2,98},{3,35},{4,100},{5,37},{6,102},{7,39},{8,104},... | collective-permute-start | bytes 3145736 | tf_op jit(solution)/shard_map/gather_d1/ppermute | solution.py:50
  58.0 6.0 %collective-permute-done.12.refs_3_ = bf16[256,2048]{1,0:T(8,128)(2,1)S(1)} collective-permute-done((bf16[256,2048]{1,0:T(8,128)(2,1)S(1)}, bf16[256,2048]{1,0:T(8,128)(2,1)S(1)}, u32[]{:S(2)}, u32[]{:S(2)}) %collective-permute-start.12) | collective-permute-done | bytes 1048608 | tf_op jit(solution)/shard_map/gather_c2/ppermute | solution.py:50
  66.0 4.7 %forward0.1 = (f32[256,2048]{1,0:T(8,128)S(1)}, f32[256,2048]{1,0:T(8,128)S(1)}) custom-call(bf16[3,512,1024]{2,1,0:T(8,128)(2,1)S(1)} %arrange.3.refs_0_, bf16[256,2048]{1,0:T(8,128)(2,1)S(1)} %pad_maximum_fusion.2.refs_1_, bf16[256,2048]{1,0:T(8,128)(2,1)S(1)} %pad_maximum_fusion.3.refs_2_, bf16[256,2048]{1,0:T(8,128)(2,1)S(1)} %pad_maximum_fusion.4.refs_3_, ...), custom_call_target="tpu_custom_call" | custom-call | flops 3221225472 | bytes 10485760 | tf_op jit(solution)/shard_map/forward0/pallas_call | solution.py:147
  70.7 3.1 %forward1.1 = (f32[256,2048]{1,0:T(8,128)S(1)}, bf16[256,2048]{1,0:T(8,128)(2,1)S(1)}) custom-call(bf16[3,512,1024]{2,1,0:T(8,128)(2,1)S(1)} %arrange.3.refs_0_, bf16[256,2048]{1,0:T(8,128)(2,1)S(1)} %collective-permute-done.10.refs_1_, bf16[256,2048]{1,0:T(8,128)(2,1)S(1)} %collective-permute-done.11.refs_2_, ...), custom_call_target="tpu_custom_call" | custom-call | flops 1610612736 | bytes 11534336 | tf_op jit(solution)/shard_map/forward1/pallas_call | solution.py:147
  75.3 3.2 %collective-permute-done.6.refs_2_ = bf16[256,2048]{1,0:T(8,128)(2,1)S(1)} collective-permute-done((bf16[256,2048]{1,0:T(8,128)(2,1)S(1)}, bf16[256,2048]{1,0:T(8,128)(2,1)S(1)}, u32[]{:S(2)}, u32[]{:S(2)}) %collective-permute-start.6) | collective-permute-done | bytes 1048608 | tf_op jit(solution)/shard_map/gather_d1/ppermute | solution.py:50
  86.2 2.3 %collective-permute-done.15 = bf16[256,2048]{1,0:T(8,128)(2,1)S(1)} collective-permute-done((bf16[256,2048]{1,0:T(8,128)(2,1)S(1)}, bf16[256,2048]{1,0:T(8,128)(2,1)S(1)}, u32[]{:S(2)}, u32[]{:S(2)}) %collective-permute-start.15) | collective-permute-done | bytes 1048608 | tf_op jit(solution)/shard_map/grad/ppermute | solution.py:54
  89.2 2.0 %collective-permute-start.17 = (bf16[256,2048]{1,0:T(8,128)(2,1)S(1)}, bf16[256,2048]{1,0:T(8,128)(2,1)S(1)}, u32[]{:S(2)}, u32[]{:S(2)}) collective-permute-start(bf16[256,2048]{1,0:T(8,128)(2,1)S(1)} %convolution_convert_fusion.4), channel_id=1, source_target_pairs={{0,6},{1,3},{2,4},{3,1},{4,2},{5,7},{6,0},{7,5},{8,14},{9,11},{10,... | collective-permute-start | bytes 3145736 | tf_op jit(solution)/shard_map/reduce_d0/ppermute | solution.py:50
  94.2 2.1 %collective-permute-start.16 = (bf16[256,2048]{1,0:T(8,128)(2,1)S(1)}, bf16[256,2048]{1,0:T(8,128)(2,1)S(1)}, u32[]{:S(2)}, u32[]{:S(2)}) collective-permute-start(bf16[256,2048]{1,0:T(8,128)(2,1)S(1)} %convolution_convert_fusion.5), channel_id=1, source_target_pairs={{0,6},{1,3},{2,4},{3,1},{4,2},{5,7},{6,0},{7,5},{8,14},{9,11},{10,... | collective-permute-start | bytes 3145736 | tf_op jit(solution)/shard_map/reduce_c0/ppermute | solution.py:50
  97.0 3.1 %collective-permute-start.25 = (bf16[256,2048]{1,0:T(8,128)(2,1)S(1)}, bf16[256,2048]{1,0:T(8,128)(2,1)S(1)}, u32[]{:S(2)}, u32[]{:S(2)}) collective-permute-start(bf16[256,2048]{1,0:T(8,128)(2,1)S(1)} %convolution_convert_fusion), channel_id=1, source_target_pairs={{0,24},{1,9},{2,26},{3,11},{4,28},{5,13},{6,30},{7,15},{8,16},{9,1... | collective-permute-start | bytes 3145736 | tf_op jit(solution)/shard_map/reduce_d2/ppermute | solution.py:50
  102.1 3.1 %collective-permute-done.17 = bf16[256,2048]{1,0:T(8,128)(2,1)S(1)} collective-permute-done((bf16[256,2048]{1,0:T(8,128)(2,1)S(1)}, bf16[256,2048]{1,0:T(8,128)(2,1)S(1)}, u32[]{:S(2)}, u32[]{:S(2)}) %collective-permute-start.17) | collective-permute-done | bytes 1048608 | tf_op jit(solution)/shard_map/reduce_d0/ppermute | solution.py:50
  106.0 2.1 %collective-permute-start.18 = (bf16[256,2048]{1,0:T(8,128)(2,1)S(1)}, bf16[256,2048]{1,0:T(8,128)(2,1)S(1)}, u32[]{:S(2)}, u32[]{:S(2)}) collective-permute-start(bf16[256,2048]{1,0:T(8,128)(2,1)S(1)} %fusion.3), channel_id=1, source_target_pairs={{0,96},{1,33},{2,98},{3,35},{4,100},{5,37},{6,102},{7,39},{8,104},... | collective-permute-start | bytes 3145736 | tf_op jit(solution)/shard_map/reduce_b0/ppermute | solution.py:50
  108.8 3.1 %collective-permute-start.22 = (bf16[256,2048]{1,0:T(8,128)(2,1)S(1)}, bf16[256,2048]{1,0:T(8,128)(2,1)S(1)}, u32[]{:S(2)}, u32[]{:S(2)}) collective-permute-start(bf16[256,2048]{1,0:T(8,128)(2,1)S(1)} %fusion.4), channel_id=1, source_target_pairs={{0,24},{1,9},{2,26},{3,11},{4,28},{5,13},{6,30},{7,15},{8,16},{9,1... | collective-permute-start | bytes 3145736 | tf_op jit(solution)/shard_map/reduce_b1/ppermute | solution.py:50
  113.1 3.0 %collective-permute-start.24 = (bf16[256,2048]{1,0:T(8,128)(2,1)S(1)}, bf16[256,2048]{1,0:T(8,128)(2,1)S(1)}, u32[]{:S(2)}, u32[]{:S(2)}) collective-permute-start(bf16[256,2048]{1,0:T(8,128)(2,1)S(1)} %convolution_convert_fusion.1), channel_id=1, source_target_pairs={{0,24},{1,9},{2,26},{3,11},{4,28},{5,13},{6,30},{7,15},{8,16},{9,1... | collective-permute-start | bytes 3145736 | tf_op jit(solution)/shard_map/reduce_c2/ppermute | solution.py:50
  118.5 12.0 %collective-permute-done.18 = bf16[256,2048]{1,0:T(8,128)(2,1)S(1)} collective-permute-done((bf16[256,2048]{1,0:T(8,128)(2,1)S(1)}, bf16[256,2048]{1,0:T(8,128)(2,1)S(1)}, u32[]{:S(2)}, u32[]{:S(2)}) %collective-permute-start.18) | collective-permute-done | bytes 1048608 | tf_op jit(solution)/shard_map/reduce_b0/ppermute | solution.py:50
  131.3 2.9 %collective-permute-start.19 = (bf16[128,2048]{1,0:T(8,128)(2,1)S(1)}, bf16[128,2048]{1,0:T(8,128)(2,1)S(1)}, u32[]{:S(2)}, u32[]{:S(2)}) collective-permute-start(bf16[128,2048]{1,0:T(8,128)(2,1)S(1)} %slice.155), channel_id=1, source_target_pairs={{0,24},{1,9},{2,26},{3,11},{4,28},{5,13},{6,30},{7,15},{8,16},{9,1... | collective-permute-start | bytes 1572872 | tf_op jit(solution)/shard_map/reduce_a0/ppermute | solution.py:50
  137.5 2.1 %collective-permute-start.27 = (bf16[128,2048]{1,0:T(8,128)(2,1)S(1)}, bf16[128,2048]{1,0:T(8,128)(2,1)S(1)}, u32[]{:S(2)}, u32[]{:S(2)}) collective-permute-start(bf16[128,2048]{1,0:T(8,128)(2,1)S(1)} %slice.153), channel_id=1, source_target_pairs={{0,96},{1,33},{2,98},{3,35},{4,100},{5,37},{6,102},{7,39},{8,104},... | collective-permute-start | bytes 1572872 | tf_op jit(solution)/shard_map/reduce_a2/ppermute | solution.py:50
  139.5 2.3 %collective-permute-done.19 = bf16[128,2048]{1,0:T(8,128)(2,1)S(1)} collective-permute-done((bf16[128,2048]{1,0:T(8,128)(2,1)S(1)}, bf16[128,2048]{1,0:T(8,128)(2,1)S(1)}, u32[]{:S(2)}, u32[]{:S(2)}) %collective-permute-start.19) | collective-permute-done | bytes 524320 | tf_op jit(solution)/shard_map/reduce_a0/ppermute | solution.py:50
  141.9 3.6 %collective-permute-done.23 = bf16[128,2048]{1,0:T(8,128)(2,1)S(1)} collective-permute-done((bf16[128,2048]{1,0:T(8,128)(2,1)S(1)}, bf16[128,2048]{1,0:T(8,128)(2,1)S(1)}, u32[]{:S(2)}, u32[]{:S(2)}) %collective-permute-start.23) | collective-permute-done | bytes 524320 | tf_op jit(solution)/shard_map/reduce_a1/ppermute | solution.py:50
  145.7 2.2 %collective-permute-done.27 = bf16[128,2048]{1,0:T(8,128)(2,1)S(1)} collective-permute-done((bf16[128,2048]{1,0:T(8,128)(2,1)S(1)}, bf16[128,2048]{1,0:T(8,128)(2,1)S(1)}, u32[]{:S(2)}, u32[]{:S(2)}) %collective-permute-start.27) | collective-permute-done | bytes 524320 | tf_op jit(solution)/shard_map/reduce_a2/ppermute | solution.py:50
  148.2 16.4 %all_to_all.21 = bf16[8,48,2048]{2,1,0:T(8,128)(2,1)S(1)} all-to-all(bf16[8,48,2048]{2,1,0:T(8,128)(2,1)S(1)} %bitcast.56), channel_id=1, replica_groups={{0,2,8,10,32,34,40,42},{1,7,25,31,97,103,121,127},{3,5,27,29,99,101,123..., dimensions={0} | all-to-all | bytes 3145728 | tf_op jit(solution)/shard_map/all_to_all | solution.py:58
  (72 shorter events, 37.5 us)
Async XLA Ops:
  0.0 7.7 %copy-start.2 = (bf16[256,6144]{1,0:T(8,128)(2,1)S(1)}, bf16[256,6144]{1,0:T(8,128)(2,1)}, u32[]{:S(2)}) copy-start(bf16[256,6144]{1,0:T(8,128)(2,1)} %own_ref) | copy-start | bytes 9437188
  0.0 7.7 %collective-permute-start = (bf16[256,6144]{1,0:T(8,128)(2,1)}, bf16[256,6144]{1,0:T(8,128)(2,1)}, u32[]{:S(2)}, u32[]{:S(2)}) collective-permute-start(bf16[256,6144]{1,0:T(8,128)(2,1)} %own_ref), channel_id=1, source_target_pairs={{0,1},{1,0},{2,3},{3,2},{4,5},{5,4},{6,7},{7,6},{8,9},{9,8},{10,11... | collective-permute-start | bytes 9437192 | tf_op jit(solution)/shard_map/cube/ppermute | solution.py:54
  2.5 19.4 %all-to-all-start = ((bf16[8,48,2048]{2,1,0:T(8,128)(2,1)}), bf16[8,48,2048]{2,1,0:T(8,128)(2,1)}, u32[]{:S(2)}, u32[]{:S(2)}) async-start(bf16[8,48,2048]{2,1,0:T(8,128)(2,1)} %tile.4), calls=%async_computation | async-start | bytes 3145728 | tf_op jit(solution)/shard_map/cube/all_to_all | solution.py:58
  23.4 11.7 %collective-permute-start.7 = (bf16[128,2048]{1,0:T(8,128)(2,1)S(1)}, bf16[128,2048]{1,0:T(8,128)(2,1)S(1)}, u32[]{:S(2)}, u32[]{:S(2)}) collective-permute-start(bf16[128,2048]{1,0:T(8,128)(2,1)S(1)} %get-tuple-element.23), channel_id=1, source_target_pairs={{0,96},{1,33},{2,98},{3,35},{4,100},{5,37},{6,102},{7,39},{8,104},... | collective-permute-start | bytes 1572872 | tf_op jit(solution)/shard_map/gather_a2/ppermute | solution.py:50
  26.2 10.4 %collective-permute-start.4 = (bf16[128,2048]{1,0:T(8,128)(2,1)S(1)}, bf16[128,2048]{1,0:T(8,128)(2,1)S(1)}, u32[]{:S(2)}, u32[]{:S(2)}) collective-permute-start(bf16[128,2048]{1,0:T(8,128)(2,1)S(1)} %get-tuple-element.24), channel_id=1, source_target_pairs={{0,6},{1,3},{2,4},{3,1},{4,2},{5,7},{6,0},{7,5},{8,14},{9,11},{10,... | collective-permute-start | bytes 1572872 | tf_op jit(solution)/shard_map/gather_a1/ppermute | solution.py:50
  28.0 11.8 %collective-permute-start.1 = (bf16[128,2048]{1,0:T(8,128)(2,1)S(1)}, bf16[128,2048]{1,0:T(8,128)(2,1)S(1)}, u32[]{:S(2)}, u32[]{:S(2)}) collective-permute-start(bf16[128,2048]{1,0:T(8,128)(2,1)S(1)} %get-tuple-element.25), channel_id=1, source_target_pairs={{0,24},{1,9},{2,26},{3,11},{4,28},{5,13},{6,30},{7,15},{8,16},{9,1... | collective-permute-start | bytes 1572872 | tf_op jit(solution)/shard_map/gather_a0/ppermute | solution.py:50
  35.2 16.1 %collective-permute-start.8 = (bf16[256,2048]{1,0:T(8,128)(2,1)S(1)}, bf16[256,2048]{1,0:T(8,128)(2,1)S(1)}, u32[]{:S(2)}, u32[]{:S(2)}) collective-permute-start(bf16[256,2048]{1,0:T(8,128)(2,1)S(1)} %pad_maximum_fusion.4.refs_3_), channel_id=1, source_target_pairs={{0,6},{1,3},{2,4},{3,1},{4,2},{5,7},{6,0},{7,5},{8,14},{9,11},{10,... | collective-permute-start | bytes 3145736 | tf_op jit(solution)/shard_map/gather_b2/ppermute | solution.py:50
  36.7 16.1 %collective-permute-start.5 = (bf16[256,2048]{1,0:T(8,128)(2,1)S(1)}, bf16[256,2048]{1,0:T(8,128)(2,1)S(1)}, u32[]{:S(2)}, u32[]{:S(2)}) collective-permute-start(bf16[256,2048]{1,0:T(8,128)(2,1)S(1)} %pad_maximum_fusion.3.refs_2_), channel_id=1, source_target_pairs={{0,24},{1,9},{2,26},{3,11},{4,28},{5,13},{6,30},{7,15},{8,16},{9,1... | collective-permute-start | bytes 3145736 | tf_op jit(solution)/shard_map/gather_b1/ppermute | solution.py:50
  39.9 16.1 %collective-permute-start.2 = (bf16[256,2048]{1,0:T(8,128)(2,1)S(1)}, bf16[256,2048]{1,0:T(8,128)(2,1)S(1)}, u32[]{:S(2)}, u32[]{:S(2)}) collective-permute-start(bf16[256,2048]{1,0:T(8,128)(2,1)S(1)} %pad_maximum_fusion.2.refs_1_), channel_id=1, source_target_pairs={{0,96},{1,33},{2,98},{3,35},{4,100},{5,37},{6,102},{7,39},{8,104},... | collective-permute-start | bytes 3145736 | tf_op jit(solution)/shard_map/gather_b0/ppermute | solution.py:50
  42.0 22.1 %collective-permute-start.12 = (bf16[256,2048]{1,0:T(8,128)(2,1)S(1)}, bf16[256,2048]{1,0:T(8,128)(2,1)S(1)}, u32[]{:S(2)}, u32[]{:S(2)}) collective-permute-start(bf16[256,2048]{1,0:T(8,128)(2,1)S(1)} %pad_maximum_fusion.4.refs_3_), channel_id=1, source_target_pairs={{0,24},{1,9},{2,26},{3,11},{4,28},{5,13},{6,30},{7,15},{8,16},{9,1... | collective-permute-start | bytes 3145736 | tf_op jit(solution)/shard_map/gather_c2/ppermute | solution.py:50
  42.2 28.5 %collective-permute-start.11 = (bf16[256,2048]{1,0:T(8,128)(2,1)S(1)}, bf16[256,2048]{1,0:T(8,128)(2,1)S(1)}, u32[]{:S(2)}, u32[]{:S(2)}) collective-permute-start(bf16[256,2048]{1,0:T(8,128)(2,1)S(1)} %pad_maximum_fusion.3.refs_2_), channel_id=1, source_target_pairs={{0,96},{1,33},{2,98},{3,35},{4,100},{5,37},{6,102},{7,39},{8,104},... | collective-permute-start | bytes 3145736 | tf_op jit(solution)/shard_map/gather_c1/ppermute | solution.py:50
  51.3 19.4 %collective-permute-start.10 = (bf16[256,2048]{1,0:T(8,128)(2,1)S(1)}, bf16[256,2048]{1,0:T(8,128)(2,1)S(1)}, u32[]{:S(2)}, u32[]{:S(2)}) collective-permute-start(bf16[256,2048]{1,0:T(8,128)(2,1)S(1)} %pad_maximum_fusion.2.refs_1_), channel_id=1, source_target_pairs={{0,6},{1,3},{2,4},{3,1},{4,2},{5,7},{6,0},{7,5},{8,14},{9,11},{10,... | collective-permute-start | bytes 3145736 | tf_op jit(solution)/shard_map/gather_c0/ppermute | solution.py:50
  52.8 22.5 %collective-permute-start.9 = (bf16[256,2048]{1,0:T(8,128)(2,1)S(1)}, bf16[256,2048]{1,0:T(8,128)(2,1)S(1)}, u32[]{:S(2)}, u32[]{:S(2)}) collective-permute-start(bf16[256,2048]{1,0:T(8,128)(2,1)S(1)} %collective-permute-done.8.refs_6_), channel_id=1, source_target_pairs={{0,24},{1,9},{2,26},{3,11},{4,28},{5,13},{6,30},{7,15},{8,16},{9,1... | collective-permute-start | bytes 3145736 | tf_op jit(solution)/shard_map/gather_d2/ppermute | solution.py:50
  56.0 22.5 %collective-permute-start.6 = (bf16[256,2048]{1,0:T(8,128)(2,1)S(1)}, bf16[256,2048]{1,0:T(8,128)(2,1)S(1)}, u32[]{:S(2)}, u32[]{:S(2)}) collective-permute-start(bf16[256,2048]{1,0:T(8,128)(2,1)S(1)} %collective-permute-done.5.refs_5_), channel_id=1, source_target_pairs={{0,96},{1,33},{2,98},{3,35},{4,100},{5,37},{6,102},{7,39},{8,104},... | collective-permute-start | bytes 3145736 | tf_op jit(solution)/shard_map/gather_d1/ppermute | solution.py:50
  64.0 16.0 %collective-permute-start.3 = (bf16[256,2048]{1,0:T(8,128)(2,1)S(1)}, bf16[256,2048]{1,0:T(8,128)(2,1)S(1)}, u32[]{:S(2)}, u32[]{:S(2)}) collective-permute-start(bf16[256,2048]{1,0:T(8,128)(2,1)S(1)} %collective-permute-done.2.refs_4_), channel_id=1, source_target_pairs={{0,6},{1,3},{2,4},{3,1},{4,2},{5,7},{6,0},{7,5},{8,14},{9,11},{10,... | collective-permute-start | bytes 3145736 | tf_op jit(solution)/shard_map/gather_d0/ppermute | solution.py:50
  73.8 8.5 %collective-permute-start.13 = (bf16[256,2048]{1,0:T(8,128)(2,1)S(1)}, bf16[256,2048]{1,0:T(8,128)(2,1)S(1)}, u32[]{:S(2)}, u32[]{:S(2)}) collective-permute-start(bf16[256,2048]{1,0:T(8,128)(2,1)S(1)} %get-tuple-element.22), channel_id=1, source_target_pairs={{0,1},{1,0},{2,3},{3,2},{4,5},{5,4},{6,7},{7,6},{8,9},{9,8},{10,11... | collective-permute-start | bytes 3145736 | tf_op jit(solution)/shard_map/forward1/ppermute | solution.py:54
  81.5 2.7 %collective-permute-start.14 = (bf16[256,2048]{1,0:T(8,128)(2,1)S(1)}, bf16[256,2048]{1,0:T(8,128)(2,1)S(1)}, u32[]{:S(2)}, u32[]{:S(2)}) collective-permute-start(bf16[256,2048]{1,0:T(8,128)(2,1)S(1)} %forward2.1), channel_id=1, source_target_pairs={{0,1},{1,0},{2,3},{3,2},{4,5},{5,4},{6,7},{7,6},{8,9},{9,8},{10,11... | collective-permute-start | bytes 3145736 | tf_op jit(solution)/shard_map/forward2/ppermute | solution.py:54
  82.3 2.0 %copy-start.3 = (bf16[256,2048]{1,0:T(8,128)(2,1)S(1)}, bf16[256,2048]{1,0:T(8,128)(2,1)}, u32[]{:S(2)}) copy-start(bf16[256,2048]{1,0:T(8,128)(2,1)} %target_ref.1) | copy-start | bytes 3145732
  84.3 4.2 %copy-start.1 = (bf16[3,8,8,16,512]{4,3,2,1,0:T(8,128)(2,1)S(1)}, bf16[3,8,8,16,512]{4,3,2,1,0:T(8,128)(2,1)}, u32[]{:S(2)}) copy-start(bf16[3,8,8,16,512]{4,3,2,1,0:T(8,128)(2,1)} %copy-done) | copy-start | bytes 9437188
  85.7 2.8 %collective-permute-start.15 = (bf16[256,2048]{1,0:T(8,128)(2,1)S(1)}, bf16[256,2048]{1,0:T(8,128)(2,1)S(1)}, u32[]{:S(2)}, u32[]{:S(2)}) collective-permute-start(bf16[256,2048]{1,0:T(8,128)(2,1)S(1)} %grad.1), channel_id=1, source_target_pairs={{0,1},{1,0},{2,3},{3,2},{4,5},{5,4},{6,7},{7,6},{8,9},{9,8},{10,11... | collective-permute-start | bytes 3145736 | tf_op jit(solution)/shard_map/grad/ppermute | solution.py:54
  89.2 16.1 %collective-permute-start.17 = (bf16[256,2048]{1,0:T(8,128)(2,1)S(1)}, bf16[256,2048]{1,0:T(8,128)(2,1)S(1)}, u32[]{:S(2)}, u32[]{:S(2)}) collective-permute-start(bf16[256,2048]{1,0:T(8,128)(2,1)S(1)} %convolution_convert_fusion.4), channel_id=1, source_target_pairs={{0,6},{1,3},{2,4},{3,1},{4,2},{5,7},{6,0},{7,5},{8,14},{9,11},{10,... | collective-permute-start | bytes 3145736 | tf_op jit(solution)/shard_map/reduce_d0/ppermute | solution.py:50
  92.0 16.1 %collective-permute-start.21 = (bf16[256,2048]{1,0:T(8,128)(2,1)S(1)}, bf16[256,2048]{1,0:T(8,128)(2,1)S(1)}, u32[]{:S(2)}, u32[]{:S(2)}) collective-permute-start(bf16[256,2048]{1,0:T(8,128)(2,1)S(1)} %convolution_convert_fusion.2), channel_id=1, source_target_pairs={{0,96},{1,33},{2,98},{3,35},{4,100},{5,37},{6,102},{7,39},{8,104},... | collective-permute-start | bytes 3145736 | tf_op jit(solution)/shard_map/reduce_d1/ppermute | solution.py:50
  94.2 22.6 %collective-permute-start.16 = (bf16[256,2048]{1,0:T(8,128)(2,1)S(1)}, bf16[256,2048]{1,0:T(8,128)(2,1)S(1)}, u32[]{:S(2)}, u32[]{:S(2)}) collective-permute-start(bf16[256,2048]{1,0:T(8,128)(2,1)S(1)} %convolution_convert_fusion.5), channel_id=1, source_target_pairs={{0,6},{1,3},{2,4},{3,1},{4,2},{5,7},{6,0},{7,5},{8,14},{9,11},{10,... | collective-permute-start | bytes 3145736 | tf_op jit(solution)/shard_map/reduce_c0/ppermute | solution.py:50
  97.0 16.1 %collective-permute-start.25 = (bf16[256,2048]{1,0:T(8,128)(2,1)S(1)}, bf16[256,2048]{1,0:T(8,128)(2,1)S(1)}, u32[]{:S(2)}, u32[]{:S(2)}) collective-permute-start(bf16[256,2048]{1,0:T(8,128)(2,1)S(1)} %convolution_convert_fusion), channel_id=1, source_target_pairs={{0,24},{1,9},{2,26},{3,11},{4,28},{5,13},{6,30},{7,15},{8,16},{9,1... | collective-permute-start | bytes 3145736 | tf_op jit(solution)/shard_map/reduce_d2/ppermute | solution.py:50
  100.8 33.5 %collective-permute-start.20 = (bf16[256,2048]{1,0:T(8,128)(2,1)S(1)}, bf16[256,2048]{1,0:T(8,128)(2,1)S(1)}, u32[]{:S(2)}, u32[]{:S(2)}) collective-permute-start(bf16[256,2048]{1,0:T(8,128)(2,1)S(1)} %convolution_convert_fusion.3), channel_id=1, source_target_pairs={{0,96},{1,33},{2,98},{3,35},{4,100},{5,37},{6,102},{7,39},{8,104},... | collective-permute-start | bytes 3145736 | tf_op jit(solution)/shard_map/reduce_c1/ppermute | solution.py:50
  106.0 24.5 %collective-permute-start.18 = (bf16[256,2048]{1,0:T(8,128)(2,1)S(1)}, bf16[256,2048]{1,0:T(8,128)(2,1)S(1)}, u32[]{:S(2)}, u32[]{:S(2)}) collective-permute-start(bf16[256,2048]{1,0:T(8,128)(2,1)S(1)} %fusion.3), channel_id=1, source_target_pairs={{0,96},{1,33},{2,98},{3,35},{4,100},{5,37},{6,102},{7,39},{8,104},... | collective-permute-start | bytes 3145736 | tf_op jit(solution)/shard_map/reduce_b0/ppermute | solution.py:50
  108.8 25.5 %collective-permute-start.22 = (bf16[256,2048]{1,0:T(8,128)(2,1)S(1)}, bf16[256,2048]{1,0:T(8,128)(2,1)S(1)}, u32[]{:S(2)}, u32[]{:S(2)}) collective-permute-start(bf16[256,2048]{1,0:T(8,128)(2,1)S(1)} %fusion.4), channel_id=1, source_target_pairs={{0,24},{1,9},{2,26},{3,11},{4,28},{5,13},{6,30},{7,15},{8,16},{9,1... | collective-permute-start | bytes 3145736 | tf_op jit(solution)/shard_map/reduce_b1/ppermute | solution.py:50
  113.1 23.5 %collective-permute-start.24 = (bf16[256,2048]{1,0:T(8,128)(2,1)S(1)}, bf16[256,2048]{1,0:T(8,128)(2,1)S(1)}, u32[]{:S(2)}, u32[]{:S(2)}) collective-permute-start(bf16[256,2048]{1,0:T(8,128)(2,1)S(1)} %convolution_convert_fusion.1), channel_id=1, source_target_pairs={{0,24},{1,9},{2,26},{3,11},{4,28},{5,13},{6,30},{7,15},{8,16},{9,1... | collective-permute-start | bytes 3145736 | tf_op jit(solution)/shard_map/reduce_c2/ppermute | solution.py:50
  116.8 19.8 %collective-permute-start.26 = (bf16[256,2048]{1,0:T(8,128)(2,1)S(1)}, bf16[256,2048]{1,0:T(8,128)(2,1)S(1)}, u32[]{:S(2)}, u32[]{:S(2)}) collective-permute-start(bf16[256,2048]{1,0:T(8,128)(2,1)S(1)} %fusion.5), channel_id=1, source_target_pairs={{0,6},{1,3},{2,4},{3,1},{4,2},{5,7},{6,0},{7,5},{8,14},{9,11},{10,... | collective-permute-start | bytes 3145736 | tf_op jit(solution)/shard_map/reduce_b2/ppermute | solution.py:50
  131.3 10.5 %collective-permute-start.19 = (bf16[128,2048]{1,0:T(8,128)(2,1)S(1)}, bf16[128,2048]{1,0:T(8,128)(2,1)S(1)}, u32[]{:S(2)}, u32[]{:S(2)}) collective-permute-start(bf16[128,2048]{1,0:T(8,128)(2,1)S(1)} %slice.155), channel_id=1, source_target_pairs={{0,24},{1,9},{2,26},{3,11},{4,28},{5,13},{6,30},{7,15},{8,16},{9,1... | collective-permute-start | bytes 1572872 | tf_op jit(solution)/shard_map/reduce_a0/ppermute | solution.py:50
  135.1 10.5 %collective-permute-start.23 = (bf16[128,2048]{1,0:T(8,128)(2,1)S(1)}, bf16[128,2048]{1,0:T(8,128)(2,1)S(1)}, u32[]{:S(2)}, u32[]{:S(2)}) collective-permute-start(bf16[128,2048]{1,0:T(8,128)(2,1)S(1)} %slice.154), channel_id=1, source_target_pairs={{0,6},{1,3},{2,4},{3,1},{4,2},{5,7},{6,0},{7,5},{8,14},{9,11},{10,... | collective-permute-start | bytes 1572872 | tf_op jit(solution)/shard_map/reduce_a1/ppermute | solution.py:50
  137.5 10.5 %collective-permute-start.27 = (bf16[128,2048]{1,0:T(8,128)(2,1)S(1)}, bf16[128,2048]{1,0:T(8,128)(2,1)S(1)}, u32[]{:S(2)}, u32[]{:S(2)}) collective-permute-start(bf16[128,2048]{1,0:T(8,128)(2,1)S(1)} %slice.153), channel_id=1, source_target_pairs={{0,96},{1,33},{2,98},{3,35},{4,100},{5,37},{6,102},{7,39},{8,104},... | collective-permute-start | bytes 1572872 | tf_op jit(solution)/shard_map/reduce_a2/ppermute | solution.py:50
  (2 other events, 3.6 us)

commit v4 on v3

--- a/solution.py
+++ b/solution.py
@@ -9,7 +9,7 @@
 AXES = ("replica", "shard")
 STRIDE = {"z": 16, "y": 4, "x": 1}
 ROUNDS = (("y", "z", "x"), ("x", "y", "z"), ("z", "x", "y"))
-LONG = ('zyx', '')
+LONG = ('zy', 'x')
 F32, BF16 = jnp.float32, jnp.bfloat16
 
 

time: 166 us -> 166 us (level)
  starting transfers between devices: 56.3 us -> 43.3 us
  waiting for transfers between devices: 56.9 us -> 68.2 us
    ppermute x24, starting transfers between devices: 50.2 us -> 36.1 us  [swap(): return lax.ppermute(value, AXES, swap_pairs(axis))]
    ppermute x24, waiting for transfers between devices: 48.2 us -> 58.3 us  [swap(): return lax.ppermute(value, AXES, swap_pairs(axis))]
  transfers between devices with their start and end apart: 29 -> 29, of which waited for: 18 -> 21; matrix products, arithmetic and copies ran while one was open for 7% -> 7% of each run, Pallas kernels for 10% -> 10%
where the time goes in v4:
time: 166 us; the launch traced here: 165 us
  waiting for transfers between devices  68.2 us (41%)
  starting transfers between devices  43.3 us (26%)
  Pallas kernels  18.7 us (11%)
  blocking collectives  17.6 us (11%)
  matrix products  8.65 us (5%)
  local copies, waits for them, and re-layouts  5.82 us (4%)
  other arithmetic  1.96 us (1%)
    ppermute x24, waiting for transfers between devices, swap(): return lax.ppermute(value, AXES, swap_pairs(axis))  58.3 us
    ppermute x24, starting transfers between devices, swap(): return lax.ppermute(value, AXES, swap_pairs(axis))  36.1 us
    all_to_all x1, blocking collectives, cube_exchange(): lax.all_to_all(value, AXES, 0, 0, axis_index_groups=cubes(), tiled=True)  17.6 us
    pallas_call x4, Pallas kernels, forward(): pl.pallas_call(kernel, grid=(width // cols,), in_specs=[pl.BlockSpec((3,...  11.1 us
    dot_general x12, matrix products, product(): jnp.dot(features[s, q * 256:(q + 1) * 256], grads, preferred_element_type...  8.65 us
    all_to_all x1, waiting for transfers between devices, cube_exchange(): lax.all_to_all(value, AXES, 0, 0, axis_index_groups=cubes(), tiled=True)  7.42 us
    all_to_all x1, starting transfers between devices, cube_exchange(): lax.all_to_all(value, AXES, 0, 0, axis_index_groups=cubes(), tiled=True)  6.48 us
    pallas_call x1, Pallas kernels, arrange(): pl.pallas_call(arrange_kernel, grid=(4,), in_specs=[pl.BlockSpec((m, 1536...  4.78 us
  transfers between devices with their start and end apart: 29, of which 21 were waited for; matrix products, arithmetic and copies ran while one was open for 7% of the time, Pallas kernels for 10%

profile of v4, /device:TPU:0, one launch (start us, length us, event | category | flops | bytes accessed | tf_op | source)
XLA Modules:
  0.0 165.2 jit_solution(12422385492135483436)
XLA Ops:
  0.0 2.5 %tile.4 = bf16[8,48,2048]{2,1,0:T(8,128)(2,1)} broadcast(bf16[48,2048]{1,0:T(8,128)(2,1)} %param.8), dimensions={1,2} | broadcast | bytes 1769472 | tf_op jit(solution)/shard_map/cube/tile | solution.py:204
  2.5 6.5 %all-to-all-start = ((bf16[8,48,2048]{2,1,0:T(8,128)(2,1)}), bf16[8,48,2048]{2,1,0:T(8,128)(2,1)}, u32[]{:S(2)}, u32[]{:S(2)}) async-start(bf16[8,48,2048]{2,1,0:T(8,128)(2,1)} %tile.4), calls=%async_computation | async-start | bytes 3145728 | tf_op jit(solution)/shard_map/cube/all_to_all | solution.py:58
  9.0 4.8 %arrange.2 = bf16[3,8,8,16,512]{4,3,2,1,0:T(8,128)(2,1)S(1)} custom-call(bf16[256,6144]{1,0:T(8,128)(2,1)S(1)} %copy-done.2, bf16[256,6144]{1,0:T(8,128)(2,1)} %collective-permute-done.other_ref), custom_call_target="tpu_custom_call" | custom-call | bytes 1024 | tf_op jit(solution)/shard_map/arrange/pallas_call | solution.py:100
  16.8 7.4 %all-to-all-done = bf16[8,48,2048]{2,1,0:T(8,128)(2,1)} async-done(((bf16[8,48,2048]{2,1,0:T(8,128)(2,1)}), bf16[8,48,2048]{2,1,0:T(8,128)(2,1)}, u32[]{:S(2)}, u32[]{:S(2)}) %all-to-all-start) | async-done | bytes 1572896 | tf_op jit(solution)/shard_map/cube/all_to_all | solution.py:58
  25.8 2.8 %collective-permute-start.7 = (bf16[128,2048]{1,0:T(8,128)(2,1)S(1)}, bf16[128,2048]{1,0:T(8,128)(2,1)S(1)}, u32[]{:S(2)}, u32[]{:S(2)}) collective-permute-start(bf16[128,2048]{1,0:T(8,128)(2,1)S(1)} %get-tuple-element.23), channel_id=1, source_target_pairs={{0,96},{1,33},{2,98},{3,35},{4,100},{5,37},{6,102},{7,39},{8,104},... | collective-permute-start | bytes 1572872 | tf_op jit(solution)/shard_map/gather_a2/ppermute | solution.py:50
  28.6 2.1 %collective-permute-start.1 = (bf16[128,2048]{1,0:T(8,128)(2,1)S(1)}, bf16[128,2048]{1,0:T(8,128)(2,1)S(1)}, u32[]{:S(2)}, u32[]{:S(2)}) collective-permute-start(bf16[128,2048]{1,0:T(8,128)(2,1)S(1)} %get-tuple-element.25), channel_id=1, source_target_pairs={{0,24},{1,9},{2,26},{3,11},{4,28},{5,13},{6,30},{7,15},{8,16},{9,1... | collective-permute-start | bytes 1572872 | tf_op jit(solution)/shard_map/gather_a0/ppermute | solution.py:50
  30.7 5.6 %collective-permute-done.7 = bf16[128,2048]{1,0:T(8,128)(2,1)S(1)} collective-permute-done((bf16[128,2048]{1,0:T(8,128)(2,1)S(1)}, bf16[128,2048]{1,0:T(8,128)(2,1)S(1)}, u32[]{:S(2)}, u32[]{:S(2)}) %collective-permute-start.7) | collective-permute-done | bytes 524320 | tf_op jit(solution)/shard_map/gather_a2/ppermute | solution.py:50
  37.8 2.1 %collective-permute-start.5 = (bf16[256,2048]{1,0:T(8,128)(2,1)S(1)}, bf16[256,2048]{1,0:T(8,128)(2,1)S(1)}, u32[]{:S(2)}, u32[]{:S(2)}) collective-permute-start(bf16[256,2048]{1,0:T(8,128)(2,1)S(1)} %pad_maximum_fusion.3.refs_2_), channel_id=1, source_target_pairs={{0,24},{1,9},{2,26},{3,11},{4,28},{5,13},{6,30},{7,15},{8,16},{9,1... | collective-permute-start | bytes 3145736 | tf_op jit(solution)/shard_map/gather_b1/ppermute | solution.py:50
  40.0 1.6 collective-permute-start.2
  42.8 1.8 %collective-permute-start.11 = (bf16[256,2048]{1,0:T(8,128)(2,1)S(1)}, bf16[256,2048]{1,0:T(8,128)(2,1)S(1)}, u32[]{:S(2)}, u32[]{:S(2)}) collective-permute-start(bf16[256,2048]{1,0:T(8,128)(2,1)S(1)} %pad_maximum_fusion.3.refs_2_), channel_id=1, source_target_pairs={{0,96},{1,33},{2,98},{3,35},{4,100},{5,37},{6,102},{7,39},{8,104},... | collective-permute-start | bytes 3145736 | tf_op jit(solution)/shard_map/gather_c1/ppermute | solution.py:50
  44.6 6.7 %collective-permute-done.8.refs_6_ = bf16[256,2048]{1,0:T(8,128)(2,1)S(1)} collective-permute-done((bf16[256,2048]{1,0:T(8,128)(2,1)S(1)}, bf16[256,2048]{1,0:T(8,128)(2,1)S(1)}, u32[]{:S(2)}, u32[]{:S(2)}) %collective-permute-start.8) | collective-permute-done | bytes 1048608 | tf_op jit(solution)/shard_map/gather_b2/ppermute | solution.py:50
  51.3 2.7 %collective-permute-done.5.refs_5_ = bf16[256,2048]{1,0:T(8,128)(2,1)S(1)} collective-permute-done((bf16[256,2048]{1,0:T(8,128)(2,1)S(1)}, bf16[256,2048]{1,0:T(8,128)(2,1)S(1)}, u32[]{:S(2)}, u32[]{:S(2)}) %collective-permute-start.5) | collective-permute-done | bytes 1048608 | tf_op jit(solution)/shard_map/gather_b1/ppermute | solution.py:50
  53.9 2.0 %collective-permute-start.9 = (bf16[256,2048]{1,0:T(8,128)(2,1)S(1)}, bf16[256,2048]{1,0:T(8,128)(2,1)S(1)}, u32[]{:S(2)}, u32[]{:S(2)}) collective-permute-start(bf16[256,2048]{1,0:T(8,128)(2,1)S(1)} %collective-permute-done.8.refs_6_), channel_id=1, source_target_pairs={{0,24},{1,9},{2,26},{3,11},{4,28},{5,13},{6,30},{7,15},{8,16},{9,1... | collective-permute-start | bytes 3145736 | tf_op jit(solution)/shard_map/gather_d2/ppermute | solution.py:50
  57.7 7.5 %collective-permute-done.12.refs_3_ = bf16[256,2048]{1,0:T(8,128)(2,1)S(1)} collective-permute-done((bf16[256,2048]{1,0:T(8,128)(2,1)S(1)}, bf16[256,2048]{1,0:T(8,128)(2,1)S(1)}, u32[]{:S(2)}, u32[]{:S(2)}) %collective-permute-start.12) | collective-permute-done | bytes 1048608 | tf_op jit(solution)/shard_map/gather_c2/ppermute | solution.py:50
  65.9 4.7 %forward0.1 = (f32[256,2048]{1,0:T(8,128)S(1)}, f32[256,2048]{1,0:T(8,128)S(1)}) custom-call(bf16[3,512,1024]{2,1,0:T(8,128)(2,1)S(1)} %arrange.3.refs_0_, bf16[256,2048]{1,0:T(8,128)(2,1)S(1)} %pad_maximum_fusion.2.refs_1_, bf16[256,2048]{1,0:T(8,128)(2,1)S(1)} %pad_maximum_fusion.3.refs_2_, bf16[256,2048]{1,0:T(8,128)(2,1)S(1)} %pad_maximum_fusion.4.refs_3_, ...), custom_call_target="tpu_custom_call" | custom-call | flops 3221225472 | bytes 10485760 | tf_op jit(solution)/shard_map/forward0/pallas_call | solution.py:147
  70.6 3.1 %forward1.1 = (f32[256,2048]{1,0:T(8,128)S(1)}, bf16[256,2048]{1,0:T(8,128)(2,1)S(1)}) custom-call(bf16[3,512,1024]{2,1,0:T(8,128)(2,1)S(1)} %arrange.3.refs_0_, bf16[256,2048]{1,0:T(8,128)(2,1)S(1)} %collective-permute-done.10.refs_1_, bf16[256,2048]{1,0:T(8,128)(2,1)S(1)} %collective-permute-done.11.refs_2_, ...), custom_call_target="tpu_custom_call" | custom-call | flops 1610612736 | bytes 11534336 | tf_op jit(solution)/shard_map/forward1/pallas_call | solution.py:147
  73.8 2.6 %collective-permute-done.9.refs_3_ = bf16[256,2048]{1,0:T(8,128)(2,1)S(1)} collective-permute-done((bf16[256,2048]{1,0:T(8,128)(2,1)S(1)}, bf16[256,2048]{1,0:T(8,128)(2,1)S(1)}, u32[]{:S(2)}, u32[]{:S(2)}) %collective-permute-start.9) | collective-permute-done | bytes 1048608 | tf_op jit(solution)/shard_map/gather_d2/ppermute | solution.py:50
  76.4 2.2 %collective-permute-done.6.refs_2_ = bf16[256,2048]{1,0:T(8,128)(2,1)S(1)} collective-permute-done((bf16[256,2048]{1,0:T(8,128)(2,1)S(1)}, bf16[256,2048]{1,0:T(8,128)(2,1)S(1)}, u32[]{:S(2)}, u32[]{:S(2)}) %collective-permute-start.6) | collective-permute-done | bytes 1048608 | tf_op jit(solution)/shard_map/gather_d1/ppermute | solution.py:50
  82.3 1.8 %forward3.1.own_ref = f32[256,2048]{1,0:T(8,128)S(1)} custom-call(bf16[3,512,1024]{2,1,0:T(8,128)(2,1)S(1)} %arrange.3.refs_0_, bf16[256,2048]{1,0:T(8,128)(2,1)S(1)} %collective-permute-done.3.refs_1_, bf16[256,2048]{1,0:T(8,128)(2,1)S(1)} %collective-permute-done.6.refs_2_, bf16[256,2048]{1,0:T(8,128)(2,1)S(1)} %collective-permute-done.9.refs_3_, ...), custom_call_target="tpu_custom_call" | custom-call | flops 805306368 | bytes 11534336 | tf_op jit(solution)/shard_map/forward3/pallas_call | solution.py:147
  86.1 2.3 %collective-permute-done.15 = bf16[256,2048]{1,0:T(8,128)(2,1)S(1)} collective-permute-done((bf16[256,2048]{1,0:T(8,128)(2,1)S(1)}, bf16[256,2048]{1,0:T(8,128)(2,1)S(1)}, u32[]{:S(2)}, u32[]{:S(2)}) %collective-permute-start.15) | collective-permute-done | bytes 1048608 | tf_op jit(solution)/shard_map/grad/ppermute | solution.py:54
  90.7 2.8 %collective-permute-start.21 = (bf16[256,2048]{1,0:T(8,128)(2,1)S(1)}, bf16[256,2048]{1,0:T(8,128)(2,1)S(1)}, u32[]{:S(2)}, u32[]{:S(2)}) collective-permute-start(bf16[256,2048]{1,0:T(8,128)(2,1)S(1)} %convolution_convert_fusion.2), channel_id=1, source_target_pairs={{0,96},{1,33},{2,98},{3,35},{4,100},{5,37},{6,102},{7,39},{8,104},... | collective-permute-start | bytes 3145736 | tf_op jit(solution)/shard_map/reduce_d1/ppermute | solution.py:50
  95.2 2.2 %collective-permute-start.25 = (bf16[256,2048]{1,0:T(8,128)(2,1)S(1)}, bf16[256,2048]{1,0:T(8,128)(2,1)S(1)}, u32[]{:S(2)}, u32[]{:S(2)}) collective-permute-start(bf16[256,2048]{1,0:T(8,128)(2,1)S(1)} %convolution_convert_fusion), channel_id=1, source_target_pairs={{0,24},{1,9},{2,26},{3,11},{4,28},{5,13},{6,30},{7,15},{8,16},{9,1... | collective-permute-start | bytes 3145736 | tf_op jit(solution)/shard_map/reduce_d2/ppermute | solution.py:50
  98.1 1.8 %collective-permute-start.20 = (bf16[256,2048]{1,0:T(8,128)(2,1)S(1)}, bf16[256,2048]{1,0:T(8,128)(2,1)S(1)}, u32[]{:S(2)}, u32[]{:S(2)}) collective-permute-start(bf16[256,2048]{1,0:T(8,128)(2,1)S(1)} %convolution_convert_fusion.3), channel_id=1, source_target_pairs={{0,96},{1,33},{2,98},{3,35},{4,100},{5,37},{6,102},{7,39},{8,104},... | collective-permute-start | bytes 3145736 | tf_op jit(solution)/shard_map/reduce_c1/ppermute | solution.py:50
  99.9 4.2 %collective-permute-done.17 = bf16[256,2048]{1,0:T(8,128)(2,1)S(1)} collective-permute-done((bf16[256,2048]{1,0:T(8,128)(2,1)S(1)}, bf16[256,2048]{1,0:T(8,128)(2,1)S(1)}, u32[]{:S(2)}, u32[]{:S(2)}) %collective-permute-start.17) | collective-permute-done | bytes 1048608 | tf_op jit(solution)/shard_map/reduce_d0/ppermute | solution.py:50
  107.5 1.7 %collective-permute-start.22 = (bf16[256,2048]{1,0:T(8,128)(2,1)S(1)}, bf16[256,2048]{1,0:T(8,128)(2,1)S(1)}, u32[]{:S(2)}, u32[]{:S(2)}) collective-permute-start(bf16[256,2048]{1,0:T(8,128)(2,1)S(1)} %fusion.4), channel_id=1, source_target_pairs={{0,24},{1,9},{2,26},{3,11},{4,28},{5,13},{6,30},{7,15},{8,16},{9,1... | collective-permute-start | bytes 3145736 | tf_op jit(solution)/shard_map/reduce_b1/ppermute | solution.py:50
  111.2 2.1 %collective-permute-start.24 = (bf16[256,2048]{1,0:T(8,128)(2,1)S(1)}, bf16[256,2048]{1,0:T(8,128)(2,1)S(1)}, u32[]{:S(2)}, u32[]{:S(2)}) collective-permute-start(bf16[256,2048]{1,0:T(8,128)(2,1)S(1)} %convolution_convert_fusion.1), channel_id=1, source_target_pairs={{0,24},{1,9},{2,26},{3,11},{4,28},{5,13},{6,30},{7,15},{8,16},{9,1... | collective-permute-start | bytes 3145736 | tf_op jit(solution)/shard_map/reduce_c2/ppermute | solution.py:50
  116.1 13.2 %collective-permute-done.18 = bf16[256,2048]{1,0:T(8,128)(2,1)S(1)} collective-permute-done((bf16[256,2048]{1,0:T(8,128)(2,1)S(1)}, bf16[256,2048]{1,0:T(8,128)(2,1)S(1)}, u32[]{:S(2)}, u32[]{:S(2)}) %collective-permute-start.18) | collective-permute-done | bytes 1048608 | tf_op jit(solution)/shard_map/reduce_b0/ppermute | solution.py:50
  132.4 1.9 %collective-permute-start.23 = (bf16[128,2048]{1,0:T(8,128)(2,1)S(1)}, bf16[128,2048]{1,0:T(8,128)(2,1)S(1)}, u32[]{:S(2)}, u32[]{:S(2)}) collective-permute-start(bf16[128,2048]{1,0:T(8,128)(2,1)S(1)} %slice.154), channel_id=1, source_target_pairs={{0,2},{1,7},{2,0},{3,5},{4,6},{5,3},{6,4},{7,1},{8,10},{9,15},{10,... | collective-permute-start | bytes 1572872 | tf_op jit(solution)/shard_map/reduce_a1/ppermute | solution.py:50
  135.6 2.8 %collective-permute-start.27 = (bf16[128,2048]{1,0:T(8,128)(2,1)S(1)}, bf16[128,2048]{1,0:T(8,128)(2,1)S(1)}, u32[]{:S(2)}, u32[]{:S(2)}) collective-permute-start(bf16[128,2048]{1,0:T(8,128)(2,1)S(1)} %slice.153), channel_id=1, source_target_pairs={{0,96},{1,33},{2,98},{3,35},{4,100},{5,37},{6,102},{7,39},{8,104},... | collective-permute-start | bytes 1572872 | tf_op jit(solution)/shard_map/reduce_a2/ppermute | solution.py:50
  138.4 2.1 %collective-permute-done.19 = bf16[128,2048]{1,0:T(8,128)(2,1)S(1)} collective-permute-done((bf16[128,2048]{1,0:T(8,128)(2,1)S(1)}, bf16[128,2048]{1,0:T(8,128)(2,1)S(1)}, u32[]{:S(2)}, u32[]{:S(2)}) %collective-permute-start.19) | collective-permute-done | bytes 524320 | tf_op jit(solution)/shard_map/reduce_a0/ppermute | solution.py:50
  141.8 4.3 %collective-permute-done.27 = bf16[128,2048]{1,0:T(8,128)(2,1)S(1)} collective-permute-done((bf16[128,2048]{1,0:T(8,128)(2,1)S(1)}, bf16[128,2048]{1,0:T(8,128)(2,1)S(1)}, u32[]{:S(2)}, u32[]{:S(2)}) %collective-permute-start.27) | collective-permute-done | bytes 524320 | tf_op jit(solution)/shard_map/reduce_a2/ppermute | solution.py:50
  146.4 17.6 %all_to_all.21 = bf16[8,48,2048]{2,1,0:T(8,128)(2,1)S(1)} all-to-all(bf16[8,48,2048]{2,1,0:T(8,128)(2,1)S(1)} %bitcast.56), channel_id=1, replica_groups={{0,6,8,14,32,38,40,46},{1,3,25,27,97,99,121,123},{2,4,10,12,34,36,42,44..., dimensions={0} | all-to-all | bytes 3145728 | tf_op jit(solution)/shard_map/all_to_all | solution.py:58
  (72 shorter events, 35.0 us)
Async XLA Ops:
  0.0 9.0 %copy-start.2 = (bf16[256,6144]{1,0:T(8,128)(2,1)S(1)}, bf16[256,6144]{1,0:T(8,128)(2,1)}, u32[]{:S(2)}) copy-start(bf16[256,6144]{1,0:T(8,128)(2,1)} %own_ref) | copy-start | bytes 9437188
  0.0 9.0 %collective-permute-start = (bf16[256,6144]{1,0:T(8,128)(2,1)}, bf16[256,6144]{1,0:T(8,128)(2,1)}, u32[]{:S(2)}, u32[]{:S(2)}) collective-permute-start(bf16[256,6144]{1,0:T(8,128)(2,1)} %own_ref), channel_id=1, source_target_pairs={{0,1},{1,0},{2,3},{3,2},{4,5},{5,4},{6,7},{7,6},{8,9},{9,8},{10,11... | collective-permute-start | bytes 9437192 | tf_op jit(solution)/shard_map/cube/ppermute | solution.py:54
  2.5 21.8 %all-to-all-start = ((bf16[8,48,2048]{2,1,0:T(8,128)(2,1)}), bf16[8,48,2048]{2,1,0:T(8,128)(2,1)}, u32[]{:S(2)}, u32[]{:S(2)}) async-start(bf16[8,48,2048]{2,1,0:T(8,128)(2,1)} %tile.4), calls=%async_computation | async-start | bytes 3145728 | tf_op jit(solution)/shard_map/cube/all_to_all | solution.py:58
  25.8 10.5 %collective-permute-start.7 = (bf16[128,2048]{1,0:T(8,128)(2,1)S(1)}, bf16[128,2048]{1,0:T(8,128)(2,1)S(1)}, u32[]{:S(2)}, u32[]{:S(2)}) collective-permute-start(bf16[128,2048]{1,0:T(8,128)(2,1)S(1)} %get-tuple-element.23), channel_id=1, source_target_pairs={{0,96},{1,33},{2,98},{3,35},{4,100},{5,37},{6,102},{7,39},{8,104},... | collective-permute-start | bytes 1572872 | tf_op jit(solution)/shard_map/gather_a2/ppermute | solution.py:50
  28.6 9.2 %collective-permute-start.4 = (bf16[128,2048]{1,0:T(8,128)(2,1)S(1)}, bf16[128,2048]{1,0:T(8,128)(2,1)S(1)}, u32[]{:S(2)}, u32[]{:S(2)}) collective-permute-start(bf16[128,2048]{1,0:T(8,128)(2,1)S(1)} %get-tuple-element.24), channel_id=1, source_target_pairs={{0,2},{1,7},{2,0},{3,5},{4,6},{5,3},{6,4},{7,1},{8,10},{9,15},{10,... | collective-permute-start | bytes 1572872 | tf_op jit(solution)/shard_map/gather_a1/ppermute | solution.py:50
  28.6 11.4 %collective-permute-start.1 = (bf16[128,2048]{1,0:T(8,128)(2,1)S(1)}, bf16[128,2048]{1,0:T(8,128)(2,1)S(1)}, u32[]{:S(2)}, u32[]{:S(2)}) collective-permute-start(bf16[128,2048]{1,0:T(8,128)(2,1)S(1)} %get-tuple-element.25), channel_id=1, source_target_pairs={{0,24},{1,9},{2,26},{3,11},{4,28},{5,13},{6,30},{7,15},{8,16},{9,1... | collective-permute-start | bytes 1572872 | tf_op jit(solution)/shard_map/gather_a0/ppermute | solution.py:50
  36.4 14.9 %collective-permute-start.8 = (bf16[256,2048]{1,0:T(8,128)(2,1)S(1)}, bf16[256,2048]{1,0:T(8,128)(2,1)S(1)}, u32[]{:S(2)}, u32[]{:S(2)}) collective-permute-start(bf16[256,2048]{1,0:T(8,128)(2,1)S(1)} %pad_maximum_fusion.4.refs_3_), channel_id=1, source_target_pairs={{0,2},{1,7},{2,0},{3,5},{4,6},{5,3},{6,4},{7,1},{8,10},{9,15},{10,... | collective-permute-start | bytes 3145736 | tf_op jit(solution)/shard_map/gather_b2/ppermute | solution.py:50
  37.8 16.1 %collective-permute-start.5 = (bf16[256,2048]{1,0:T(8,128)(2,1)S(1)}, bf16[256,2048]{1,0:T(8,128)(2,1)S(1)}, u32[]{:S(2)}, u32[]{:S(2)}) collective-permute-start(bf16[256,2048]{1,0:T(8,128)(2,1)S(1)} %pad_maximum_fusion.3.refs_2_), channel_id=1, source_target_pairs={{0,24},{1,9},{2,26},{3,11},{4,28},{5,13},{6,30},{7,15},{8,16},{9,1... | collective-permute-start | bytes 3145736 | tf_op jit(solution)/shard_map/gather_b1/ppermute | solution.py:50
  40.0 16.1 %collective-permute-start.2 = (bf16[256,2048]{1,0:T(8,128)(2,1)S(1)}, bf16[256,2048]{1,0:T(8,128)(2,1)S(1)}, u32[]{:S(2)}, u32[]{:S(2)}) collective-permute-start(bf16[256,2048]{1,0:T(8,128)(2,1)S(1)} %pad_maximum_fusion.2.refs_1_), channel_id=1, source_target_pairs={{0,96},{1,33},{2,98},{3,35},{4,100},{5,37},{6,102},{7,39},{8,104},... | collective-permute-start | bytes 3145736 | tf_op jit(solution)/shard_map/gather_b0/ppermute | solution.py:50
  41.7 23.5 %collective-permute-start.12 = (bf16[256,2048]{1,0:T(8,128)(2,1)S(1)}, bf16[256,2048]{1,0:T(8,128)(2,1)S(1)}, u32[]{:S(2)}, u32[]{:S(2)}) collective-permute-start(bf16[256,2048]{1,0:T(8,128)(2,1)S(1)} %pad_maximum_fusion.4.refs_3_), channel_id=1, source_target_pairs={{0,24},{1,9},{2,26},{3,11},{4,28},{5,13},{6,30},{7,15},{8,16},{9,1... | collective-permute-start | bytes 3145736 | tf_op jit(solution)/shard_map/gather_c2/ppermute | solution.py:50
  42.8 27.8 %collective-permute-start.11 = (bf16[256,2048]{1,0:T(8,128)(2,1)S(1)}, bf16[256,2048]{1,0:T(8,128)(2,1)S(1)}, u32[]{:S(2)}, u32[]{:S(2)}) collective-permute-start(bf16[256,2048]{1,0:T(8,128)(2,1)S(1)} %pad_maximum_fusion.3.refs_2_), channel_id=1, source_target_pairs={{0,96},{1,33},{2,98},{3,35},{4,100},{5,37},{6,102},{7,39},{8,104},... | collective-permute-start | bytes 3145736 | tf_op jit(solution)/shard_map/gather_c1/ppermute | solution.py:50
  51.3 19.4 %collective-permute-start.10 = (bf16[256,2048]{1,0:T(8,128)(2,1)S(1)}, bf16[256,2048]{1,0:T(8,128)(2,1)S(1)}, u32[]{:S(2)}, u32[]{:S(2)}) collective-permute-start(bf16[256,2048]{1,0:T(8,128)(2,1)S(1)} %pad_maximum_fusion.2.refs_1_), channel_id=1, source_target_pairs={{0,2},{1,7},{2,0},{3,5},{4,6},{5,3},{6,4},{7,1},{8,10},{9,15},{10,... | collective-permute-start | bytes 3145736 | tf_op jit(solution)/shard_map/gather_c0/ppermute | solution.py:50
  53.9 22.5 %collective-permute-start.9 = (bf16[256,2048]{1,0:T(8,128)(2,1)S(1)}, bf16[256,2048]{1,0:T(8,128)(2,1)S(1)}, u32[]{:S(2)}, u32[]{:S(2)}) collective-permute-start(bf16[256,2048]{1,0:T(8,128)(2,1)S(1)} %collective-permute-done.8.refs_6_), channel_id=1, source_target_pairs={{0,24},{1,9},{2,26},{3,11},{4,28},{5,13},{6,30},{7,15},{8,16},{9,1... | collective-permute-start | bytes 3145736 | tf_op jit(solution)/shard_map/gather_d2/ppermute | solution.py:50
  56.1 22.5 %collective-permute-start.6 = (bf16[256,2048]{1,0:T(8,128)(2,1)S(1)}, bf16[256,2048]{1,0:T(8,128)(2,1)S(1)}, u32[]{:S(2)}, u32[]{:S(2)}) collective-permute-start(bf16[256,2048]{1,0:T(8,128)(2,1)S(1)} %collective-permute-done.5.refs_5_), channel_id=1, source_target_pairs={{0,96},{1,33},{2,98},{3,35},{4,100},{5,37},{6,102},{7,39},{8,104},... | collective-permute-start | bytes 3145736 | tf_op jit(solution)/shard_map/gather_d1/ppermute | solution.py:50
  65.2 14.8 %collective-permute-start.3 = (bf16[256,2048]{1,0:T(8,128)(2,1)S(1)}, bf16[256,2048]{1,0:T(8,128)(2,1)S(1)}, u32[]{:S(2)}, u32[]{:S(2)}) collective-permute-start(bf16[256,2048]{1,0:T(8,128)(2,1)S(1)} %collective-permute-done.2.refs_4_), channel_id=1, source_target_pairs={{0,2},{1,7},{2,0},{3,5},{4,6},{5,3},{6,4},{7,1},{8,10},{9,15},{10,... | collective-permute-start | bytes 3145736 | tf_op jit(solution)/shard_map/gather_d0/ppermute | solution.py:50
  73.7 8.5 %collective-permute-start.13 = (bf16[256,2048]{1,0:T(8,128)(2,1)S(1)}, bf16[256,2048]{1,0:T(8,128)(2,1)S(1)}, u32[]{:S(2)}, u32[]{:S(2)}) collective-permute-start(bf16[256,2048]{1,0:T(8,128)(2,1)S(1)} %get-tuple-element.22), channel_id=1, source_target_pairs={{0,1},{1,0},{2,3},{3,2},{4,5},{5,4},{6,7},{7,6},{8,9},{9,8},{10,11... | collective-permute-start | bytes 3145736 | tf_op jit(solution)/shard_map/forward1/ppermute | solution.py:54
  81.5 2.7 %collective-permute-start.14 = (bf16[256,2048]{1,0:T(8,128)(2,1)S(1)}, bf16[256,2048]{1,0:T(8,128)(2,1)S(1)}, u32[]{:S(2)}, u32[]{:S(2)}) collective-permute-start(bf16[256,2048]{1,0:T(8,128)(2,1)S(1)} %forward2.1), channel_id=1, source_target_pairs={{0,1},{1,0},{2,3},{3,2},{4,5},{5,4},{6,7},{7,6},{8,9},{9,8},{10,11... | collective-permute-start | bytes 3145736 | tf_op jit(solution)/shard_map/forward2/ppermute | solution.py:54
  82.2 2.0 %copy-start.3 = (bf16[256,2048]{1,0:T(8,128)(2,1)S(1)}, bf16[256,2048]{1,0:T(8,128)(2,1)}, u32[]{:S(2)}) copy-start(bf16[256,2048]{1,0:T(8,128)(2,1)} %target_ref.1) | copy-start | bytes 3145732
  84.2 4.2 %copy-start.1 = (bf16[3,8,8,16,512]{4,3,2,1,0:T(8,128)(2,1)S(1)}, bf16[3,8,8,16,512]{4,3,2,1,0:T(8,128)(2,1)}, u32[]{:S(2)}) copy-start(bf16[3,8,8,16,512]{4,3,2,1,0:T(8,128)(2,1)} %copy-done) | copy-start | bytes 9437188
  85.6 2.8 %collective-permute-start.15 = (bf16[256,2048]{1,0:T(8,128)(2,1)S(1)}, bf16[256,2048]{1,0:T(8,128)(2,1)S(1)}, u32[]{:S(2)}, u32[]{:S(2)}) collective-permute-start(bf16[256,2048]{1,0:T(8,128)(2,1)S(1)} %grad.1), channel_id=1, source_target_pairs={{0,1},{1,0},{2,3},{3,2},{4,5},{5,4},{6,7},{7,6},{8,9},{9,8},{10,11... | collective-permute-start | bytes 3145736 | tf_op jit(solution)/shard_map/grad/ppermute | solution.py:54
  89.1 14.9 %collective-permute-start.17 = (bf16[256,2048]{1,0:T(8,128)(2,1)S(1)}, bf16[256,2048]{1,0:T(8,128)(2,1)S(1)}, u32[]{:S(2)}, u32[]{:S(2)}) collective-permute-start(bf16[256,2048]{1,0:T(8,128)(2,1)S(1)} %convolution_convert_fusion.4), channel_id=1, source_target_pairs={{0,2},{1,7},{2,0},{3,5},{4,6},{5,3},{6,4},{7,1},{8,10},{9,15},{10,... | collective-permute-start | bytes 3145736 | tf_op jit(solution)/shard_map/reduce_d0/ppermute | solution.py:50
  90.7 16.1 %collective-permute-start.21 = (bf16[256,2048]{1,0:T(8,128)(2,1)S(1)}, bf16[256,2048]{1,0:T(8,128)(2,1)S(1)}, u32[]{:S(2)}, u32[]{:S(2)}) collective-permute-start(bf16[256,2048]{1,0:T(8,128)(2,1)S(1)} %convolution_convert_fusion.2), channel_id=1, source_target_pairs={{0,96},{1,33},{2,98},{3,35},{4,100},{5,37},{6,102},{7,39},{8,104},... | collective-permute-start | bytes 3145736 | tf_op jit(solution)/shard_map/reduce_d1/ppermute | solution.py:50
  94.2 21.1 %collective-permute-start.16 = (bf16[256,2048]{1,0:T(8,128)(2,1)S(1)}, bf16[256,2048]{1,0:T(8,128)(2,1)S(1)}, u32[]{:S(2)}, u32[]{:S(2)}) collective-permute-start(bf16[256,2048]{1,0:T(8,128)(2,1)S(1)} %convolution_convert_fusion.5), channel_id=1, source_target_pairs={{0,2},{1,7},{2,0},{3,5},{4,6},{5,3},{6,4},{7,1},{8,10},{9,15},{10,... | collective-permute-start | bytes 3145736 | tf_op jit(solution)/shard_map/reduce_c0/ppermute | solution.py:50
  95.2 16.1 %collective-permute-start.25 = (bf16[256,2048]{1,0:T(8,128)(2,1)S(1)}, bf16[256,2048]{1,0:T(8,128)(2,1)S(1)}, u32[]{:S(2)}, u32[]{:S(2)}) collective-permute-start(bf16[256,2048]{1,0:T(8,128)(2,1)S(1)} %convolution_convert_fusion), channel_id=1, source_target_pairs={{0,24},{1,9},{2,26},{3,11},{4,28},{5,13},{6,30},{7,15},{8,16},{9,1... | collective-permute-start | bytes 3145736 | tf_op jit(solution)/shard_map/reduce_d2/ppermute | solution.py:50
  98.1 33.5 %collective-permute-start.20 = (bf16[256,2048]{1,0:T(8,128)(2,1)S(1)}, bf16[256,2048]{1,0:T(8,128)(2,1)S(1)}, u32[]{:S(2)}, u32[]{:S(2)}) collective-permute-start(bf16[256,2048]{1,0:T(8,128)(2,1)S(1)} %convolution_convert_fusion.3), channel_id=1, source_target_pairs={{0,96},{1,33},{2,98},{3,35},{4,100},{5,37},{6,102},{7,39},{8,104},... | collective-permute-start | bytes 3145736 | tf_op jit(solution)/shard_map/reduce_c1/ppermute | solution.py:50
  104.7 24.5 %collective-permute-start.18 = (bf16[256,2048]{1,0:T(8,128)(2,1)S(1)}, bf16[256,2048]{1,0:T(8,128)(2,1)S(1)}, u32[]{:S(2)}, u32[]{:S(2)}) collective-permute-start(bf16[256,2048]{1,0:T(8,128)(2,1)S(1)} %fusion.3), channel_id=1, source_target_pairs={{0,96},{1,33},{2,98},{3,35},{4,100},{5,37},{6,102},{7,39},{8,104},... | collective-permute-start | bytes 3145736 | tf_op jit(solution)/shard_map/reduce_b0/ppermute | solution.py:50
  107.5 24.1 %collective-permute-start.22 = (bf16[256,2048]{1,0:T(8,128)(2,1)S(1)}, bf16[256,2048]{1,0:T(8,128)(2,1)S(1)}, u32[]{:S(2)}, u32[]{:S(2)}) collective-permute-start(bf16[256,2048]{1,0:T(8,128)(2,1)S(1)} %fusion.4), channel_id=1, source_target_pairs={{0,24},{1,9},{2,26},{3,11},{4,28},{5,13},{6,30},{7,15},{8,16},{9,1... | collective-permute-start | bytes 3145736 | tf_op jit(solution)/shard_map/reduce_b1/ppermute | solution.py:50
  111.2 23.6 %collective-permute-start.24 = (bf16[256,2048]{1,0:T(8,128)(2,1)S(1)}, bf16[256,2048]{1,0:T(8,128)(2,1)S(1)}, u32[]{:S(2)}, u32[]{:S(2)}) collective-permute-start(bf16[256,2048]{1,0:T(8,128)(2,1)S(1)} %convolution_convert_fusion.1), channel_id=1, source_target_pairs={{0,24},{1,9},{2,26},{3,11},{4,28},{5,13},{6,30},{7,15},{8,16},{9,1... | collective-permute-start | bytes 3145736 | tf_op jit(solution)/shard_map/reduce_c2/ppermute | solution.py:50
  115.2 19.6 %collective-permute-start.26 = (bf16[256,2048]{1,0:T(8,128)(2,1)S(1)}, bf16[256,2048]{1,0:T(8,128)(2,1)S(1)}, u32[]{:S(2)}, u32[]{:S(2)}) collective-permute-start(bf16[256,2048]{1,0:T(8,128)(2,1)S(1)} %fusion.5), channel_id=1, source_target_pairs={{0,2},{1,7},{2,0},{3,5},{4,6},{5,3},{6,4},{7,1},{8,10},{9,15},{10,... | collective-permute-start | bytes 3145736 | tf_op jit(solution)/shard_map/reduce_b2/ppermute | solution.py:50
  130.1 10.5 %collective-permute-start.19 = (bf16[128,2048]{1,0:T(8,128)(2,1)S(1)}, bf16[128,2048]{1,0:T(8,128)(2,1)S(1)}, u32[]{:S(2)}, u32[]{:S(2)}) collective-permute-start(bf16[128,2048]{1,0:T(8,128)(2,1)S(1)} %slice.155), channel_id=1, source_target_pairs={{0,24},{1,9},{2,26},{3,11},{4,28},{5,13},{6,30},{7,15},{8,16},{9,1... | collective-permute-start | bytes 1572872 | tf_op jit(solution)/shard_map/reduce_a0/ppermute | solution.py:50
  132.4 9.3 %collective-permute-start.23 = (bf16[128,2048]{1,0:T(8,128)(2,1)S(1)}, bf16[128,2048]{1,0:T(8,128)(2,1)S(1)}, u32[]{:S(2)}, u32[]{:S(2)}) collective-permute-start(bf16[128,2048]{1,0:T(8,128)(2,1)S(1)} %slice.154), channel_id=1, source_target_pairs={{0,2},{1,7},{2,0},{3,5},{4,6},{5,3},{6,4},{7,1},{8,10},{9,15},{10,... | collective-permute-start | bytes 1572872 | tf_op jit(solution)/shard_map/reduce_a1/ppermute | solution.py:50
  135.6 10.5 %collective-permute-start.27 = (bf16[128,2048]{1,0:T(8,128)(2,1)S(1)}, bf16[128,2048]{1,0:T(8,128)(2,1)S(1)}, u32[]{:S(2)}, u32[]{:S(2)}) collective-permute-start(bf16[128,2048]{1,0:T(8,128)(2,1)S(1)} %slice.153), channel_id=1, source_target_pairs={{0,96},{1,33},{2,98},{3,35},{4,100},{5,37},{6,102},{7,39},{8,104},... | collective-permute-start | bytes 1572872 | tf_op jit(solution)/shard_map/reduce_a2/ppermute | solution.py:50
  (2 other events, 3.6 us)

commit v5 on v4

--- a/solution.py
+++ b/solution.py
@@ -1,3 +1,5 @@
+import functools
+
 import jax
 import jax.numpy as jnp
 from jax import lax
@@ -159,15 +161,16 @@
     )(rows, *pieces, *added)
 
 
-def grad_kernel(count_ref, own_ref, other_ref, target_ref, gain_ref, out_ref):
+def grad_kernel(first, count_ref, own_ref, other_ref, target_ref, gain_ref, out_ref):
     rows, width = out_ref.shape
     tile = 64
     gain = gain_ref[...]
 
     @pl.loop(0, rows // tile)
     def _(i):
-        at = pl.ds(pl.multiple_of(i * tile, tile), tile)
-        row = lax.broadcasted_iota(jnp.int32, (tile, 1), 0) + i * tile
+        to = pl.ds(pl.multiple_of(i * tile, tile), tile)
+        at = pl.ds(pl.multiple_of(first + i * tile, tile), tile)
+        row = lax.broadcasted_iota(jnp.int32, (tile, 1), 0) + first + i * tile
         live = (row < count_ref[0]).astype(F32)
         joined = own_ref[at, :].astype(F32) + other_ref[at, :].astype(F32)
         inverse = lax.rsqrt(jnp.mean(joined * joined, axis=1, keepdims=True) + epsilon)
@@ -175,14 +178,14 @@
         error = live * (normed * gain - target_ref[at, :].astype(F32))
         scaled = error * gain
         mean = jnp.mean(scaled * normed, axis=1, keepdims=True)
-        out_ref[at, :] = (inverse * (scaled - normed * mean)).astype(BF16)
-
-
-def joined_grad_of(row_counts, own, other, target_rows, norm_gain):
-    rows, width = target_rows.shape
+        out_ref[to, :] = (inverse * (scaled - normed * mean)).astype(BF16)
+
+
+def joined_grad_of(first, row_counts, own, other, target_rows, norm_gain):
+    rows, width = target_rows.shape[0] // 2, target_rows.shape[1]
     whole = pl.BlockSpec(memory_space=pltpu.VMEM)
     return pl.pallas_call(
-        grad_kernel,
+        functools.partial(grad_kernel, first),
         in_specs=[pl.BlockSpec(memory_space=pltpu.SMEM)] + [whole] * 4,
         out_specs=whole,
         out_shape=jax.ShapeDtypeStruct((rows, width), BF16),
@@ -237,9 +240,8 @@
     with jax.named_scope("forward3"):
         (own,) = step((3,), [own, own_rest], 0, (F32,))
     with jax.named_scope("grad"):
-        grad = joined_grad_of(row_counts, own, other, target_rows, norm_gain)
-        other_grad = swap_core(grad)
-        grads = jnp.concatenate([grad, other_grad], 0)
+        grad = [joined_grad_of(first, row_counts, own, other, target_rows, norm_gain) for first in (0, row_total // 2)]
+        grads = jnp.concatenate(grad + [swap_core(part) for part in grad], 0)
 
     def product(s, q):
         return jnp.dot(features[s, q * 256 : (q + 1) * 256], grads, preferred_element_type=F32)

time: 166 us -> 168 us (1.012)
  waiting for transfers between devices: 68.2 us -> 72.3 us
  starting transfers between devices: 43.3 us -> 41.1 us
    ppermute x24, waiting for transfers between devices: 58.3 us -> 63 us  [swap(): return lax.ppermute(value, AXES, swap_pairs(axis))]
    ppermute x24, starting transfers between devices: 36.1 us -> 33.8 us  [swap(): return lax.ppermute(value, AXES, swap_pairs(axis))]
  transfers between devices with their start and end apart: 29 -> 30, of which waited for: 21 -> 21; matrix products, arithmetic and copies ran while one was open for 7% -> 7% of each run, Pallas kernels for 10% -> 11%
where the time goes in v5:
time: 168 us; the launch traced here: 167 us
  waiting for transfers between devices  72.3 us (43%)
  starting transfers between devices  41.1 us (24%)
  Pallas kernels  18.7 us (11%)
  blocking collectives  17.6 us (10%)
  matrix products  8.65 us (5%)
  local copies, waits for them, and re-layouts  5.83 us (3%)
  other arithmetic  1.96 us (1%)
    ppermute x24, waiting for transfers between devices, swap(): return lax.ppermute(value, AXES, swap_pairs(axis))  63 us
    ppermute x24, starting transfers between devices, swap(): return lax.ppermute(value, AXES, swap_pairs(axis))  33.8 us
    all_to_all x1, blocking collectives, cube_exchange(): lax.all_to_all(value, AXES, 0, 0, axis_index_groups=cubes(), tiled=True)  17.6 us
    pallas_call x4, Pallas kernels, forward(): pl.pallas_call(kernel, grid=(width // cols,), in_specs=[pl.BlockSpec((3,...  11.1 us
    dot_general x12, matrix products, product(): jnp.dot(features[s, q * 256:(q + 1) * 256], grads, preferred_element_type...  8.65 us
    all_to_all x1, waiting for transfers between devices, cube_exchange(): lax.all_to_all(value, AXES, 0, 0, axis_index_groups=cubes(), tiled=True)  7.45 us
    all_to_all x1, starting transfers between devices, cube_exchange(): lax.all_to_all(value, AXES, 0, 0, axis_index_groups=cubes(), tiled=True)  6.48 us
    pallas_call x1, Pallas kernels, arrange(): pl.pallas_call(arrange_kernel, grid=(4,), in_specs=[pl.BlockSpec((m, 1536...  4.76 us
  transfers between devices with their start and end apart: 30, of which 21 were waited for; matrix products, arithmetic and copies ran while one was open for 7% of the time, Pallas kernels for 11%

profile of v5, /device:TPU:0, one launch (start us, length us, event | category | flops | bytes accessed | tf_op | source)
XLA Modules:
  0.0 167.2 jit_solution(12409171934767427421)
XLA Ops:
  0.0 2.5 %tile.4 = bf16[8,48,2048]{2,1,0:T(8,128)(2,1)} broadcast(bf16[48,2048]{1,0:T(8,128)(2,1)} %param.8), dimensions={1,2} | broadcast | bytes 1769472 | tf_op jit(solution)/shard_map/cube/tile | solution.py:207
  2.5 6.5 %all-to-all-start = ((bf16[8,48,2048]{2,1,0:T(8,128)(2,1)}), bf16[8,48,2048]{2,1,0:T(8,128)(2,1)}, u32[]{:S(2)}, u32[]{:S(2)}) async-start(bf16[8,48,2048]{2,1,0:T(8,128)(2,1)} %tile.4), calls=%async_computation | async-start | bytes 3145728 | tf_op jit(solution)/shard_map/cube/all_to_all | solution.py:60
  9.0 4.8 %arrange.2 = bf16[3,8,8,16,512]{4,3,2,1,0:T(8,128)(2,1)S(1)} custom-call(bf16[256,6144]{1,0:T(8,128)(2,1)S(1)} %copy-done.3, bf16[256,6144]{1,0:T(8,128)(2,1)} %collective-permute-done.other_ref), custom_call_target="tpu_custom_call" | custom-call | bytes 1024 | tf_op jit(solution)/shard_map/arrange/pallas_call | solution.py:102
  15.2 1.6 copy-done
  16.8 7.4 %all-to-all-done = bf16[8,48,2048]{2,1,0:T(8,128)(2,1)} async-done(((bf16[8,48,2048]{2,1,0:T(8,128)(2,1)}), bf16[8,48,2048]{2,1,0:T(8,128)(2,1)}, u32[]{:S(2)}, u32[]{:S(2)}) %all-to-all-start) | async-done | bytes 1572896 | tf_op jit(solution)/shard_map/cube/all_to_all | solution.py:60
  25.8 2.8 %collective-permute-start.7 = (bf16[128,2048]{1,0:T(8,128)(2,1)S(1)}, bf16[128,2048]{1,0:T(8,128)(2,1)S(1)}, u32[]{:S(2)}, u32[]{:S(2)}) collective-permute-start(bf16[128,2048]{1,0:T(8,128)(2,1)S(1)} %get-tuple-element.23), channel_id=1, source_target_pairs={{0,96},{1,33},{2,98},{3,35},{4,100},{5,37},{6,102},{7,39},{8,104},... | collective-permute-start | bytes 1572872 | tf_op jit(solution)/shard_map/gather_a2/ppermute | solution.py:52
  28.6 2.1 %collective-permute-start.1 = (bf16[128,2048]{1,0:T(8,128)(2,1)S(1)}, bf16[128,2048]{1,0:T(8,128)(2,1)S(1)}, u32[]{:S(2)}, u32[]{:S(2)}) collective-permute-start(bf16[128,2048]{1,0:T(8,128)(2,1)S(1)} %get-tuple-element.25), channel_id=1, source_target_pairs={{0,24},{1,9},{2,26},{3,11},{4,28},{5,13},{6,30},{7,15},{8,16},{9,1... | collective-permute-start | bytes 1572872 | tf_op jit(solution)/shard_map/gather_a0/ppermute | solution.py:52
  30.7 5.6 %collective-permute-done.7 = bf16[128,2048]{1,0:T(8,128)(2,1)S(1)} collective-permute-done((bf16[128,2048]{1,0:T(8,128)(2,1)S(1)}, bf16[128,2048]{1,0:T(8,128)(2,1)S(1)}, u32[]{:S(2)}, u32[]{:S(2)}) %collective-permute-start.7) | collective-permute-done | bytes 524320 | tf_op jit(solution)/shard_map/gather_a2/ppermute | solution.py:52
  37.9 2.1 %collective-permute-start.5 = (bf16[256,2048]{1,0:T(8,128)(2,1)S(1)}, bf16[256,2048]{1,0:T(8,128)(2,1)S(1)}, u32[]{:S(2)}, u32[]{:S(2)}) collective-permute-start(bf16[256,2048]{1,0:T(8,128)(2,1)S(1)} %pad_maximum_fusion.3.refs_2_), channel_id=1, source_target_pairs={{0,24},{1,9},{2,26},{3,11},{4,28},{5,13},{6,30},{7,15},{8,16},{9,1... | collective-permute-start | bytes 3145736 | tf_op jit(solution)/shard_map/gather_b1/ppermute | solution.py:52
  40.1 1.6 collective-permute-start.2
  42.8 1.8 %collective-permute-start.11 = (bf16[256,2048]{1,0:T(8,128)(2,1)S(1)}, bf16[256,2048]{1,0:T(8,128)(2,1)S(1)}, u32[]{:S(2)}, u32[]{:S(2)}) collective-permute-start(bf16[256,2048]{1,0:T(8,128)(2,1)S(1)} %pad_maximum_fusion.3.refs_2_), channel_id=1, source_target_pairs={{0,96},{1,33},{2,98},{3,35},{4,100},{5,37},{6,102},{7,39},{8,104},... | collective-permute-start | bytes 3145736 | tf_op jit(solution)/shard_map/gather_c1/ppermute | solution.py:52
  44.6 6.7 %collective-permute-done.8.refs_6_ = bf16[256,2048]{1,0:T(8,128)(2,1)S(1)} collective-permute-done((bf16[256,2048]{1,0:T(8,128)(2,1)S(1)}, bf16[256,2048]{1,0:T(8,128)(2,1)S(1)}, u32[]{:S(2)}, u32[]{:S(2)}) %collective-permute-start.8) | collective-permute-done | bytes 1048608 | tf_op jit(solution)/shard_map/gather_b2/ppermute | solution.py:52
  51.3 2.7 %collective-permute-done.5.refs_5_ = bf16[256,2048]{1,0:T(8,128)(2,1)S(1)} collective-permute-done((bf16[256,2048]{1,0:T(8,128)(2,1)S(1)}, bf16[256,2048]{1,0:T(8,128)(2,1)S(1)}, u32[]{:S(2)}, u32[]{:S(2)}) %collective-permute-start.5) | collective-permute-done | bytes 1048608 | tf_op jit(solution)/shard_map/gather_b1/ppermute | solution.py:52
  53.9 2.0 %collective-permute-start.9 = (bf16[256,2048]{1,0:T(8,128)(2,1)S(1)}, bf16[256,2048]{1,0:T(8,128)(2,1)S(1)}, u32[]{:S(2)}, u32[]{:S(2)}) collective-permute-start(bf16[256,2048]{1,0:T(8,128)(2,1)S(1)} %collective-permute-done.8.refs_6_), channel_id=1, source_target_pairs={{0,24},{1,9},{2,26},{3,11},{4,28},{5,13},{6,30},{7,15},{8,16},{9,1... | collective-permute-start | bytes 3145736 | tf_op jit(solution)/shard_map/gather_d2/ppermute | solution.py:52
  57.7 7.5 %collective-permute-done.12.refs_3_ = bf16[256,2048]{1,0:T(8,128)(2,1)S(1)} collective-permute-done((bf16[256,2048]{1,0:T(8,128)(2,1)S(1)}, bf16[256,2048]{1,0:T(8,128)(2,1)S(1)}, u32[]{:S(2)}, u32[]{:S(2)}) %collective-permute-start.12) | collective-permute-done | bytes 1048608 | tf_op jit(solution)/shard_map/gather_c2/ppermute | solution.py:52
  65.9 4.7 %forward0.1 = (f32[256,2048]{1,0:T(8,128)S(1)}, f32[256,2048]{1,0:T(8,128)S(1)}) custom-call(bf16[3,512,1024]{2,1,0:T(8,128)(2,1)S(1)} %arrange.3.refs_0_, bf16[256,2048]{1,0:T(8,128)(2,1)S(1)} %pad_maximum_fusion.2.refs_1_, bf16[256,2048]{1,0:T(8,128)(2,1)S(1)} %pad_maximum_fusion.3.refs_2_, bf16[256,2048]{1,0:T(8,128)(2,1)S(1)} %pad_maximum_fusion.4.refs_3_, ...), custom_call_target="tpu_custom_call" | custom-call | flops 3221225472 | bytes 10485760 | tf_op jit(solution)/shard_map/forward0/pallas_call | solution.py:149
  70.6 3.1 %forward1.1 = (f32[256,2048]{1,0:T(8,128)S(1)}, bf16[256,2048]{1,0:T(8,128)(2,1)S(1)}) custom-call(bf16[3,512,1024]{2,1,0:T(8,128)(2,1)S(1)} %arrange.3.refs_0_, bf16[256,2048]{1,0:T(8,128)(2,1)S(1)} %collective-permute-done.10.refs_1_, bf16[256,2048]{1,0:T(8,128)(2,1)S(1)} %collective-permute-done.11.refs_2_, ...), custom_call_target="tpu_custom_call" | custom-call | flops 1610612736 | bytes 11534336 | tf_op jit(solution)/shard_map/forward1/pallas_call | solution.py:149
  73.8 2.6 %collective-permute-done.9.refs_3_ = bf16[256,2048]{1,0:T(8,128)(2,1)S(1)} collective-permute-done((bf16[256,2048]{1,0:T(8,128)(2,1)S(1)}, bf16[256,2048]{1,0:T(8,128)(2,1)S(1)}, u32[]{:S(2)}, u32[]{:S(2)}) %collective-permute-start.9) | collective-permute-done | bytes 1048608 | tf_op jit(solution)/shard_map/gather_d2/ppermute | solution.py:52
  76.4 2.2 %collective-permute-done.6.refs_2_ = bf16[256,2048]{1,0:T(8,128)(2,1)S(1)} collective-permute-done((bf16[256,2048]{1,0:T(8,128)(2,1)S(1)}, bf16[256,2048]{1,0:T(8,128)(2,1)S(1)}, u32[]{:S(2)}, u32[]{:S(2)}) %collective-permute-start.6) | collective-permute-done | bytes 1048608 | tf_op jit(solution)/shard_map/gather_d1/ppermute | solution.py:52
  82.3 1.8 %forward3.1.own_ref = f32[256,2048]{1,0:T(8,128)S(1)} custom-call(bf16[3,512,1024]{2,1,0:T(8,128)(2,1)S(1)} %arrange.3.refs_0_, bf16[256,2048]{1,0:T(8,128)(2,1)S(1)} %collective-permute-done.3.refs_1_, bf16[256,2048]{1,0:T(8,128)(2,1)S(1)} %collective-permute-done.6.refs_2_, bf16[256,2048]{1,0:T(8,128)(2,1)S(1)} %collective-permute-done.9.refs_3_, ...), custom_call_target="tpu_custom_call" | custom-call | flops 805306368 | bytes 11534336 | tf_op jit(solution)/shard_map/forward3/pallas_call | solution.py:149
  94.9 1.9 %collective-permute-start.21 = (bf16[256,2048]{1,0:T(8,128)(2,1)S(1)}, bf16[256,2048]{1,0:T(8,128)(2,1)S(1)}, u32[]{:S(2)}, u32[]{:S(2)}) collective-permute-start(bf16[256,2048]{1,0:T(8,128)(2,1)S(1)} %convolution_convert_fusion.3), channel_id=1, source_target_pairs={{0,96},{1,33},{2,98},{3,35},{4,100},{5,37},{6,102},{7,39},{8,104},... | collective-permute-start | bytes 3145736 | tf_op jit(solution)/shard_map/reduce_c1/ppermute | solution.py:52
  97.5 2.1 %collective-permute-start.26 = (bf16[256,2048]{1,0:T(8,128)(2,1)S(1)}, bf16[256,2048]{1,0:T(8,128)(2,1)S(1)}, u32[]{:S(2)}, u32[]{:S(2)}) collective-permute-start(bf16[256,2048]{1,0:T(8,128)(2,1)S(1)} %convolution_convert_fusion), channel_id=1, source_target_pairs={{0,24},{1,9},{2,26},{3,11},{4,28},{5,13},{6,30},{7,15},{8,16},{9,1... | collective-permute-start | bytes 3145736 | tf_op jit(solution)/shard_map/reduce_d2/ppermute | solution.py:52
  99.6 4.2 %collective-permute-done.18 = bf16[256,2048]{1,0:T(8,128)(2,1)S(1)} collective-permute-done((bf16[256,2048]{1,0:T(8,128)(2,1)S(1)}, bf16[256,2048]{1,0:T(8,128)(2,1)S(1)}, u32[]{:S(2)}, u32[]{:S(2)}) %collective-permute-start.18) | collective-permute-done | bytes 1048608 | tf_op jit(solution)/shard_map/reduce_d0/ppermute | solution.py:52
  106.0 2.8 %collective-permute-done.22 = bf16[256,2048]{1,0:T(8,128)(2,1)S(1)} collective-permute-done((bf16[256,2048]{1,0:T(8,128)(2,1)S(1)}, bf16[256,2048]{1,0:T(8,128)(2,1)S(1)}, u32[]{:S(2)}, u32[]{:S(2)}) %collective-permute-start.22) | collective-permute-done | bytes 1048608 | tf_op jit(solution)/shard_map/reduce_d1/ppermute | solution.py:52
  109.5 2.1 %collective-permute-start.23 = (bf16[256,2048]{1,0:T(8,128)(2,1)S(1)}, bf16[256,2048]{1,0:T(8,128)(2,1)S(1)}, u32[]{:S(2)}, u32[]{:S(2)}) collective-permute-start(bf16[256,2048]{1,0:T(8,128)(2,1)S(1)} %fusion.4), channel_id=1, source_target_pairs={{0,24},{1,9},{2,26},{3,11},{4,28},{5,13},{6,30},{7,15},{8,16},{9,1... | collective-permute-start | bytes 3145736 | tf_op jit(solution)/shard_map/reduce_b1/ppermute | solution.py:52
  113.6 2.0 %collective-permute-start.25 = (bf16[256,2048]{1,0:T(8,128)(2,1)S(1)}, bf16[256,2048]{1,0:T(8,128)(2,1)S(1)}, u32[]{:S(2)}, u32[]{:S(2)}) collective-permute-start(bf16[256,2048]{1,0:T(8,128)(2,1)S(1)} %convolution_convert_fusion.1), channel_id=1, source_target_pairs={{0,24},{1,9},{2,26},{3,11},{4,28},{5,13},{6,30},{7,15},{8,16},{9,1... | collective-permute-start | bytes 3145736 | tf_op jit(solution)/shard_map/reduce_c2/ppermute | solution.py:52
  116.6 14.6 %collective-permute-done.19 = bf16[256,2048]{1,0:T(8,128)(2,1)S(1)} collective-permute-done((bf16[256,2048]{1,0:T(8,128)(2,1)S(1)}, bf16[256,2048]{1,0:T(8,128)(2,1)S(1)}, u32[]{:S(2)}, u32[]{:S(2)}) %collective-permute-start.19) | collective-permute-done | bytes 1048608 | tf_op jit(solution)/shard_map/reduce_b0/ppermute | solution.py:52
  132.0 2.1 %collective-permute-start.20 = (bf16[128,2048]{1,0:T(8,128)(2,1)S(1)}, bf16[128,2048]{1,0:T(8,128)(2,1)S(1)}, u32[]{:S(2)}, u32[]{:S(2)}) collective-permute-start(bf16[128,2048]{1,0:T(8,128)(2,1)S(1)} %slice.155), channel_id=1, source_target_pairs={{0,24},{1,9},{2,26},{3,11},{4,28},{5,13},{6,30},{7,15},{8,16},{9,1... | collective-permute-start | bytes 1572872 | tf_op jit(solution)/shard_map/reduce_a0/ppermute | solution.py:52
  137.6 1.8 %collective-permute-start.28 = (bf16[128,2048]{1,0:T(8,128)(2,1)S(1)}, bf16[128,2048]{1,0:T(8,128)(2,1)S(1)}, u32[]{:S(2)}, u32[]{:S(2)}) collective-permute-start(bf16[128,2048]{1,0:T(8,128)(2,1)S(1)} %slice.153), channel_id=1, source_target_pairs={{0,96},{1,33},{2,98},{3,35},{4,100},{5,37},{6,102},{7,39},{8,104},... | collective-permute-start | bytes 1572872 | tf_op jit(solution)/shard_map/reduce_a2/ppermute | solution.py:52
  139.4 3.1 %collective-permute-done.20 = bf16[128,2048]{1,0:T(8,128)(2,1)S(1)} collective-permute-done((bf16[128,2048]{1,0:T(8,128)(2,1)S(1)}, bf16[128,2048]{1,0:T(8,128)(2,1)S(1)}, u32[]{:S(2)}, u32[]{:S(2)}) %collective-permute-start.20) | collective-permute-done | bytes 524320 | tf_op jit(solution)/shard_map/reduce_a0/ppermute | solution.py:52
  144.3 3.8 %collective-permute-done.28 = bf16[128,2048]{1,0:T(8,128)(2,1)S(1)} collective-permute-done((bf16[128,2048]{1,0:T(8,128)(2,1)S(1)}, bf16[128,2048]{1,0:T(8,128)(2,1)S(1)}, u32[]{:S(2)}, u32[]{:S(2)}) %collective-permute-start.28) | collective-permute-done | bytes 524320 | tf_op jit(solution)/shard_map/reduce_a2/ppermute | solution.py:52
  148.4 17.6 %all_to_all.21 = bf16[8,48,2048]{2,1,0:T(8,128)(2,1)S(1)} all-to-all(bf16[8,48,2048]{2,1,0:T(8,128)(2,1)S(1)} %bitcast.57), channel_id=1, replica_groups={{0,6,8,14,32,38,40,46},{1,3,25,27,97,99,121,123},{2,4,10,12,34,36,42,44..., dimensions={0} | all-to-all | bytes 3145728 | tf_op jit(solution)/shard_map/all_to_all | solution.py:60
  (75 shorter events, 36.2 us)
Async XLA Ops:
  0.0 9.0 %copy-start.3 = (bf16[256,6144]{1,0:T(8,128)(2,1)S(1)}, bf16[256,6144]{1,0:T(8,128)(2,1)}, u32[]{:S(2)}) copy-start(bf16[256,6144]{1,0:T(8,128)(2,1)} %own_ref) | copy-start | bytes 9437188
  0.0 9.0 %collective-permute-start = (bf16[256,6144]{1,0:T(8,128)(2,1)}, bf16[256,6144]{1,0:T(8,128)(2,1)}, u32[]{:S(2)}, u32[]{:S(2)}) collective-permute-start(bf16[256,6144]{1,0:T(8,128)(2,1)} %own_ref), channel_id=1, source_target_pairs={{0,1},{1,0},{2,3},{3,2},{4,5},{5,4},{6,7},{7,6},{8,9},{9,8},{10,11... | collective-permute-start | bytes 9437192 | tf_op jit(solution)/shard_map/cube/ppermute | solution.py:56
  2.5 21.8 %all-to-all-start = ((bf16[8,48,2048]{2,1,0:T(8,128)(2,1)}), bf16[8,48,2048]{2,1,0:T(8,128)(2,1)}, u32[]{:S(2)}, u32[]{:S(2)}) async-start(bf16[8,48,2048]{2,1,0:T(8,128)(2,1)} %tile.4), calls=%async_computation | async-start | bytes 3145728 | tf_op jit(solution)/shard_map/cube/all_to_all | solution.py:60
  25.8 10.5 %collective-permute-start.7 = (bf16[128,2048]{1,0:T(8,128)(2,1)S(1)}, bf16[128,2048]{1,0:T(8,128)(2,1)S(1)}, u32[]{:S(2)}, u32[]{:S(2)}) collective-permute-start(bf16[128,2048]{1,0:T(8,128)(2,1)S(1)} %get-tuple-element.23), channel_id=1, source_target_pairs={{0,96},{1,33},{2,98},{3,35},{4,100},{5,37},{6,102},{7,39},{8,104},... | collective-permute-start | bytes 1572872 | tf_op jit(solution)/shard_map/gather_a2/ppermute | solution.py:52
  28.6 9.2 %collective-permute-start.4 = (bf16[128,2048]{1,0:T(8,128)(2,1)S(1)}, bf16[128,2048]{1,0:T(8,128)(2,1)S(1)}, u32[]{:S(2)}, u32[]{:S(2)}) collective-permute-start(bf16[128,2048]{1,0:T(8,128)(2,1)S(1)} %get-tuple-element.24), channel_id=1, source_target_pairs={{0,2},{1,7},{2,0},{3,5},{4,6},{5,3},{6,4},{7,1},{8,10},{9,15},{10,... | collective-permute-start | bytes 1572872 | tf_op jit(solution)/shard_map/gather_a1/ppermute | solution.py:52
  28.6 11.4 %collective-permute-start.1 = (bf16[128,2048]{1,0:T(8,128)(2,1)S(1)}, bf16[128,2048]{1,0:T(8,128)(2,1)S(1)}, u32[]{:S(2)}, u32[]{:S(2)}) collective-permute-start(bf16[128,2048]{1,0:T(8,128)(2,1)S(1)} %get-tuple-element.25), channel_id=1, source_target_pairs={{0,24},{1,9},{2,26},{3,11},{4,28},{5,13},{6,30},{7,15},{8,16},{9,1... | collective-permute-start | bytes 1572872 | tf_op jit(solution)/shard_map/gather_a0/ppermute | solution.py:52
  36.4 14.9 %collective-permute-start.8 = (bf16[256,2048]{1,0:T(8,128)(2,1)S(1)}, bf16[256,2048]{1,0:T(8,128)(2,1)S(1)}, u32[]{:S(2)}, u32[]{:S(2)}) collective-permute-start(bf16[256,2048]{1,0:T(8,128)(2,1)S(1)} %pad_maximum_fusion.4.refs_3_), channel_id=1, source_target_pairs={{0,2},{1,7},{2,0},{3,5},{4,6},{5,3},{6,4},{7,1},{8,10},{9,15},{10,... | collective-permute-start | bytes 3145736 | tf_op jit(solution)/shard_map/gather_b2/ppermute | solution.py:52
  37.9 16.1 %collective-permute-start.5 = (bf16[256,2048]{1,0:T(8,128)(2,1)S(1)}, bf16[256,2048]{1,0:T(8,128)(2,1)S(1)}, u32[]{:S(2)}, u32[]{:S(2)}) collective-permute-start(bf16[256,2048]{1,0:T(8,128)(2,1)S(1)} %pad_maximum_fusion.3.refs_2_), channel_id=1, source_target_pairs={{0,24},{1,9},{2,26},{3,11},{4,28},{5,13},{6,30},{7,15},{8,16},{9,1... | collective-permute-start | bytes 3145736 | tf_op jit(solution)/shard_map/gather_b1/ppermute | solution.py:52
  40.1 16.1 %collective-permute-start.2 = (bf16[256,2048]{1,0:T(8,128)(2,1)S(1)}, bf16[256,2048]{1,0:T(8,128)(2,1)S(1)}, u32[]{:S(2)}, u32[]{:S(2)}) collective-permute-start(bf16[256,2048]{1,0:T(8,128)(2,1)S(1)} %pad_maximum_fusion.2.refs_1_), channel_id=1, source_target_pairs={{0,96},{1,33},{2,98},{3,35},{4,100},{5,37},{6,102},{7,39},{8,104},... | collective-permute-start | bytes 3145736 | tf_op jit(solution)/shard_map/gather_b0/ppermute | solution.py:52
  41.7 23.5 %collective-permute-start.12 = (bf16[256,2048]{1,0:T(8,128)(2,1)S(1)}, bf16[256,2048]{1,0:T(8,128)(2,1)S(1)}, u32[]{:S(2)}, u32[]{:S(2)}) collective-permute-start(bf16[256,2048]{1,0:T(8,128)(2,1)S(1)} %pad_maximum_fusion.4.refs_3_), channel_id=1, source_target_pairs={{0,24},{1,9},{2,26},{3,11},{4,28},{5,13},{6,30},{7,15},{8,16},{9,1... | collective-permute-start | bytes 3145736 | tf_op jit(solution)/shard_map/gather_c2/ppermute | solution.py:52
  42.8 27.8 %collective-permute-start.11 = (bf16[256,2048]{1,0:T(8,128)(2,1)S(1)}, bf16[256,2048]{1,0:T(8,128)(2,1)S(1)}, u32[]{:S(2)}, u32[]{:S(2)}) collective-permute-start(bf16[256,2048]{1,0:T(8,128)(2,1)S(1)} %pad_maximum_fusion.3.refs_2_), channel_id=1, source_target_pairs={{0,96},{1,33},{2,98},{3,35},{4,100},{5,37},{6,102},{7,39},{8,104},... | collective-permute-start | bytes 3145736 | tf_op jit(solution)/shard_map/gather_c1/ppermute | solution.py:52
  51.3 19.4 %collective-permute-start.10 = (bf16[256,2048]{1,0:T(8,128)(2,1)S(1)}, bf16[256,2048]{1,0:T(8,128)(2,1)S(1)}, u32[]{:S(2)}, u32[]{:S(2)}) collective-permute-start(bf16[256,2048]{1,0:T(8,128)(2,1)S(1)} %pad_maximum_fusion.2.refs_1_), channel_id=1, source_target_pairs={{0,2},{1,7},{2,0},{3,5},{4,6},{5,3},{6,4},{7,1},{8,10},{9,15},{10,... | collective-permute-start | bytes 3145736 | tf_op jit(solution)/shard_map/gather_c0/ppermute | solution.py:52
  53.9 22.5 %collective-permute-start.9 = (bf16[256,2048]{1,0:T(8,128)(2,1)S(1)}, bf16[256,2048]{1,0:T(8,128)(2,1)S(1)}, u32[]{:S(2)}, u32[]{:S(2)}) collective-permute-start(bf16[256,2048]{1,0:T(8,128)(2,1)S(1)} %collective-permute-done.8.refs_6_), channel_id=1, source_target_pairs={{0,24},{1,9},{2,26},{3,11},{4,28},{5,13},{6,30},{7,15},{8,16},{9,1... | collective-permute-start | bytes 3145736 | tf_op jit(solution)/shard_map/gather_d2/ppermute | solution.py:52
  56.1 22.5 %collective-permute-start.6 = (bf16[256,2048]{1,0:T(8,128)(2,1)S(1)}, bf16[256,2048]{1,0:T(8,128)(2,1)S(1)}, u32[]{:S(2)}, u32[]{:S(2)}) collective-permute-start(bf16[256,2048]{1,0:T(8,128)(2,1)S(1)} %collective-permute-done.5.refs_5_), channel_id=1, source_target_pairs={{0,96},{1,33},{2,98},{3,35},{4,100},{5,37},{6,102},{7,39},{8,104},... | collective-permute-start | bytes 3145736 | tf_op jit(solution)/shard_map/gather_d1/ppermute | solution.py:52
  65.2 14.8 %collective-permute-start.3 = (bf16[256,2048]{1,0:T(8,128)(2,1)S(1)}, bf16[256,2048]{1,0:T(8,128)(2,1)S(1)}, u32[]{:S(2)}, u32[]{:S(2)}) collective-permute-start(bf16[256,2048]{1,0:T(8,128)(2,1)S(1)} %collective-permute-done.2.refs_4_), channel_id=1, source_target_pairs={{0,2},{1,7},{2,0},{3,5},{4,6},{5,3},{6,4},{7,1},{8,10},{9,15},{10,... | collective-permute-start | bytes 3145736 | tf_op jit(solution)/shard_map/gather_d0/ppermute | solution.py:52
  73.7 8.5 %collective-permute-start.13 = (bf16[256,2048]{1,0:T(8,128)(2,1)S(1)}, bf16[256,2048]{1,0:T(8,128)(2,1)S(1)}, u32[]{:S(2)}, u32[]{:S(2)}) collective-permute-start(bf16[256,2048]{1,0:T(8,128)(2,1)S(1)} %get-tuple-element.22), channel_id=1, source_target_pairs={{0,1},{1,0},{2,3},{3,2},{4,5},{5,4},{6,7},{7,6},{8,9},{9,8},{10,11... | collective-permute-start | bytes 3145736 | tf_op jit(solution)/shard_map/forward1/ppermute | solution.py:56
  81.5 2.7 %collective-permute-start.14 = (bf16[256,2048]{1,0:T(8,128)(2,1)S(1)}, bf16[256,2048]{1,0:T(8,128)(2,1)S(1)}, u32[]{:S(2)}, u32[]{:S(2)}) collective-permute-start(bf16[256,2048]{1,0:T(8,128)(2,1)S(1)} %forward2.1), channel_id=1, source_target_pairs={{0,1},{1,0},{2,3},{3,2},{4,5},{5,4},{6,7},{7,6},{8,9},{9,8},{10,11... | collective-permute-start | bytes 3145736 | tf_op jit(solution)/shard_map/forward2/ppermute | solution.py:56
  84.9 3.2 %copy-start.1 = (bf16[3,8,8,16,512]{4,3,2,1,0:T(8,128)(2,1)S(1)}, bf16[3,8,8,16,512]{4,3,2,1,0:T(8,128)(2,1)}, u32[]{:S(2)}) copy-start(bf16[3,8,8,16,512]{4,3,2,1,0:T(8,128)(2,1)} %copy-done) | copy-start | bytes 9437188
  85.0 2.0 %collective-permute-start.15 = (bf16[128,2048]{1,0:T(8,128)(2,1)S(1)}, bf16[128,2048]{1,0:T(8,128)(2,1)S(1)}, u32[]{:S(2)}, u32[]{:S(2)}) collective-permute-start(bf16[128,2048]{1,0:T(8,128)(2,1)S(1)} %grad.2), channel_id=1, source_target_pairs={{0,1},{1,0},{2,3},{3,2},{4,5},{5,4},{6,7},{7,6},{8,9},{9,8},{10,11... | collective-permute-start | bytes 1572872 | tf_op jit(solution)/shard_map/grad/ppermute | solution.py:56
  86.1 2.0 %collective-permute-start.16 = (bf16[128,2048]{1,0:T(8,128)(2,1)S(1)}, bf16[128,2048]{1,0:T(8,128)(2,1)S(1)}, u32[]{:S(2)}, u32[]{:S(2)}) collective-permute-start(bf16[128,2048]{1,0:T(8,128)(2,1)S(1)} %grad.3), channel_id=1, source_target_pairs={{0,1},{1,0},{2,3},{3,2},{4,5},{5,4},{6,7},{7,6},{8,9},{9,8},{10,11... | collective-permute-start | bytes 1572872 | tf_op jit(solution)/shard_map/grad/ppermute | solution.py:56
  88.9 14.9 %collective-permute-start.18 = (bf16[256,2048]{1,0:T(8,128)(2,1)S(1)}, bf16[256,2048]{1,0:T(8,128)(2,1)S(1)}, u32[]{:S(2)}, u32[]{:S(2)}) collective-permute-start(bf16[256,2048]{1,0:T(8,128)(2,1)S(1)} %convolution_convert_fusion.4), channel_id=1, source_target_pairs={{0,2},{1,7},{2,0},{3,5},{4,6},{5,3},{6,4},{7,1},{8,10},{9,15},{10,... | collective-permute-start | bytes 3145736 | tf_op jit(solution)/shard_map/reduce_d0/ppermute | solution.py:52
  90.4 25.9 %collective-permute-start.17 = (bf16[256,2048]{1,0:T(8,128)(2,1)S(1)}, bf16[256,2048]{1,0:T(8,128)(2,1)S(1)}, u32[]{:S(2)}, u32[]{:S(2)}) collective-permute-start(bf16[256,2048]{1,0:T(8,128)(2,1)S(1)} %convolution_convert_fusion.5), channel_id=1, source_target_pairs={{0,2},{1,7},{2,0},{3,5},{4,6},{5,3},{6,4},{7,1},{8,10},{9,15},{10,... | collective-permute-start | bytes 3145736 | tf_op jit(solution)/shard_map/reduce_c0/ppermute | solution.py:52
  92.7 16.1 %collective-permute-start.22 = (bf16[256,2048]{1,0:T(8,128)(2,1)S(1)}, bf16[256,2048]{1,0:T(8,128)(2,1)S(1)}, u32[]{:S(2)}, u32[]{:S(2)}) collective-permute-start(bf16[256,2048]{1,0:T(8,128)(2,1)S(1)} %convolution_convert_fusion.2), channel_id=1, source_target_pairs={{0,96},{1,33},{2,98},{3,35},{4,100},{5,37},{6,102},{7,39},{8,104},... | collective-permute-start | bytes 3145736 | tf_op jit(solution)/shard_map/reduce_d1/ppermute | solution.py:52
  94.9 39.3 %collective-permute-start.21 = (bf16[256,2048]{1,0:T(8,128)(2,1)S(1)}, bf16[256,2048]{1,0:T(8,128)(2,1)S(1)}, u32[]{:S(2)}, u32[]{:S(2)}) collective-permute-start(bf16[256,2048]{1,0:T(8,128)(2,1)S(1)} %convolution_convert_fusion.3), channel_id=1, source_target_pairs={{0,96},{1,33},{2,98},{3,35},{4,100},{5,37},{6,102},{7,39},{8,104},... | collective-permute-start | bytes 3145736 | tf_op jit(solution)/shard_map/reduce_c1/ppermute | solution.py:52
  97.5 16.1 %collective-permute-start.26 = (bf16[256,2048]{1,0:T(8,128)(2,1)S(1)}, bf16[256,2048]{1,0:T(8,128)(2,1)S(1)}, u32[]{:S(2)}, u32[]{:S(2)}) collective-permute-start(bf16[256,2048]{1,0:T(8,128)(2,1)S(1)} %convolution_convert_fusion), channel_id=1, source_target_pairs={{0,24},{1,9},{2,26},{3,11},{4,28},{5,13},{6,30},{7,15},{8,16},{9,1... | collective-permute-start | bytes 3145736 | tf_op jit(solution)/shard_map/reduce_d2/ppermute | solution.py:52
  104.5 26.8 %collective-permute-start.19 = (bf16[256,2048]{1,0:T(8,128)(2,1)S(1)}, bf16[256,2048]{1,0:T(8,128)(2,1)S(1)}, u32[]{:S(2)}, u32[]{:S(2)}) collective-permute-start(bf16[256,2048]{1,0:T(8,128)(2,1)S(1)} %fusion.3), channel_id=1, source_target_pairs={{0,96},{1,33},{2,98},{3,35},{4,100},{5,37},{6,102},{7,39},{8,104},... | collective-permute-start | bytes 3145736 | tf_op jit(solution)/shard_map/reduce_b0/ppermute | solution.py:52
  109.5 24.7 %collective-permute-start.23 = (bf16[256,2048]{1,0:T(8,128)(2,1)S(1)}, bf16[256,2048]{1,0:T(8,128)(2,1)S(1)}, u32[]{:S(2)}, u32[]{:S(2)}) collective-permute-start(bf16[256,2048]{1,0:T(8,128)(2,1)S(1)} %fusion.4), channel_id=1, source_target_pairs={{0,24},{1,9},{2,26},{3,11},{4,28},{5,13},{6,30},{7,15},{8,16},{9,1... | collective-permute-start | bytes 3145736 | tf_op jit(solution)/shard_map/reduce_b1/ppermute | solution.py:52
  113.6 23.2 %collective-permute-start.25 = (bf16[256,2048]{1,0:T(8,128)(2,1)S(1)}, bf16[256,2048]{1,0:T(8,128)(2,1)S(1)}, u32[]{:S(2)}, u32[]{:S(2)}) collective-permute-start(bf16[256,2048]{1,0:T(8,128)(2,1)S(1)} %convolution_convert_fusion.1), channel_id=1, source_target_pairs={{0,24},{1,9},{2,26},{3,11},{4,28},{5,13},{6,30},{7,15},{8,16},{9,1... | collective-permute-start | bytes 3145736 | tf_op jit(solution)/shard_map/reduce_c2/ppermute | solution.py:52
  116.3 20.5 %collective-permute-start.27 = (bf16[256,2048]{1,0:T(8,128)(2,1)S(1)}, bf16[256,2048]{1,0:T(8,128)(2,1)S(1)}, u32[]{:S(2)}, u32[]{:S(2)}) collective-permute-start(bf16[256,2048]{1,0:T(8,128)(2,1)S(1)} %fusion.5), channel_id=1, source_target_pairs={{0,2},{1,7},{2,0},{3,5},{4,6},{5,3},{6,4},{7,1},{8,10},{9,15},{10,... | collective-permute-start | bytes 3145736 | tf_op jit(solution)/shard_map/reduce_b2/ppermute | solution.py:52
  132.0 10.5 %collective-permute-start.20 = (bf16[128,2048]{1,0:T(8,128)(2,1)S(1)}, bf16[128,2048]{1,0:T(8,128)(2,1)S(1)}, u32[]{:S(2)}, u32[]{:S(2)}) collective-permute-start(bf16[128,2048]{1,0:T(8,128)(2,1)S(1)} %slice.155), channel_id=1, source_target_pairs={{0,24},{1,9},{2,26},{3,11},{4,28},{5,13},{6,30},{7,15},{8,16},{9,1... | collective-permute-start | bytes 1572872 | tf_op jit(solution)/shard_map/reduce_a0/ppermute | solution.py:52
  135.0 9.3 %collective-permute-start.24 = (bf16[128,2048]{1,0:T(8,128)(2,1)S(1)}, bf16[128,2048]{1,0:T(8,128)(2,1)S(1)}, u32[]{:S(2)}, u32[]{:S(2)}) collective-permute-start(bf16[128,2048]{1,0:T(8,128)(2,1)S(1)} %slice.154), channel_id=1, source_target_pairs={{0,2},{1,7},{2,0},{3,5},{4,6},{5,3},{6,4},{7,1},{8,10},{9,15},{10,... | collective-permute-start | bytes 1572872 | tf_op jit(solution)/shard_map/reduce_a1/ppermute | solution.py:52
  137.6 10.5 %collective-permute-start.28 = (bf16[128,2048]{1,0:T(8,128)(2,1)S(1)}, bf16[128,2048]{1,0:T(8,128)(2,1)S(1)}, u32[]{:S(2)}, u32[]{:S(2)}) collective-permute-start(bf16[128,2048]{1,0:T(8,128)(2,1)S(1)} %slice.153), channel_id=1, source_target_pairs={{0,96},{1,33},{2,98},{3,35},{4,100},{5,37},{6,102},{7,39},{8,104},... | collective-permute-start | bytes 1572872 | tf_op jit(solution)/shard_map/reduce_a2/ppermute | solution.py:52
  (3 other events, 5.6 us)
